TPU v7x, 32 devices: a whole 2x2x4 slice. The times are simulated.
32 devices in a mesh: tower: 2 (over core), dp: 8 (over z, x), mp: 2 (over y).
Axes of the slice: x: 2, y: 2, z: 4, core: 2. Of those that a mesh axis runs over, the one named last changes fastest.
Arguments:
- token_ids: int32 [2, 8192], P('tower', 'dp'), may hold values from 0 to 30527
- seq_lengths: int32 [2, 8, 16], replicated, may hold values from 0 to 1024, as said below
- positives: int32 [8, 16], replicated, may hold values from 0 to 127, as said below
- embedding: float32 [30528, 768], P('dp', 'mp'), may hold values from -0.21875 to 0.21875
- attn_in: float32 [768, 3, 768], P(('tower', 'dp'), None, 'mp'), may hold values from -0.21875 to 0.21875
- attn_out: float32 [768, 768], P(('tower', 'dp'), 'mp'), may hold values from -0.875 to 0.875
- ffn_in: float32 [768, 2, 3072], P(('tower', 'dp'), None, 'mp'), may hold values from -0.21875 to 0.21875
- ffn_out: float32 [768, 3072], P(('tower', 'dp'), 'mp'), may hold values from -0.109375 to 0.109375
- norm_params: float32 [6, 768], replicated, as said below
- logit_scale: float32 [1], replicated, may hold values from 2.6 to 3.6
- embed_m: float32 [30528, 768], P('dp', 'mp'), as said below
- embed_v: float32 [30528, 768], P('dp', 'mp'), as said below
- attn_in_m: float32 [768, 3, 768], P(('tower', 'dp'), None, 'mp'), as said below
- attn_in_v: float32 [768, 3, 768], P(('tower', 'dp'), None, 'mp'), as said below
- attn_out_m: float32 [768, 768], P(('tower', 'dp'), 'mp'), as said below
- attn_out_v: float32 [768, 768], P(('tower', 'dp'), 'mp'), as said below
- ffn_in_m: float32 [768, 2, 3072], P(('tower', 'dp'), None, 'mp'), as said below
- ffn_in_v: float32 [768, 2, 3072], P(('tower', 'dp'), None, 'mp'), as said below
- ffn_out_m: float32 [768, 3072], P(('tower', 'dp'), 'mp'), as said below
- ffn_out_v: float32 [768, 3072], P(('tower', 'dp'), 'mp'), as said below
- norm_m: float32 [6, 768], replicated, as said below
- norm_v: float32 [6, 768], replicated, as said below
- scale_m: float32 [1], replicated, as said below
- scale_v: float32 [1], replicated, as said below
Outputs:
- new_embedding: float32 [30528, 768], P('dp', 'mp')
- new_embed_m: float32 [30528, 768], P('dp', 'mp')
- new_embed_v: float32 [30528, 768], P('dp', 'mp')
- new_attn_in: float32 [768, 3, 768], P(('tower', 'dp'), None, 'mp')
- new_attn_in_m: float32 [768, 3, 768], P(('tower', 'dp'), None, 'mp')
- new_attn_in_v: float32 [768, 3, 768], P(('tower', 'dp'), None, 'mp')
- new_attn_out: float32 [768, 768], P(('tower', 'dp'), 'mp')
- new_attn_out_m: float32 [768, 768], P(('tower', 'dp'), 'mp')
- new_attn_out_v: float32 [768, 768], P(('tower', 'dp'), 'mp')
- new_ffn_in: float32 [768, 2, 3072], P(('tower', 'dp'), None, 'mp')
- new_ffn_in_m: float32 [768, 2, 3072], P(('tower', 'dp'), None, 'mp')
- new_ffn_in_v: float32 [768, 2, 3072], P(('tower', 'dp'), None, 'mp')
- new_ffn_out: float32 [768, 3072], P(('tower', 'dp'), 'mp')
- new_ffn_out_m: float32 [768, 3072], P(('tower', 'dp'), 'mp')
- new_ffn_out_v: float32 [768, 3072], P(('tower', 'dp'), 'mp')
- new_norms: float32 [6, 768], replicated
- new_norm_m: float32 [6, 768], replicated
- new_norm_v: float32 [6, 768], replicated
- new_scale: float32 [1], replicated
- new_scale_m: float32 [1], replicated
- new_scale_v: float32 [1], replicated
- loss_sum: float32 [1], replicated
- query_count: float32 [1], replicated
- grad_norm: float32 [1], replicated
Inputs may be any that keep to these rules, and one draw needn't show every extreme that they name: seq_lengths[0] are query lengths of 4 to 64 tokens, at least 8 per row; seq_lengths[1] are document lengths; in every row the slots of positive length come first and sum to at most 1024; every row of seq_lengths[1] holds a document, one row holds a single document of exactly 1024 tokens, and the last row holds 16 documents of 64 tokens. `positives`: each entry is i * 16 + s for a slot s of positive length in seq_lengths[1, i]. `norm_params`: rows 0, 2, 4 are gains, rows 1, 3, 5 biases. `embed_m`: moments of both signs. `embed_v`: positive. `attn_in_m`: moments of both signs. `attn_in_v`: positive. `attn_out_m`: moments of both signs. `attn_out_v`: positive. `ffn_in_m`: moments of both signs. `ffn_in_v`: positive. `ffn_out_m`: moments of both signs. `ffn_out_v`: positive. `norm_m`: moments of both signs. `norm_v`: positive. `scale_m`: a moment. `scale_v`: positive.
All inputs are finite; a program needn't handle non-finite values.
Results may differ from a plain program's by a relative error of at most 0.019.
The roundings to bfloat16 on the way count: a program that leaves them out, or rounds other values in their place, can miss the bound.
Values may be sent and summed in bfloat16 or wider, within the bound.
A program may use at most 320 MiB of HBM per device.

v0:
```python
import jax
import jax.numpy as jnp
from jax import lax
from jax.sharding import PartitionSpec as P

HDIM = 64
STEP = 5


norm_eps = 1e-06
cap_value = 3.4
clip_max = 0.01
beta_one = 0.9
beta_two = 0.999
learn_rate = 0.02
out_rate = 0.05
norm_rate = 0.3
decay_rate = 0.01
adam_eps = 1e-08
neg_large = -1e30
highest = lax.Precision.HIGHEST


def layer_norm(stream, gain_row, bias_row):
    average = jnp.mean(stream, -1, keepdims=True)
    centered = stream - average
    variance = jnp.mean(centered * centered, -1, keepdims=True)
    return centered * lax.rsqrt(variance + norm_eps) * gain_row + bias_row


def rotate(values, cosine, sine_table):
    half_dim = values.shape[-1] // 2
    turned = jnp.concatenate([-values[..., half_dim:], values[..., :half_dim]], -1)
    return values * cosine + turned * sine_table


def rotary_tables(positions, head_dim):
    half_dim = head_dim // 2
    inverse = 1000.0 ** (-2.0 * jnp.arange(half_dim, dtype=jnp.float32) / head_dim)
    angles = positions.astype(jnp.float32)[:, None] * inverse[None, :]
    angles = jnp.concatenate([angles, angles], 1)[:, None, :]
    return (jnp.cos(angles), jnp.sin(angles))


def layout(lengths, tok_count, slot_count):
    end_points = jnp.cumsum(lengths)
    places = jnp.arange(tok_count, dtype=jnp.int32)
    segment = jnp.sum((places[:, None] >= end_points[None, :]).astype(jnp.int32), 1)
    starts = jnp.concatenate([jnp.zeros((1,), jnp.int32), end_points])
    slot_ids = jnp.arange(slot_count + 1, dtype=jnp.int32)
    segment_start = jnp.sum(jnp.where(segment[:, None] == slot_ids[None, :], starts[None, :], 0), 1)
    return (segment, places - segment_start)


def glu(gate_vals, up_vals):
    return jax.nn.silu(gate_vals) * up_vals


def pool_rows(stream_two, member, counts):
    pooled = jnp.dot(member, stream_two, precision=highest) / counts[:, None]
    return pooled * lax.rsqrt(jnp.sum(pooled * pooled, 1, keepdims=True) + 1e-06)


def model_total(values):
    return lax.psum(values.astype(jnp.bfloat16), "mp").astype(jnp.float32)


def block_scores(query_block, seg_block, key_low, segment, factor):
    scores = (
        jnp.einsum("thd,shd->hts", query_block, key_low, preferred_element_type=jnp.float32)
        * factor
    )
    return jnp.where((seg_block[:, None] == segment[None, :])[None], scores, neg_large)


def attention(query_low, key_low, value_low, segment):
    tok_count, heads_local, head_dim = query_low.shape
    block_rows = min(512, tok_count)
    block_count = tok_count // block_rows
    factor = head_dim ** (-0.5)
    query_blocks = query_low.reshape(block_count, block_rows, heads_local, head_dim)
    seg_blocks = segment.reshape(block_count, block_rows)

    def one_block(operands):
        scores = block_scores(operands[0], operands[1], key_low, segment, factor)
        row_peak = jnp.max(scores, 2, keepdims=True)
        row_total = jnp.sum(jnp.exp(scores - row_peak), 2, keepdims=True)
        log_total = row_peak + jnp.log(row_total)
        soft_rows = jnp.exp(scores - log_total)
        attended = jnp.einsum(
            "hts,shd->thd",
            soft_rows.astype(jnp.bfloat16),
            value_low,
            preferred_element_type=jnp.float32,
        )
        return (attended, log_total[..., 0])

    attended, log_total = lax.map(one_block, (query_blocks, seg_blocks))
    return (attended.reshape(tok_count, heads_local * head_dim), log_total)


def attention_back(query_low, key_low, value_low, grad_attended, log_total, segment):
    tok_count, heads_local, head_dim = query_low.shape
    block_rows = min(512, tok_count)
    block_count = tok_count // block_rows
    factor = head_dim ** (-0.5)
    query_blocks = query_low.reshape(block_count, block_rows, heads_local, head_dim)
    grad_blocks = grad_attended.reshape(block_count, block_rows, heads_local, head_dim)
    seg_blocks = segment.reshape(block_count, block_rows)

    def one_block(running, operands):
        query_block, grad_block, seg_block, lse_block = operands
        scores = block_scores(query_block, seg_block, key_low, segment, factor)
        soft_rows = jnp.exp(scores - lse_block[..., None])
        grad_soft = jnp.einsum(
            "thd,shd->hts", grad_block, value_low, preferred_element_type=jnp.float32
        )
        inner = jnp.sum(soft_rows * grad_soft, 2, keepdims=True)
        grad_scores = (soft_rows * (grad_soft - inner)).astype(jnp.bfloat16)
        grad_query = (
            jnp.einsum("hts,shd->thd", grad_scores, key_low, preferred_element_type=jnp.float32)
            * factor
        )
        grad_key = (
            running[0]
            + jnp.einsum(
                "hts,thd->shd", grad_scores, query_block, preferred_element_type=jnp.float32
            )
            * factor
        )
        grad_value = running[1] + jnp.einsum(
            "hts,thd->shd",
            soft_rows.astype(jnp.bfloat16),
            grad_block,
            preferred_element_type=jnp.float32,
        )
        return ((grad_key, grad_value), grad_query)

    zeros_kv = jnp.zeros(key_low.shape, jnp.float32)
    (grad_key, grad_value), grad_query = lax.scan(
        one_block, (zeros_kv, zeros_kv), (query_blocks, grad_blocks, seg_blocks, log_total)
    )
    return (grad_query.reshape(tok_count, heads_local, head_dim), grad_key, grad_value)


def layer_forward(embed_rows, segment, positions, weights, norm_rows):
    w_qkv, w_out, w_ffn, w_down = weights
    tok_count = embed_rows.shape[0]
    heads_local = w_qkv.shape[2] // HDIM
    stream_zero = layer_norm(embed_rows, norm_rows[0], norm_rows[1])
    input_zero = stream_zero.astype(jnp.bfloat16)
    projected = jnp.einsum("td,dcf->tcf", input_zero, w_qkv, preferred_element_type=jnp.float32)
    heads_view = projected.reshape(tok_count, 3, heads_local, HDIM)
    cosine, sine_table = rotary_tables(positions, HDIM)
    query_low = rotate(heads_view[:, 0], cosine, sine_table).astype(jnp.bfloat16)
    key_low = rotate(heads_view[:, 1], cosine, sine_table).astype(jnp.bfloat16)
    value_low = heads_view[:, 2].astype(jnp.bfloat16)
    attended, log_total = attention(query_low, key_low, value_low, segment)
    attended_low = attended.astype(jnp.bfloat16)
    attn_branch = model_total(
        jnp.einsum("tf,df->td", attended_low, w_out, preferred_element_type=jnp.float32)
    )
    sum_one = stream_zero + attn_branch
    stream_one = layer_norm(sum_one, norm_rows[2], norm_rows[3])
    input_one = stream_one.astype(jnp.bfloat16)
    gate_up = jnp.einsum("td,dcf->tcf", input_one, w_ffn, preferred_element_type=jnp.float32)
    hidden_low = glu(gate_up[:, 0], gate_up[:, 1]).astype(jnp.bfloat16)
    ffn_branch = model_total(
        jnp.einsum("tf,df->td", hidden_low, w_down, preferred_element_type=jnp.float32)
    )
    sum_two = stream_one + ffn_branch
    stream_two = layer_norm(sum_two, norm_rows[4], norm_rows[5])
    kept_vals = (
        embed_rows,
        sum_one,
        sum_two,
        input_zero,
        input_one,
        query_low,
        key_low,
        value_low,
        log_total,
        attended_low,
        gate_up,
        hidden_low,
    )
    return (stream_two, kept_vals)


def layer_backward(grad_two, kept_vals, weights, norm_rows, segment, positions):
    w_qkv, w_out, w_ffn, w_down = weights
    (
        embed_rows,
        sum_one,
        sum_two,
        input_zero,
        input_one,
        query_low,
        key_low,
        value_low,
        log_total,
        attended_low,
        gate_up,
        hidden_low,
    ) = kept_vals
    tok_count, heads_local, head_dim = query_low.shape
    grad_sum_two, gain_two, bias_two = jax.vjp(layer_norm, sum_two, norm_rows[4], norm_rows[5])[1](
        grad_two
    )
    ffn_low = grad_sum_two.astype(jnp.bfloat16)
    grad_down = jnp.einsum("td,tf->df", ffn_low, hidden_low, preferred_element_type=jnp.float32)
    grad_hidden = jnp.einsum("td,df->tf", ffn_low, w_down, preferred_element_type=jnp.float32)
    grad_gate, grad_up = jax.vjp(glu, gate_up[:, 0], gate_up[:, 1])[1](grad_hidden)
    gate_grads = jnp.stack([grad_gate, grad_up], 1).astype(jnp.bfloat16)
    grad_ffn = jnp.einsum("td,tcf->dcf", input_one, gate_grads, preferred_element_type=jnp.float32)
    grad_stream_one = grad_sum_two + model_total(
        jnp.einsum("tcf,dcf->td", gate_grads, w_ffn, preferred_element_type=jnp.float32)
    )
    grad_sum_one, gain_one, bias_one = jax.vjp(layer_norm, sum_one, norm_rows[2], norm_rows[3])[1](
        grad_stream_one
    )
    attn_low = grad_sum_one.astype(jnp.bfloat16)
    grad_out = jnp.einsum("td,tf->df", attn_low, attended_low, preferred_element_type=jnp.float32)
    grad_attended = jnp.einsum(
        "td,df->tf", attn_low, w_out, preferred_element_type=jnp.float32
    ).astype(jnp.bfloat16)
    grad_query, grad_key, grad_value = attention_back(
        query_low,
        key_low,
        value_low,
        grad_attended.reshape(tok_count, heads_local, head_dim),
        log_total,
        segment,
    )
    cosine, sine_table = rotary_tables(positions, head_dim)
    turn_back = jax.vjp(lambda values: rotate(values, cosine, sine_table), grad_query)[1]
    grad_projected = jnp.stack([turn_back(grad_query)[0], turn_back(grad_key)[0], grad_value], 1)
    grad_projected = grad_projected.reshape(tok_count, 3, heads_local * head_dim).astype(
        jnp.bfloat16
    )
    grad_qkv = jnp.einsum(
        "td,tcf->dcf", input_zero, grad_projected, preferred_element_type=jnp.float32
    )
    grad_stream_zero = grad_sum_one + model_total(
        jnp.einsum("tcf,dcf->td", grad_projected, w_qkv, preferred_element_type=jnp.float32)
    )
    grad_embed, gain_zero, bias_zero = jax.vjp(layer_norm, embed_rows, norm_rows[0], norm_rows[1])[
        1
    ](grad_stream_zero)
    norm_grads = jnp.stack([gain_zero, bias_zero, gain_one, bias_one, gain_two, bias_two])
    return (grad_embed, (grad_qkv, grad_out, grad_ffn, grad_down), norm_grads)


def adamw(weight_in, gradient, first_mom, second, factor, step_num, rate):
    gradient = gradient * factor
    first_new = beta_one * first_mom + (1.0 - beta_one) * gradient
    second_new = beta_two * second + (1.0 - beta_two) * gradient * gradient
    first_hat = first_new / (1.0 - beta_one**step_num)
    second_hat = second_new / (1.0 - beta_two**step_num)
    weight_new = weight_in - rate * (
        first_hat / (jnp.sqrt(second_hat) + adam_eps) + decay_rate * weight_in
    )
    return (weight_new, first_new, second_new)


def local(
    token_ids,
    seq_lengths,
    positives,
    embedding,
    attn_in,
    attn_out,
    ffn_in,
    ffn_out,
    norm_params,
    logit_scale,
    embed_m,
    embed_v,
    attn_in_m,
    attn_in_v,
    attn_out_m,
    attn_out_v,
    ffn_in_m,
    ffn_in_v,
    ffn_out_m,
    ffn_out_v,
    norm_m,
    norm_v,
    scale_m,
    scale_v,
):
    n_data = lax.axis_size("dp")
    tower_idx = lax.axis_index("tower")
    data_idx = lax.axis_index("dp")
    model_idx = lax.axis_index("mp")
    slot_count = seq_lengths.shape[2]
    token_list = token_ids[0]
    tok_count = token_list.shape[0]
    model_width = norm_params.shape[1]
    local_width = embedding.shape[1]
    row_count = embedding.shape[0]
    weights = (
        lax.all_gather(attn_in.astype(jnp.bfloat16), ("tower", "dp"), axis=0, tiled=True),
        lax.all_gather(attn_out.astype(jnp.bfloat16), ("tower", "dp"), axis=0, tiled=True),
        lax.all_gather(ffn_in.astype(jnp.bfloat16), ("tower", "dp"), axis=0, tiled=True),
        lax.all_gather(ffn_out.astype(jnp.bfloat16), ("tower", "dp"), axis=0, tiled=True),
    )
    shard_piece = lax.all_gather(embedding.astype(jnp.bfloat16), "dp", axis=0, tiled=True)
    inside = (token_list >= 0) & (token_list < shard_piece.shape[0])
    picked = jnp.take(shard_piece, jnp.clip(token_list, 0, shard_piece.shape[0] - 1), axis=0)
    looked = jnp.where(inside[:, None], picked.astype(jnp.float32), 0.0)
    embed_rows = lax.all_gather(looked.astype(jnp.bfloat16), "mp", axis=1, tiled=True).astype(
        jnp.float32
    )
    lengths_row = seq_lengths[tower_idx, data_idx]
    segment, positions = layout(lengths_row, tok_count, slot_count)
    stream_two, kept_vals = layer_forward(embed_rows, segment, positions, weights, norm_params)
    member = (segment[None, :] == jnp.arange(slot_count, dtype=jnp.int32)[:, None]).astype(
        jnp.float32
    )
    counts = jnp.maximum(lengths_row, 1).astype(jnp.float32)
    own_embeds, pool_back = jax.vjp(lambda stream: pool_rows(stream, member, counts), stream_two)
    all_embeds = lax.all_gather(
        own_embeds.astype(jnp.bfloat16), ("tower", "dp"), axis=0, tiled=True
    )
    query_total = n_data * slot_count
    rows_per = slot_count // 2
    first_row = (tower_idx * n_data + data_idx) * rows_per
    query_rows = lax.dynamic_slice_in_dim(all_embeds, first_row, rows_per, 0)
    documents = all_embeds[query_total:]
    cosines = jnp.einsum("qd,kd->qk", query_rows, documents, preferred_element_type=jnp.float32)
    logit_factor = jnp.exp(jnp.minimum(logit_scale[0], cap_value))
    doc_ok = seq_lengths[1].reshape(-1) > 0
    query_ok_all = seq_lengths[0].reshape(-1) > 0
    query_count = jnp.sum(query_ok_all.astype(jnp.float32))
    query_ok = lax.dynamic_slice_in_dim(query_ok_all, first_row, rows_per, 0)
    logits = jnp.where(doc_ok[None, :], logit_factor * cosines, neg_large)
    row_peak = jnp.max(logits, 1, keepdims=True)
    log_total = row_peak + jnp.log(jnp.sum(jnp.exp(logits - row_peak), 1, keepdims=True))
    soft_rows = jnp.exp(logits - log_total)
    targets = lax.dynamic_slice_in_dim(positives.reshape(-1), first_row, rows_per, 0)
    target_mask = jnp.arange(query_total, dtype=jnp.int32)[None, :] == targets[:, None]
    picked = jnp.sum(jnp.where(target_mask, logits, 0.0), 1)
    loss_part = jnp.sum(jnp.where(query_ok, log_total[:, 0] - picked, 0.0))
    grad_logits = (
        jnp.where(query_ok[:, None], soft_rows - target_mask.astype(jnp.float32), 0.0) / query_count
    )
    scale_part = (
        jnp.sum(grad_logits * cosines)
        * logit_factor
        * (logit_scale[0] < cap_value).astype(jnp.float32)
    )
    grad_cos = (logit_factor * grad_logits).astype(jnp.bfloat16)
    grad_queries = jnp.einsum("qk,kd->qd", grad_cos, documents, preferred_element_type=jnp.float32)
    grad_documents = jnp.einsum(
        "qk,qd->kd", grad_cos, query_rows, preferred_element_type=jnp.float32
    )
    grad_term = jnp.concatenate(
        [jnp.zeros((query_total, model_width), jnp.float32), grad_documents], 0
    )
    grad_term = lax.dynamic_update_slice_in_dim(grad_term, grad_queries, first_row, 0)
    own_grad = lax.psum_scatter(grad_term, ("tower", "dp"), scatter_dimension=0, tiled=True)
    grad_two = pool_back(own_grad)[0]
    grad_embed, layer_grads, norm_grads = layer_backward(
        grad_two, kept_vals, weights, norm_params, segment, positions
    )
    embed_low = grad_embed.astype(jnp.bfloat16)
    column_part = lax.dynamic_slice_in_dim(embed_low, model_idx * local_width, local_width, 1)
    row_start = data_idx * row_count
    all_ids = lax.all_gather(token_list, ("tower", "dp"), axis=0, tiled=True)
    piece_ids = all_ids - row_start
    inside = (piece_ids >= 0) & (piece_ids < row_count)
    slot_ids = jnp.where(inside, piece_ids, row_count)
    embed_grad = jax.ops.segment_sum(
        lax.all_gather(column_part, ("tower", "dp"), axis=0, tiled=True).astype(jnp.float32),
        slot_ids,
        num_segments=row_count + 1,
    )[:row_count]
    shard_grads = (
        lax.psum_scatter(layer_grads[0], ("tower", "dp"), scatter_dimension=0, tiled=True),
        lax.psum_scatter(layer_grads[1], ("tower", "dp"), scatter_dimension=0, tiled=True),
        lax.psum_scatter(layer_grads[2], ("tower", "dp"), scatter_dimension=0, tiled=True),
        lax.psum_scatter(layer_grads[3], ("tower", "dp"), scatter_dimension=0, tiled=True),
    )
    norm_grad, loss_sum, scale_grad = lax.psum((norm_grads, loss_part, scale_part), ("tower", "dp"))
    local_sq = sum((jnp.sum(gradient * gradient) for gradient in shard_grads)) + 0.5 * jnp.sum(
        embed_grad * embed_grad
    )
    total_sq = (
        lax.psum(local_sq, ("tower", "dp", "mp"))
        + jnp.sum(norm_grad * norm_grad)
        + scale_grad * scale_grad
    )
    grad_norm = jnp.sqrt(total_sq)
    factor = jnp.minimum(1.0, clip_max / (grad_norm + 1e-06))
    step_num = float(STEP)
    embed_new = adamw(embedding, embed_grad, embed_m, embed_v, factor, step_num, learn_rate)
    qkv_new = adamw(attn_in, shard_grads[0], attn_in_m, attn_in_v, factor, step_num, learn_rate)
    out_new = adamw(attn_out, shard_grads[1], attn_out_m, attn_out_v, factor, step_num, out_rate)
    ffn_new = adamw(ffn_in, shard_grads[2], ffn_in_m, ffn_in_v, factor, step_num, learn_rate)
    down_new = adamw(ffn_out, shard_grads[3], ffn_out_m, ffn_out_v, factor, step_num, learn_rate)
    norms_new = adamw(norm_params, norm_grad, norm_m, norm_v, factor, step_num, norm_rate)
    scale_new = adamw(
        logit_scale, scale_grad.reshape(1), scale_m, scale_v, factor, step_num, learn_rate
    )
    return (
        embed_new[0],
        embed_new[1],
        embed_new[2],
        qkv_new[0],
        qkv_new[1],
        qkv_new[2],
        out_new[0],
        out_new[1],
        out_new[2],
        ffn_new[0],
        ffn_new[1],
        ffn_new[2],
        down_new[0],
        down_new[1],
        down_new[2],
        norms_new[0],
        norms_new[1],
        norms_new[2],
        scale_new[0],
        scale_new[1],
        scale_new[2],
        loss_sum.reshape(1),
        query_count.reshape(1),
        grad_norm.reshape(1),
    )


def solution(mesh):
    return jax.shard_map(
        local,
        mesh=mesh,
        in_specs=(
            P("tower", "dp"),
            P(),
            P(),
            P("dp", "mp"),
            P(("tower", "dp"), None, "mp"),
            P(("tower", "dp"), "mp"),
            P(("tower", "dp"), None, "mp"),
            P(("tower", "dp"), "mp"),
            P(),
            P(),
            P("dp", "mp"),
            P("dp", "mp"),
            P(("tower", "dp"), None, "mp"),
            P(("tower", "dp"), None, "mp"),
            P(("tower", "dp"), "mp"),
            P(("tower", "dp"), "mp"),
            P(("tower", "dp"), None, "mp"),
            P(("tower", "dp"), None, "mp"),
            P(("tower", "dp"), "mp"),
            P(("tower", "dp"), "mp"),
            P(),
            P(),
            P(),
            P(),
        ),
        out_specs=(
            P("dp", "mp"),
            P("dp", "mp"),
            P("dp", "mp"),
            P(("tower", "dp"), None, "mp"),
            P(("tower", "dp"), None, "mp"),
            P(("tower", "dp"), None, "mp"),
            P(("tower", "dp"), "mp"),
            P(("tower", "dp"), "mp"),
            P(("tower", "dp"), "mp"),
            P(("tower", "dp"), None, "mp"),
            P(("tower", "dp"), None, "mp"),
            P(("tower", "dp"), None, "mp"),
            P(("tower", "dp"), "mp"),
            P(("tower", "dp"), "mp"),
            P(("tower", "dp"), "mp"),
            P(),
            P(),
            P(),
            P(),
            P(),
            P(),
            P(),
            P(),
            P(),
        ),
        check_vma=False,
    )
```

profile of v0, /device:TPU:1, one launch (start us, length us, event | category | flops | bytes accessed | tf_op | source)
XLA Modules:
  0.0 1779.1 jit_solution(18094539239358740573)
XLA Ops:
  12.1 450.2 %all-gather.8.cloned.1.call-done = bf16[30528,384]{1,0:T(8,128)(2,1)} async-done(((bf16[3816,384]{1,0:T(8,128)(2,1)}), bf16[30528,384]{1,0:T(8,128)(2,1)}) %all-gather.8.cloned.1.call-update) | async-done | bytes 23445520 | tf_op jit(solution)/shard_map/all_gather | solution.py:308
  462.3 14.5 gather_fusion
  483.0 37.6 %all_gather.31 = bf16[768,384]{1,0:T(8,128)(2,1)} all-gather(bf16[48,384]{1,0:T(8,128)(2,1)S(1)} %convert_element_type.153), channel_id=1, replica_groups=mesh['tower'=2,'dp'=8,'mp'=2] {'tower','dp'}, dimensions={0}, use_global_device_ids=true | all-gather | bytes 626688 | tf_op jit(solution)/shard_map/all_gather | solution.py:304
  524.5 24.5 %all-gather.12.cloned.1.call-done = bf16[768,3,384]{2,0,1:T(8,128)(2,1)} async-done(((bf16[48,3,384]{2,0,1:T(8,128)(2,1)}), bf16[768,3,384]{2,0,1:T(8,128)(2,1)}) %all-gather.12.cloned.1.call-update) | async-done | bytes 1769488 | tf_op jit(solution)/shard_map/all_gather | solution.py:303
  567.0 32.5 %while.27 = (s32[]{:T(128)}, bf16[2,512,6,64]{1,3,2,0:T(8,128)(2,1)S(1)}, f32[2,6,512]{2,1,0:T(8,128)S(1)}, s32[2,512]{1,0:T(2,128)S(1)}, s32[1024]{0:T(1024)S(1...) while((s32[]{:T(128)}, ...), condition=%wide.region_8.9_spmd, body=%wide.region_5.8_spmd.sunk | while | flops 840430592 | bytes 93059216 | solution.py:98
  575.3 7.9 fusion.182
  591.5 7.9 fusion.182
  605.4 48.2 %all-reduce.11.cloned.1.call-done = bf16[1024,768]{1,0:T(8,128)(2,1)} async-done(((bf16[1024,768]{1,0:T(8,128)(2,1)}), bf16[1024,768]{1,0:T(8,128)(2,1)}) %all-reduce.11.cloned.1.call-update) | async-done | bytes 1572880 | tf_op jit(solution)/shard_map/psum | solution.py:65
  658.0 52.4 %all-gather.14.cloned.1.call-done = bf16[768,2,1536]{2,0,1:T(8,128)(2,1)} async-done(((bf16[48,2,1536]{2,0,1:T(8,128)(2,1)}), bf16[768,2,1536]{2,0,1:T(8,128)(2,1)}) %all-gather.14.cloned.1.call-update) | async-done | bytes 4718608 | tf_op jit(solution)/shard_map/all_gather | solution.py:305
  710.4 8.5 fusion.126
  726.6 27.6 %all-gather.16.cloned.1.call-done = bf16[768,1536]{1,0:T(8,128)(2,1)} async-done(((bf16[48,1536]{1,0:T(8,128)(2,1)}), bf16[768,1536]{1,0:T(8,128)(2,1)}) %all-gather.16.cloned.1.call-update) | async-done | bytes 2359312 | tf_op jit(solution)/shard_map/all_gather | solution.py:306
  762.3 48.2 %all-reduce.13.cloned.1.call-done = bf16[1024,768]{1,0:T(8,128)(2,1)} async-done(((bf16[1024,768]{1,0:T(8,128)(2,1)}), bf16[1024,768]{1,0:T(8,128)(2,1)}) %all-reduce.13.cloned.1.call-update) | async-done | bytes 1572880 | tf_op jit(solution)/shard_map/psum | solution.py:65
  816.3 35.6 %all_gather.34 = bf16[256,768]{1,0:T(8,128)(2,1)S(1)} all-gather(bf16[16,768]{1,0:T(8,128)(2,1)S(1)} %multiply_convert_fusion.3), channel_id=1, replica_groups=mesh['tower'=2,'dp'=8,'mp'=2] {'tower','dp'}, dimensions={0}, use_global_device_ids=true | all-gather | bytes 417792 | tf_op jit(solution)/shard_map/all_gather | solution.py:323
  855.2 50.5 %reduce-scatter.6.cloned.1.call-done = f32[16,768]{1,0:T(8,128)} async-done(((f32[256,768]{1,0:T(8,128)}), f32[16,768]{1,0:T(8,128)}) %reduce-scatter.6.cloned.1.call-update) | async-done | bytes 49168 | tf_op jit(solution)/shard_map/reduce_scatter | solution.py:362
  913.2 9.0 fusion.59
  931.1 52.5 %all-reduce.15.cloned.1.call-done = bf16[1024,768]{1,0:T(8,128)(2,1)} async-done(((bf16[1024,768]{1,0:T(8,128)(2,1)}), bf16[1024,768]{1,0:T(8,128)(2,1)}) %all-reduce.15.cloned.1.call-update) | async-done | bytes 1572880 | tf_op jit(solution)/shard_map/psum | solution.py:65
  1000.2 89.3 %while.28 = (s32[]{:T(128)}, f32[1024,6,64]{0,2,1:T(8,128)S(1)}, f32[1024,6,64]{0,2,1:T(8,128)}, f32[2,512,6,64]{1,0,3,2:T(2,128)}, bf16[2,512,6,64]{1,3,2,0:T(8...) while((s32[]{:T(128)}, f32[1024,6,64]{0,2,1:T(8,128)S(1)}, ...), condition=%wide.region_28.29_spmd.clone, body=%wide.region_26.28_spmd.clone.sunk | while | flops 2063135744 | bytes 110721200 | solution.py:140
  1009.3 8.4 multiply_reduce_fusion.17
  1029.8 14.9 dynamic_update_slice.24
  1054.0 8.4 multiply_reduce_fusion.17
  1074.4 14.9 dynamic_update_slice.24
  1127.0 12.4 fusion.41
  1139.5 19.0 %all-reduce.17.cloned.1.call-done = bf16[1024,768]{1,0:T(8,128)(2,1)} async-done(((bf16[1024,768]{1,0:T(8,128)(2,1)}), bf16[1024,768]{1,0:T(8,128)(2,1)}) %all-reduce.17.cloned.1.call-update) | async-done | bytes 1572880 | tf_op jit(solution)/shard_map/psum | solution.py:65
  1166.8 33.4 %all-gather = s32[1,16384]{1,0:T(1,128)S(1)} all-gather(s32[1,1024]{1,0:T(1,128)S(1)} %copy-done.75), channel_id=2, replica_groups=mesh['tower'=2,'dp'=8,'mp'=2] {'tower','dp'}, dimensions={1}, use_global_device_ids=true | all-gather | bytes 69632 | tf_op jit(solution)/shard_map/all_gather | solution.py:370
  1203.1 58.1 %all-reduce.5 = (f32[6,768]{1,0:T(8,128)S(1)}, f32[]{:T(128)}, f32[1]{0:T(128)}) all-reduce(f32[6,768]{1,0:T(8,128)S(1)} %stack.40, f32[]{:T(128)S(6)} %mul.804, f32[1]{0:T(128)} %bitcast.31), channel_id=1, replica_groups=mesh['tower'=2,'dp'=8,'mp'=2] {'tower','dp'}, use_global_device_ids=true, to_apply=%region_49.50 | all-reduce | flops 4610 | bytes 36880 | tf_op jit(solution)/shard_map/psum | solution.py:385
  1263.3 28.2 %reduce-scatter.8.cloned.1.call-done = f32[48,3,384]{2,0,1:T(8,128)} async-done(((f32[768,3,384]{2,0,1:T(8,128)}), f32[48,3,384]{2,0,1:T(8,128)}) %reduce-scatter.8.cloned.1.call-update) | async-done | bytes 221200 | tf_op jit(solution)/shard_map/reduce_scatter | solution.py:380
  1294.4 76.9 %reduce-scatter.14.cloned.1.call-done = f32[48,1536]{1,0:T(8,128)} async-done(((f32[768,1536]{1,0:T(8,128)}), f32[48,1536]{1,0:T(8,128)}) %reduce-scatter.14.cloned.1.call-update) | async-done | bytes 294928 | tf_op jit(solution)/shard_map/reduce_scatter | solution.py:383
  1372.9 113.7 %reduce-scatter.12.cloned.1.call-done = f32[48,2,1536]{2,0,1:T(8,128)} async-done(((f32[768,2,1536]{2,0,1:T(8,128)}), f32[48,2,1536]{2,0,1:T(8,128)}) %reduce-scatter.12.cloned.1.call-update) | async-done | bytes 589840 | tf_op jit(solution)/shard_map/reduce_scatter | solution.py:382
  1489.7 100.8 %all-gather.18.cloned.1.call-done = bf16[16384,384]{1,0:T(8,128)(2,1)} async-done(((bf16[1024,384]{1,0:T(8,128)(2,1)}), bf16[16384,384]{1,0:T(8,128)(2,1)}) %all-gather.18.cloned.1.call-update) | async-done | bytes 12582928 | tf_op jit(solution)/shard_map/all_gather | solution.py:375
  1590.5 108.9 %scatter_custom_fusion = f32[3817,384]{1,0:T(8,128)} fusion(s32[16384]{0:T(1024)S(1)} %and_select_fusion, bf16[16384,384]{1,0:T(8,128)(2,1)} %all-gather.18.cloned.1.call-done, f32[]{:T(128)} %constant.75.clone.1), kind=kCustom, calls=%fused_computation.49 | custom fusion | flops 12582912 | bytes 18445828 | tf_op jit(solution)/shard_map/scatter-add | solution.py:374
  1706.3 37.6 %psum.60 = f32[]{:T(128)} all-reduce(f32[]{:T(128)S(6)} %add.368), channel_id=1, replica_groups=mesh['tower'=2,'dp'=8,'mp'=2] {'tower','dp','mp'}, use_global_device_ids=true, to_apply=%region_42.43 | all-reduce | flops 1 | bytes 8 | tf_op jit(solution)/shard_map/psum | solution.py:390
  1752.6 12.2 multiply_subtract_fusion
  (411 shorter events, 225.6 us)
Async XLA Ops:
  7.2 455.1 %all-gather.8.cloned.1.call-start = ((), (), s32[]{:S(2)}) async-start(), calls=%async_computation.5 | async-start | bytes 26376192 | tf_op jit(solution)/shard_map/all_gather | solution.py:308
  11.9 508.8 %all-gather.10.cloned.1.call-start = ((), (), s32[]{:S(2)}) async-start(), calls=%async_computation.6 | async-start | bytes 2359296 | tf_op jit(solution)/shard_map/all_gather | solution.py:312
  12.0 466.0 %copy-start.34 = (f32[48,3,384]{2,0,1:T(8,128)S(1)}, f32[48,3,384]{2,0,1:T(8,128)}, u32[]{:S(2)}) copy-start(f32[48,3,384]{2,0,1:T(8,128)} %param.32) | copy-start | bytes 663556
  12.0 466.8 %copy-start.88 = (s32[2,8,16]{2,1,0:T(8,128)S(1)}, s32[2,8,16]{2,1,0:T(8,128)}, u32[]{:S(2)}) copy-start(s32[2,8,16]{2,1,0:T(8,128)} %param.29) | copy-start | bytes 3076
  12.0 467.3 %copy-start.51 = (f32[48,384]{1,0:T(8,128)S(1)}, f32[48,384]{1,0:T(8,128)}, u32[]{:S(2)}) copy-start(f32[48,384]{1,0:T(8,128)} %param.33) | copy-start | bytes 221188
  12.0 467.4 %copy-start.64 = (f32[6,768]{1,0:T(8,128)S(1)}, f32[6,768]{1,0:T(8,128)}, u32[]{:S(2)}) copy-start(f32[6,768]{1,0:T(8,128)} %param.36) | copy-start | bytes 55300
  478.0 71.1 %all-gather.12.cloned.1.call-start = ((), (), s32[]{:S(2)}) async-start(), calls=%async_computation.7 | async-start | bytes 1880064 | tf_op jit(solution)/shard_map/all_gather | solution.py:303
  478.7 174.9 %all-reduce.11.cloned.1.call-start = ((), (), s32[]{:S(2)}) async-start(), calls=%async_computation.8 | async-start | bytes 3145728 | tf_op jit(solution)/shard_map/psum | solution.py:65
  479.5 331.1 %copy-start.82 = (f32[768]{0:T(1024)}, f32[768]{0:T(1024)S(1)}, u32[]{:S(2)}) copy-start(f32[768]{0:T(1024)S(1)} %get-tuple-element.282) | copy-start | bytes 9220
  479.5 509.2 %copy-start.56 = (f32[768]{0:T(1024)}, f32[768]{0:T(1024)S(1)}, u32[]{:S(2)}) copy-start(f32[768]{0:T(1024)S(1)} %get-tuple-element.285) | copy-start | bytes 9220
  479.5 509.2 %copy-start.60 = (f32[768]{0:T(1024)}, f32[768]{0:T(1024)S(1)}, u32[]{:S(2)}) copy-start(f32[768]{0:T(1024)S(1)} %get-tuple-element.284) | copy-start | bytes 9220
  479.5 509.2 %copy-start.70 = (f32[768]{0:T(1024)}, f32[768]{0:T(1024)S(1)}, u32[]{:S(2)}) copy-start(f32[768]{0:T(1024)S(1)} %get-tuple-element.283) | copy-start | bytes 9220
  481.2 81.6 %copy-start.25 = (f32[1024,64]{0,1:T(8,128)}, f32[1024,64]{0,1:T(8,128)S(1)}, u32[]{:S(2)}) copy-start(f32[1024,64]{0,1:T(8,128)S(1)} %get-tuple-element.381) | copy-start | bytes 786436
  522.4 466.3 %copy-start.45 = (f32[1024]{0:T(1024)}, f32[1024]{0:T(1024)S(1)}, u32[]{:S(2)}) copy-start(f32[1024]{0:T(1024)S(1)} %broadcast_multiply_fusion.6) | copy-start | bytes 12292
  524.5 464.2 %copy-start.54 = (f32[1024]{0:T(1024)}, f32[1024]{0:T(1024)S(1)}, u32[]{:S(2)}) copy-start(f32[1024]{0:T(1024)S(1)} %fusion.111) | copy-start | bytes 12292
  603.5 106.9 %all-gather.14.cloned.1.call-start = ((), (), s32[]{:S(2)}) async-start(), calls=%async_computation.9 | async-start | bytes 5013504 | tf_op jit(solution)/shard_map/all_gather | solution.py:305
  604.4 149.7 %all-gather.16.cloned.1.call-start = ((), (), s32[]{:S(2)}) async-start(), calls=%async_computation.10 | async-start | bytes 2506752 | tf_op jit(solution)/shard_map/all_gather | solution.py:306
  605.2 205.4 %all-reduce.13.cloned.1.call-start = ((), (), s32[]{:S(2)}) async-start(), calls=%async_computation.11 | async-start | bytes 3145728 | tf_op jit(solution)/shard_map/psum | solution.py:65
  656.4 332.3 %copy-start.62 = (f32[1024]{0:T(1024)}, f32[1024]{0:T(1024)S(1)}, u32[]{:S(2)}) copy-start(f32[1024]{0:T(1024)S(1)} %broadcast_multiply_fusion.5) | copy-start | bytes 12292
  658.0 330.7 %copy-start.68 = (f32[1024]{0:T(1024)}, f32[1024]{0:T(1024)S(1)}, u32[]{:S(2)}) copy-start(f32[1024]{0:T(1024)S(1)} %fusion.112) | copy-start | bytes 12292
  760.5 145.2 %reduce-scatter.6.cloned.1.call-start = ((), (), s32[]{:S(2)}) async-start(), calls=%async_computation.12 | async-start | bytes 835584 | tf_op jit(solution)/shard_map/reduce_scatter | solution.py:362
  761.5 91.9 %copy-start.89 = (pred[128]{0:T(512)(128)(4,1)}, pred[128]{0:T(512)(128)(4,1)S(1)}, u32[]{:S(2)}) copy-start(pred[128]{0:T(512)(128)(4,1)S(1)} %gt.20) | copy-start | bytes 388
  762.3 91.2 %copy-start.94 = (s32[8]{0:T(128)}, s32[8]{0:T(128)S(1)}, u32[]{:S(2)}) copy-start(s32[8]{0:T(128)S(1)} %dynamic_slice.39) | copy-start | bytes 100
  762.3 91.1 %copy-start.96 = (pred[8]{0:T(512)(128)(4,1)}, pred[8]{0:T(512)(128)(4,1)S(1)}, u32[]{:S(2)}) copy-start(pred[8]{0:T(512)(128)(4,1)S(1)} %dynamic_slice.37) | copy-start | bytes 28
  855.2 128.4 %all-reduce.15.cloned.1.call-start = ((), (), s32[]{:S(2)}) async-start(), calls=%async_computation.13 | async-start | bytes 3145728 | tf_op jit(solution)/shard_map/psum | solution.py:65
  913.0 75.7 %copy-start.47 = (f32[1024]{0:T(1024)}, f32[1024]{0:T(1024)S(1)}, u32[]{:S(2)}) copy-start(f32[1024]{0:T(1024)S(1)} %negate_multiply_fusion.2) | copy-start | bytes 12292
  931.0 227.4 %all-reduce.17.cloned.1.call-start = ((), (), s32[]{:S(2)}) async-start(), calls=%async_computation.14 | async-start | bytes 3145728 | tf_op jit(solution)/shard_map/psum | solution.py:65
  1106.9 154.9 %reduce-scatter.10.cloned.1.call-start = ((), (), s32[]{:S(2)}) async-start(), calls=%async_computation.17 | async-start | bytes 1253376 | tf_op jit(solution)/shard_map/reduce_scatter | solution.py:381
  1111.3 180.2 %reduce-scatter.8.cloned.1.call-start = ((), (), s32[]{:S(2)}) async-start(), calls=%async_computation.16 | async-start | bytes 3760128 | tf_op jit(solution)/shard_map/reduce_scatter | solution.py:380
  1117.1 254.1 %reduce-scatter.14.cloned.1.call-start = ((), (), s32[]{:S(2)}) async-start(), calls=%async_computation.19 | async-start | bytes 5013504 | tf_op jit(solution)/shard_map/reduce_scatter | solution.py:383
  1125.7 360.9 %reduce-scatter.12.cloned.1.call-start = ((), (), s32[]{:S(2)}) async-start(), calls=%async_computation.18 | async-start | bytes 10027008 | tf_op jit(solution)/shard_map/reduce_scatter | solution.py:382
  1139.4 451.0 %all-gather.18.cloned.1.call-start = ((), (), s32[]{:S(2)}) async-start(), calls=%async_computation.15 | async-start | bytes 13369344 | tf_op jit(solution)/shard_map/all_gather | solution.py:375
  (91 other events, 1227.9 us)
Sparse Core Ops, SparseCore 0:
  12.0 450.2 all-gather.7
  478.1 27.1 all-gather.9
  508.2 40.8 all-gather.11
  603.7 49.9 all-reduce.10
  656.5 53.8 all-gather.13
  713.3 40.7 all-gather.15
  760.7 49.8 all-reduce.12
  855.3 50.3 reduce-scatter.5
  931.2 52.3 all-reduce.14
  1106.9 51.4 all-reduce.16
  1162.5 56.5 reduce-scatter.9
  1223.9 67.5 reduce-scatter.7
  1296.4 74.7 reduce-scatter.13
  1375.2 111.2 reduce-scatter.11
  1489.4 100.9 all-gather.17
where the time goes:
time: 1790 us; the launch traced here: 1780 us
  waiting for transfers between devices  1090 us (61%)
  other arithmetic  216 us (12%)
  blocking collectives  202 us (11%)
  matrix products  148 us (8%)
  local copies, waits for them, and re-layouts  88.5 us (5%)
  between operations  29.9 us (2%)
    all_gather x1, waiting for transfers between devices, local(): lax.all_gather(embedding.astype(jnp.bfloat16), 'dp', axis=0, tiled=True)  450 us
    psum x4, waiting for transfers between devices, model_total(): return lax.psum(values.astype(jnp.bfloat16), 'mp').astype(jnp.float32)  168 us
    reduce_scatter x1, waiting for transfers between devices, local(): lax.psum_scatter(layer_grads[2], ('tower', 'dp'), scatter_dimension=0, ti...  114 us
    scatter-add x1, other arithmetic, local(): jax.ops.segment_sum(lax.all_gather(column_part, ('tower', 'dp'), axis=0,...  109 us
    all_gather x1, waiting for transfers between devices, local(): lax.all_gather(column_part, ('tower', 'dp'), axis=0, tiled=True)  101 us
    reduce_scatter x1, waiting for transfers between devices, local(): lax.psum_scatter(layer_grads[3], ('tower', 'dp'), scatter_dimension=0, ti...  76.9 us
    psum x1, blocking collectives, local(): lax.psum((norm_grads, loss_part, scale_part), ('tower', 'dp'))  58.1 us
    all_gather x1, waiting for transfers between devices, local(): lax.all_gather(ffn_in.astype(jnp.bfloat16), ('tower', 'dp'), axis=0, tile...  52.4 us
  transfers between devices with their start and end apart: 15, of which 13 were waited for; matrix products, arithmetic and copies ran while one was open for 4% of the time, Pallas kernels for 0%

commit v1 on v0

v1 whole, which is shorter than its diff:
```python
import jax
import jax.numpy as jnp
from jax import lax
from jax.sharding import PartitionSpec as P
from jax.experimental import pallas as pl
from jax.experimental.pallas import tpu as pltpu

HDIM = 64
STEP = 5

norm_eps = 1e-06
cap_value = 3.4
clip_max = 0.01
beta_one = 0.9
beta_two = 0.999
learn_rate = 0.02
out_rate = 0.05
norm_rate = 0.3
decay_rate = 0.01
adam_eps = 1e-08
neg_large = -1e30
highest = lax.Precision.HIGHEST
f32 = jnp.float32
bf16 = jnp.bfloat16
MESH = pl.DeviceIdType.MESH
ANY = pl.BlockSpec(memory_space=pl.ANY)
VM = pl.BlockSpec(memory_space=pltpu.VMEM)


def sds(shape, dtype):
    return jax.ShapeDtypeStruct(shape, dtype)


def params(ident, limit=58):
    return pltpu.CompilerParams(
        collective_id=ident, has_side_effects=True, vmem_limit_bytes=limit << 20
    )


class Place:
    def __init__(self):
        self.n_dp = lax.axis_size("dp")
        self.count = self.n_dp.bit_length() - 1
        self.t = lax.axis_index("tower")
        self.d = lax.axis_index("dp")
        self.m = lax.axis_index("mp")
        self.bits = [(self.d // (1 << (self.count - 1 - j))) % 2 for j in range(self.count)]

    def across(self, dim):
        if dim == "t":
            return {"tower": 1 - self.t}
        if dim == "y":
            return {"mp": 1 - self.m}
        step = 1 << (self.count - 1 - dim)
        return {"dp": self.d + (1 - 2 * self.bits[dim]) * step}

    def mixed(self, rel):
        out = self.d
        for j in range(self.count):
            step = 1 << (self.count - 1 - j)
            if rel & step:
                out = out + (1 - 2 * self.bits[j]) * step
        return out


def remote(src, dst, send, recv, where):
    return pltpu.make_async_remote_copy(
        src_ref=src, dst_ref=dst, send_sem=send, recv_sem=recv, device_id=where, device_id_type=MESH
    )


def greet(peers):
    barrier = pltpu.get_barrier_semaphore()
    for where in peers:
        pl.semaphore_signal(barrier, inc=1, device_id=where, device_id_type=MESH)
    pl.semaphore_wait(barrier, len(peers))


def tdot(lhs, rhs):
    return lax.dot_general(lhs, rhs, (((1,), (1,)), ((), ())), preferred_element_type=f32)


def mdot(lhs, rhs):
    return jnp.dot(lhs, rhs, preferred_element_type=f32)


class Gather:
    def __init__(self, here, shard, full, other, order, sems, local_sem):
        self.here, self.shard, self.full, self.other = here, shard, full, other
        self.order, self.sems, self.local_sem = order, sems, local_sem
        self.done = set()
        self.live = []
        self.arrays = [full]
        self.slot = 0

    def view(self):
        here = self.here
        return (here.t,) + tuple(
            slice(None) if j in self.done else here.bits[j] for j in range(here.count)
        )

    def begin(self):
        self.place = pltpu.make_async_copy(
            self.shard, self.full.at[self.view()], self.local_sem
        )
        self.place.start()
        self.sent = []

    def stage(self, step):
        here = self.here
        if step > 0:
            for copy in self.live:
                copy.wait_recv()
        if step == 1:
            self.place.wait()
        self.sent += self.live
        self.live = []
        if step == len(self.order):
            for copy in self.sent:
                copy.wait_send()
            return
        dim = self.order[step]
        pairs = []
        if dim == "y":
            pairs = [(self.full.at[self.view()], self.other.at[self.view()])]
            self.arrays = [self.full, self.other]
        elif dim == "t":
            pairs = [(ref.at[here.t], ref.at[here.t]) for ref in self.arrays]
        elif step == 0:
            pairs = [(self.shard, self.full.at[self.view()])]
        else:
            pairs = [(ref.at[self.view()], ref.at[self.view()]) for ref in self.arrays]
        for src, dst in pairs:
            copy = remote(
                src, dst, self.sems[0].at[self.slot], self.sems[1].at[self.slot], here.across(dim)
            )
            copy.start()
            self.live.append(copy)
            self.slot += 1
        if dim not in ("t", "y"):
            self.done.add(dim)


def run_gathers(gathers):
    longest = max(len(g.order) for g in gathers)
    for tick in range(longest + len(gathers)):
        for lag, g in enumerate(gathers):
            step = tick - lag
            if 0 <= step <= len(g.order):
                g.stage(step)


def gather_orders(count):
    far = list(range(count - 1))
    near = [count - 1]
    return {
        "plain": far + near + ["t"],
        "late": far + near + ["y", "t"],
        "early": far + ["y"] + near + ["t"],
    }


def fetch_body(kinds, room, *refs):
    here = Place()
    n, count = here.n_dp, here.count
    refs = list(refs)
    table, lists = refs[0], refs[1]
    shards = refs[2 : 2 + len(kinds)]
    pos = 2 + len(kinds)
    rows, heard, flag = refs[pos : pos + 3]
    pos += 3
    fulls = []
    for kind in kinds:
        if kind == "plain":
            fulls.append((refs[pos], None))
            pos += 1
        else:
            fulls.append((refs[pos], refs[pos + 1]))
            pos += 2
    low_table, served, flags = refs[pos : pos + 3]
    pos += 3
    lows = refs[pos : pos + len(kinds)]
    pos += len(kinds)
    lsem, rsem, ysem, fsem, wsend, wrecv, wlocal = refs[pos:]

    peers = [{"dp": here.mixed(k)} for k in range(1, n)]
    greet(peers + [here.across("t"), here.across("y")])

    list_copies = []
    for k in range(1, n):
        copy = remote(lists.at[k], heard.at[k], lsem.at[0, k], lsem.at[1, k], {"dp": here.mixed(k)})
        copy.start()
        list_copies.append(copy)
    orders = gather_orders(count)
    gathers = []
    for j, kind in enumerate(kinds):
        lows[j][...] = shards[j][...].astype(bf16)
        gathers.append(
            Gather(
                here, lows[j], fulls[j][0], fulls[j][1], orders[kind],
                (wsend.at[j], wrecv.at[j]), wlocal.at[j],
            )
        )
        gathers[-1].begin()
    heard[0] = lists[0]
    low_table[...] = table[...].astype(bf16)
    row_count = table.shape[0]
    out_copies = []
    y_copies = []
    for k in range(n):
        if k > 0:
            list_copies[k - 1].wait_recv()
        column = jnp.transpose(heard[k])[:room, 0:1]
        hot = (lax.broadcasted_iota(jnp.int32, (room, row_count), 1) == column).astype(f32)
        found = mdot(hot.astype(bf16), low_table[...]).astype(bf16)
        if k == 0:
            rows[here.m, 0] = found
            copy = remote(
                rows.at[here.m, 0], rows.at[here.m, 0], ysem.at[0, 0], ysem.at[1, 0], here.across("y")
            )
            copy.start()
            y_copies.append(copy)
        else:
            served[k] = found
            copy = remote(
                served.at[k], rows.at[here.m, k], rsem.at[0, k], rsem.at[1, k],
                {"dp": here.mixed(k)},
            )
            copy.start()
            out_copies.append(copy)
    own_flag = jnp.max(heard[...], axis=0)
    flags[0] = own_flag
    flag_copy = remote(flags.at[0], flags.at[1], fsem.at[0], fsem.at[1], here.across("t"))
    flag_copy.start()
    for k in range(1, n):
        out_copies[k - 1].wait_recv()
        copy = remote(
            rows.at[here.m, k], rows.at[here.m, k], ysem.at[0, k], ysem.at[1, k], here.across("y")
        )
        copy.start()
        y_copies.append(copy)
    run_gathers(gathers)
    flag_copy.wait()
    flag[...] = jnp.maximum(flags[0], flags[1])
    for copy in list_copies + out_copies:
        copy.wait_send()
    for copy in y_copies:
        copy.wait()


def fetch(table, lists, shards, kinds, room):
    n_dp = lists.shape[0]
    count = n_dp.bit_length() - 1
    halves = (2,) + (2,) * count
    width = table.shape[1]
    outs = [
        sds((2, n_dp, room, width), bf16),
        sds(lists.shape, jnp.int32),
        sds(lists.shape[1:], jnp.int32),
    ]
    specs = [VM, VM, VM]
    for shard, kind in zip(shards, kinds):
        full = sds(halves + shard.shape, bf16)
        outs += [full] if kind == "plain" else [full, full]
        specs += [ANY] if kind == "plain" else [ANY, ANY]
    dma = pltpu.SemaphoreType.DMA
    steps = count + 6
    scratch = (
        [
            pltpu.VMEM(table.shape, bf16),
            pltpu.VMEM((n_dp, room, width), bf16),
            pltpu.VMEM((2,) + lists.shape[1:], jnp.int32),
        ]
        + [pltpu.VMEM(shard.shape, bf16) for shard in shards]
        + [dma((2, n_dp)), dma((2, n_dp)), dma((2, n_dp)), dma((2,))]
        + [dma((len(kinds), steps)), dma((len(kinds), steps)), dma((len(kinds),))]
    )
    out = pl.pallas_call(
        lambda *refs: fetch_body(kinds, room, *refs),
        out_shape=outs,
        in_specs=[VM] * (2 + len(shards)),
        out_specs=specs,
        scratch_shapes=scratch,
        compiler_params=params(1),
        name="fetch",
    )(table, lists, *shards)
    rows, heard, flag = out[:3]
    weights, pos = [], 3
    for shard, kind in zip(shards, kinds):
        whole = (2 * n_dp * shard.shape[0], shard.shape[1])
        if kind == "plain":
            weights.append(out[pos].reshape(whole))
            pos += 1
        else:
            weights.append((out[pos].reshape(whole), out[pos + 1].reshape(whole)))
            pos += 2
    return rows, heard, flag, weights


def turned(values):
    lanes = lax.broadcasted_iota(jnp.int32, values.shape, 1) % HDIM
    size = values.shape[1]
    return jnp.where(
        lanes < HDIM // 2,
        -pltpu.roll(values, size - HDIM // 2, 1),
        pltpu.roll(values, HDIM // 2, 1),
    )


def norm_parts(stream):
    average = jnp.mean(stream, -1, keepdims=True)
    centered = stream - average
    variance = jnp.mean(centered * centered, -1, keepdims=True)
    scale = lax.rsqrt(variance + norm_eps)
    return centered * scale, scale


def forward_body(rows, pos, norm_rows, w_qkv, cosine, sine, seg_row, seg_col,
                 emb_out, zero_out, input_out, q_out, k_out, v_out, lse_out, att_out, vt):
    tok = pos.shape[0]
    half = tok // 2
    width = rows.shape[3]
    slots = rows.shape[1] * rows.shape[2]
    feats = q_out.shape[1]
    block = 256

    @pl.loop(0, tok // block)
    def _(i):
        at = pl.ds(pl.multiple_of(i * block, block), block)
        hot = (lax.broadcasted_iota(jnp.int32, (block, slots), 1) == pos[at, :]).astype(f32)
        hot = hot.astype(bf16)
        emb = jnp.concatenate(
            [mdot(hot, rows[h].reshape(slots, width)) for h in range(2)], 1
        )
        hat, _scale = norm_parts(emb)
        stream = hat * norm_rows[0:1, :] + norm_rows[1:2, :]
        low = stream.astype(bf16)
        input_out[at, :] = low

        @pl.when(i < half // block)
        def _():
            emb_out[at, :] = emb.astype(bf16)
            zero_out[at, :] = stream

        cos, sin = cosine[at, :], sine[at, :]
        for c in range(3):
            proj = mdot(low, w_qkv[:, c * feats : (c + 1) * feats])
            for g in range(feats // 128):
                cols = slice(g * 128, (g + 1) * 128)
                part = proj[:, cols]
                if c < 2:
                    part = part * cos + turned(part) * sin
                part = part.astype(bf16)
                if c == 0:
                    q_out[at, cols] = part * bf16(HDIM**-0.5)
                elif c == 1:
                    k_out[at, cols] = part
                else:
                    v_out[at, cols] = part

    lane = lax.broadcasted_iota(jnp.int32, (1, 128), 1)
    for g in range(feats // 128):
        cols = slice(g * 128, (g + 1) * 128)
        vt[...] = jnp.transpose(v_out[:, cols].astype(f32)).astype(bf16)
        keys = [
            jnp.where((lane // HDIM) == h, k_out[:, cols], bf16(0)) for h in range(2)
        ]

        @pl.loop(0, tok // block)
        def _(i):
            at = pl.ds(pl.multiple_of(i * block, block), block)
            query = q_out[at, cols]
            same = seg_col[...] == seg_row[:, at]
            outs = []
            for h in range(2):
                scores = jnp.where(same, tdot(keys[h], query), neg_large)
                peak = jnp.max(scores, 0, keepdims=True)
                soft = jnp.exp(scores - peak)
                total = jnp.sum(soft, 0, keepdims=True)
                lse_out[2 * g + h, :, at] = peak + jnp.log(total)
                soft = (soft * (1.0 / total)).astype(bf16)
                outs.append(mdot(vt[h * HDIM : (h + 1) * HDIM, :], soft))
            att_out[at, cols] = jnp.transpose(jnp.concatenate(outs, 0)).astype(bf16)


def forward_attention(rows, pos, norm_rows, w_qkv, cosine, sine, seg_row, seg_col):
    tok = pos.shape[0]
    width = 2 * rows.shape[3]
    feats = w_qkv.shape[1] // 3
    half = tok // 2
    return pl.pallas_call(
        forward_body,
        out_shape=[
            sds((half, width), bf16),
            sds((half, width), f32),
            sds((tok, width), bf16),
            sds((tok, feats), bf16),
            sds((tok, feats), bf16),
            sds((tok, feats), bf16),
            sds((feats // HDIM, 1, tok), f32),
            sds((tok, feats), bf16),
        ],
        in_specs=[VM] * 8,
        out_specs=[VM] * 8,
        scratch_shapes=[pltpu.VMEM((128, tok), bf16)],
        compiler_params=pltpu.CompilerParams(vmem_limit_bytes=58 << 20),
        name="forward",
    )(rows, pos, norm_rows, w_qkv, cosine, sine, seg_row, seg_col)


def backward_body(query, key, value, grad_att, lse, cosine, sine, seg_row, seg_col,
                  out, kt, dq, dk, dv):
    tok, feats = query.shape
    block = 256
    lane = lax.broadcasted_iota(jnp.int32, (1, 128), 1)
    for g in range(feats // 128):
        cols = slice(g * 128, (g + 1) * 128)
        kt[...] = jnp.transpose(key[:, cols].astype(f32)).astype(bf16)
        keys = [jnp.where((lane // HDIM) == h, key[:, cols], bf16(0)) for h in range(2)]
        values = [jnp.where((lane // HDIM) == h, value[:, cols], bf16(0)) for h in range(2)]
        dk[...] = jnp.zeros_like(dk)
        dv[...] = jnp.zeros_like(dv)

        @pl.loop(0, tok // block)
        def _(i):
            at = pl.ds(pl.multiple_of(i * block, block), block)
            q_part = query[at, cols]
            g_part = grad_att[at, cols]
            same = seg_col[...] == seg_row[:, at]
            turns = []
            for h in range(2):
                mine = (lane // HDIM) == h
                scores = jnp.where(same, tdot(keys[h], q_part), neg_large)
                soft = jnp.exp(scores - lse[2 * g + h, :, at])
                grad_soft = tdot(values[h], g_part)
                inner = jnp.sum(soft * grad_soft, 0, keepdims=True)
                grad_scores = (soft * (grad_soft - inner)).astype(bf16)
                dv[...] += mdot(soft.astype(bf16), jnp.where(mine, g_part, bf16(0)))
                dk[...] += mdot(grad_scores, jnp.where(mine, q_part, bf16(0)))
                turns.append(mdot(kt[h * HDIM : (h + 1) * HDIM, :], grad_scores))
            dq[at, :] = jnp.transpose(jnp.concatenate(turns, 0)) * (HDIM**-0.5)

        cos, sin = cosine[...], sine[...]
        for c, grad in ((0, dq), (1, dk)):
            whole = grad[...]
            back = whole * cos - turned(whole) * sin
            out[:, c * feats + g * 128 : c * feats + (g + 1) * 128] = back.astype(bf16)
        out[:, 2 * feats + g * 128 : 2 * feats + (g + 1) * 128] = dv[...].astype(bf16)


def backward_attention(query, key, value, grad_att, lse, cosine, sine, seg_row, seg_col):
    tok, feats = query.shape
    return pl.pallas_call(
        backward_body,
        out_shape=sds((tok, 3 * feats), bf16),
        in_specs=[VM] * 9,
        out_specs=VM,
        scratch_shapes=[pltpu.VMEM((128, tok), bf16)] + [pltpu.VMEM((tok, 128), f32)] * 3,
        compiler_params=pltpu.CompilerParams(vmem_limit_bytes=58 << 20),
        name="backward",
    )(query, key, value, grad_att, lse, cosine, sine, seg_row, seg_col)


def loss_body(part, counts, doc_ok, query_ok, target, scale, grad_out, stats, other, low_all, turn,
              psend, precv, esend, erecv):
    here = Place()
    n = here.n_dp
    slots, width = part.shape
    peers = []
    for rt in range(2):
        for rd in range(n):
            if rt or rd:
                peers.append(
                    (rt * n + rd, {"tower": here.t + rt * (1 - 2 * here.t), "dp": here.mixed(rd)})
                )
    greet([where for _, where in peers] + [here.across("y")])
    copy = remote(part, other, psend, precv, here.across("y"))
    copy.start()
    copy.wait()
    pooled = (part[...] + other[...]) / counts[...]
    scale_row = lax.rsqrt(jnp.sum(pooled * pooled, 1, keepdims=True) + 1e-06)
    unit = pooled * scale_row
    low_all[here.t, here.d] = unit.astype(bf16)
    copies = []
    for rel, where in peers:
        copy = remote(
            low_all.at[here.t, here.d], low_all.at[here.t, here.d], esend.at[rel], erecv.at[rel], where
        )
        copy.start()
        copies.append(copy)
    for copy in copies:
        copy.wait()
    total = n * slots
    queries = low_all[0].reshape(total, width)
    documents = low_all[1].reshape(total, width)
    cosines = tdot(queries, documents)
    factor = jnp.exp(jnp.minimum(scale[...], cap_value))
    logits = jnp.where(doc_ok[...] > 0, factor * cosines, neg_large)
    peak = jnp.max(logits, 1, keepdims=True)
    log_total = peak + jnp.log(jnp.sum(jnp.exp(logits - peak), 1, keepdims=True))
    soft = jnp.exp(logits - log_total)
    mask = lax.broadcasted_iota(jnp.int32, (total, total), 1) == target[...]
    picked = jnp.sum(jnp.where(mask, logits, 0.0), 1, keepdims=True)
    valid = query_ok[...] > 0
    query_count = jnp.sum(valid.astype(f32), axis=0, keepdims=True)
    loss_sum = jnp.sum(jnp.where(valid, log_total - picked, 0.0), axis=0, keepdims=True)
    grad_logits = jnp.where(valid, soft - mask.astype(f32), 0.0) / query_count
    by_row = jnp.sum(grad_logits * cosines, 1, keepdims=True)
    grad_scale = (
        jnp.sum(by_row, 0, keepdims=True) * factor * (scale[...] < cap_value).astype(f32)
    )
    grad_cos = factor * grad_logits
    at = pl.ds(pl.multiple_of(here.d * slots, slots), slots)
    turn[0] = grad_cos
    turn[1] = jnp.transpose(grad_cos)
    left = turn[here.t, at, :].astype(bf16)
    right = low_all[1 - here.t].reshape(total, width)
    grad_unit = mdot(left, right)
    grad_pooled = scale_row * (
        grad_unit - unit * jnp.sum(unit * grad_unit, 1, keepdims=True)
    )
    grad_out[...] = grad_pooled / counts[...]
    row = lax.broadcasted_iota(jnp.int32, stats.shape, 0)
    stats[...] = jnp.where(row == 0, loss_sum, jnp.where(row == 1, query_count, grad_scale))


def loss_step(part, counts, doc_ok, query_ok, target, scale):
    n_dp = lax.axis_size("dp")
    slots, width = part.shape
    total = n_dp * slots
    dma = pltpu.SemaphoreType.DMA
    return pl.pallas_call(
        loss_body,
        out_shape=[sds(part.shape, f32), sds((8, 128), f32)],
        in_specs=[VM] * 6,
        out_specs=[VM] * 2,
        scratch_shapes=[
            pltpu.VMEM(part.shape, f32),
            pltpu.VMEM((2, n_dp, slots, width), bf16),
            pltpu.VMEM((2, total, total), f32),
            dma, dma, dma((2 * n_dp,)), dma((2 * n_dp,)),
        ],
        compiler_params=params(2),
        name="loss",
    )(part, counts, doc_ok, query_ok, target, scale)


class Scatter:
    def __init__(self, here, own, other, order, held, landed, out, sems):
        self.here, self.own, self.other, self.order = here, own, other, order
        self.held, self.landed, self.out, self.sems = held, landed, out, sems
        self.fixed = {}
        self.live = []
        self.sent = []
        self.slot = 0
        self.land = 0
        self.arrays = [0] if other is None else [0, 1]

    def view(self, extra=None):
        fixed = dict(self.fixed)
        if extra:
            fixed.update(extra)
        return tuple(fixed.get(j, slice(None)) for j in range(self.here.count))

    def send(self, src, where, index):
        here = self.here
        dst = self.landed[self.land]
        copy = remote(src, dst, self.sems[0].at[self.slot], self.sems[1].at[self.slot], where)
        copy.start()
        self.slot += 1
        self.live.append((copy, self.land, index))
        self.land += 1

    def start(self, step):
        here = self.here
        dim = self.order[step]
        if dim == "t":
            for index in self.arrays:
                src = (self.own, self.other)[index]
                self.send(src.at[1 - here.t], here.across("t"), index)
        elif dim == "y":
            self.send(self.held[1].at[self.view()], here.across("y"), 0)
            self.arrays = [0]
        else:
            bit = here.bits[dim]
            for index in self.arrays:
                self.send(self.held[index].at[self.view({dim: 1 - bit})], here.across(dim), index)

    def finish(self, step):
        here = self.here
        dim = self.order[step]
        if dim not in ("t", "y"):
            self.fixed[dim] = here.bits[dim]
        view = self.view()
        last = step == len(self.order) - 1
        for copy, land, index in self.live:
            copy.wait()
            got = self.landed[land][...].astype(f32)
            if dim == "t":
                mine = (self.own, self.other)[index][here.t]
            else:
                mine = self.held[index][view]
            total = mine.astype(f32) + got
            if last:
                self.out[...] = total
            elif dim == "t":
                self.held[index][...] = total.astype(bf16)
            else:
                self.held[index][view] = total.astype(bf16)
        self.live = []


def scatter_lands(order, count, pair, rows, cols):
    shapes, free, live = [], count, 2 if pair else 1
    for dim in order:
        if dim == "y":
            live = 1
        elif dim != "t":
            free -= 1
        shapes += [(2,) * free + (rows, cols)] * live
    return shapes


def scatter_orders(count):
    near = [count - 1]
    far = list(range(count - 2, -1, -1))
    return {
        "plain": ["t"] + near + far,
        "early": ["t", "y"] + near + far,
        "late": ["t"] + near + ["y"] + far,
    }


def run_scatters(scatters):
    longest = max(len(s.order) for s in scatters)
    for tick in range(longest + len(scatters)):
        for lag, s in enumerate(scatters):
            step = tick - lag
            if 0 < step <= len(s.order):
                s.finish(step - 1)
            if 0 <= step < len(s.order):
                s.start(step)


def reduce_body(kinds, sizes, *refs):
    here = Place()
    count = here.count
    orders = scatter_orders(count)
    refs = list(refs)
    ins, pos = [], 0
    for kind in kinds:
        if kind == "plain":
            ins.append((refs[pos], None))
            pos += 1
        else:
            ins.append((refs[pos], refs[pos + 1]))
            pos += 2
    outs = refs[pos : pos + len(kinds)]
    pos += len(kinds)
    scatters = []
    held_all, land_all = [], []
    for kind in kinds:
        width = 1 if kind == "plain" else 2
        held_all.append(refs[pos : pos + width])
        pos += width
    for kind, (rows, cols) in zip(kinds, sizes):
        amount = len(scatter_lands(orders[kind], count, kind != "plain", rows, cols))
        land_all.append(refs[pos : pos + amount])
        pos += amount
    send, recv = refs[pos:]
    greet([here.across("t"), here.across("y")] + [here.across(j) for j in range(count)])
    for j, kind in enumerate(kinds):
        scatters.append(
            Scatter(
                here, ins[j][0], ins[j][1], orders[kind], held_all[j], land_all[j], outs[j],
                (send.at[j], recv.at[j]),
            )
        )
    run_scatters(scatters)


def reduce_grads(grads, kinds, ident):
    n_dp = lax.axis_size("dp")
    count = n_dp.bit_length() - 1
    orders = scatter_orders(count)
    args, sizes, held, lands, outs = [], [], [], [], []
    for grad, kind in zip(grads, kinds):
        pair = [grad] if kind == "plain" else list(grad)
        rows, cols = pair[0].shape[0] // (2 * n_dp), pair[0].shape[1]
        sizes.append((rows, cols))
        args += [g.reshape((2,) + (2,) * count + (rows, cols)) for g in pair]
        held += [pltpu.VMEM((2,) * count + (rows, cols), bf16)] * len(pair)
        lands += [
            pltpu.VMEM(shape, bf16)
            for shape in scatter_lands(orders[kind], count, len(pair) == 2, rows, cols)
        ]
        outs.append(sds((rows, cols), f32))
    dma = pltpu.SemaphoreType.DMA
    steps = 2 * count + 6
    return pl.pallas_call(
        lambda *refs: reduce_body(kinds, sizes, *refs),
        out_shape=outs,
        in_specs=[VM] * len(args),
        out_specs=[VM] * len(outs),
        scratch_shapes=held + lands + [dma((len(kinds), steps)), dma((len(kinds), steps))],
        compiler_params=params(ident),
        name="reduce",
    )(*args)


def spread_body(room, grad, pos, heard, norm_grad, out, lists_out, norms_out,
                other, packed, mine, theirs, heard_o, norms,
                ysem, rsem, csem, lsem, nsem):
    here = Place()
    n = here.n_dp
    width = grad.shape[1] // 2
    half = grad.shape[0]
    slots = n * room
    peers = []
    for rt in range(2):
        for rd in range(n):
            for rm in range(2):
                if rt or rd or rm:
                    peers.append(
                        (
                            (rt * n + rd) * 2 + rm,
                            {
                                "tower": here.t + rt * (1 - 2 * here.t),
                                "dp": here.mixed(rd),
                                "mp": here.m + rm * (1 - 2 * here.m),
                            },
                        )
                    )
    greet([where for _, where in peers])
    theirs_at = pl.ds(pl.multiple_of((1 - here.m) * width, 128), width)
    mine_at = pl.ds(pl.multiple_of(here.m * width, 128), width)
    swap = remote(grad.at[:, theirs_at], other, ysem.at[0], ysem.at[1], here.across("y"))
    swap.start()
    list_copy = remote(heard, heard_o, lsem.at[0], lsem.at[1], here.across("t"))
    list_copy.start()
    me = (here.t * n + here.d) * 2 + here.m
    norm_copies = []
    for rel, where in peers:
        copy = remote(norm_grad, norms.at[me], nsem.at[0, rel], nsem.at[1, rel], where)
        copy.start()
        norm_copies.append(copy)
    norms[me] = norm_grad[...]
    swap.wait()
    both = jnp.concatenate([grad[:, mine_at], other[...]], 0)
    copies = []
    for k in list(range(1, n)) + [0]:
        hot = (
            lax.broadcasted_iota(jnp.int32, (room, pos.shape[1]), 0) + k * room == pos[...]
        ).astype(f32)
        packed[k] = mdot(hot.astype(bf16), both).astype(bf16)
        if k:
            copy = remote(
                packed.at[k], mine.at[k], rsem.at[0, k], rsem.at[1, k], {"dp": here.mixed(k)}
            )
        else:
            mine[0] = packed[0]
            copy = remote(mine.at[0], theirs.at[0], csem.at[0, 0], csem.at[1, 0], here.across("t"))
        copy.start()
        copies.append(copy)
    passed = [copies.pop()]
    for k in range(1, n):
        copies[k - 1].wait_recv()
        copy = remote(mine.at[k], theirs.at[k], csem.at[0, k], csem.at[1, k], here.across("t"))
        copy.start()
        passed.append(copy)
    for copy in copies:
        copy.wait_send()
    for copy in passed:
        copy.wait()
    list_copy.wait()
    row_count = out.shape[0]
    block = row_count
    for size in range(512, 255, -8):
        if row_count % size == 0:
            block = size
            break

    @pl.loop(0, row_count // block)
    def _(i):
        at = pl.ds(pl.multiple_of(i * block, 8) if block != row_count else 0, block)
        base = lax.broadcasted_iota(jnp.int32, (block, room), 0) + i * block
        hots = []
        for source in (heard, heard_o):
            for k in range(n):
                hots.append((base == source[k, 0:1, :room]).astype(f32).astype(bf16))
        whole = jnp.concatenate(hots, 1)
        data = jnp.concatenate(
            [mine[...].reshape(slots, width), theirs[...].reshape(slots, width)], 0
        )
        out[at, :] = mdot(whole, data)

    for copy in norm_copies:
        copy.wait()
    total = norms[0]
    for j in range(1, 4 * n):
        total = total + norms[j]
    norms_out[...] = total


def spread_rows(grad, pos_row, heard, norm_grad, row_count, room):
    n_dp = lax.axis_size("dp")
    width = grad.shape[1] // 2
    half = grad.shape[0]
    dma = pltpu.SemaphoreType.DMA

    def body(grad, pos, heard, norm_grad, out, norms_out, *scratch):
        spread_body(room, grad, pos, heard, norm_grad, out, None, norms_out, *scratch)

    return pl.pallas_call(
        body,
        out_shape=[sds((row_count, width), f32), sds(norm_grad.shape, f32)],
        in_specs=[VM] * 4,
        out_specs=[VM] * 2,
        scratch_shapes=[
            pltpu.VMEM((half, width), bf16),
            pltpu.VMEM((n_dp, room, width), bf16),
            pltpu.VMEM((n_dp, room, width), bf16),
            pltpu.VMEM((n_dp, room, width), bf16),
            pltpu.VMEM(heard.shape, jnp.int32),
            pltpu.VMEM((4 * n_dp,) + norm_grad.shape, f32),
            dma((2,)), dma((2, n_dp)), dma((2, n_dp)), dma((2,)), dma((2, 4 * n_dp)),
        ],
        compiler_params=params(5),
        name="spread",
    )(grad, pos_row, heard, norm_grad)


def total_body(value, out, parts, send, recv):
    here = Place()
    n = here.n_dp
    peers = []
    for rt in range(2):
        for rd in range(n):
            for rm in range(2):
                if rt or rd or rm:
                    where = {
                        "tower": here.t + rt * (1 - 2 * here.t),
                        "dp": here.mixed(rd),
                        "mp": here.m + rm * (1 - 2 * here.m),
                    }
                    peers.append(((rt * n + rd) * 2 + rm, where))
    greet([where for _, where in peers])
    me = (here.t * n + here.d) * 2 + here.m
    copies = []
    for rel, where in peers:
        copy = remote(value, parts.at[me], send.at[rel], recv.at[rel], where)
        copy.start()
        copies.append(copy)
    parts[me] = value[...]
    for copy in copies:
        copy.wait()
    out[...] = jnp.sum(parts[...], 0)


def total_of(value):
    n_dp = lax.axis_size("dp")
    dma = pltpu.SemaphoreType.DMA
    return pl.pallas_call(
        total_body,
        out_shape=sds(value.shape, f32),
        in_specs=[VM],
        out_specs=VM,
        scratch_shapes=[
            pltpu.VMEM((4 * n_dp,) + value.shape, f32), dma((4 * n_dp,)), dma((4 * n_dp,))
        ],
        compiler_params=params(6),
        name="total",
    )(value)


def swap(values):
    return lax.ppermute(values, "mp", [(0, 1), (1, 0)])


def rotary_tables(positions):
    half_dim = HDIM // 2
    inverse = 1000.0 ** (-2.0 * jnp.arange(half_dim, dtype=f32) / HDIM)
    angles = positions.astype(f32)[:, None] * inverse[None, :]
    angles = jnp.concatenate([angles] * 4, 1)
    return jnp.cos(angles), jnp.sin(angles)


def layout(lengths, places, slot_count):
    end_points = jnp.cumsum(lengths)
    segment = jnp.sum((places[:, None] >= end_points[None, :]).astype(jnp.int32), 1)
    starts = jnp.concatenate([jnp.zeros((1,), jnp.int32), end_points])
    slot_ids = jnp.arange(slot_count + 1, dtype=jnp.int32)
    segment_start = jnp.sum(jnp.where(segment[:, None] == slot_ids[None, :], starts[None, :], 0), 1)
    return segment, places - segment_start


def norm_back(grad, hat, scale, gain):
    grad_hat = grad * gain
    first = jnp.mean(grad_hat, -1, keepdims=True)
    second = jnp.mean(grad_hat * hat, -1, keepdims=True)
    return (
        scale * (grad_hat - first - hat * second),
        jnp.sum(grad * hat, 0),
        jnp.sum(grad, 0),
    )


def glu(gate_vals, up_vals):
    return jax.nn.silu(gate_vals) * up_vals


def adamw(weight_in, gradient, first_mom, second, factor, step_num, rate):
    gradient = gradient * factor
    first_new = beta_one * first_mom + (1.0 - beta_one) * gradient
    second_new = beta_two * second + (1.0 - beta_two) * gradient * gradient
    first_hat = first_new / (1.0 - beta_one**step_num)
    second_hat = second_new / (1.0 - beta_two**step_num)
    weight_new = weight_in - rate * (
        first_hat / (jnp.sqrt(second_hat) + adam_eps) + decay_rate * weight_in
    )
    return (weight_new, first_new, second_new)


def name_rows(ids, d, n_dp, row_count, room):
    tok = ids.shape[0]
    owner = ids // row_count
    local = ids - owner * row_count
    order = jnp.bitwise_xor(owner, d)
    places = jnp.arange(tok, dtype=jnp.int32)
    first_at = jnp.min(
        jnp.where(ids[:, None] == ids[None, :], places[None, :], tok), 1
    )
    is_first = first_at == places
    slot = jnp.sum(
        (
            (places[None, :] < first_at[:, None])
            & is_first[None, :]
            & (owner[None, :] == owner[:, None])
        ).astype(jnp.int32),
        1,
    )
    over = jnp.max(slot) >= room
    pos = order * room + slot
    wanted = jnp.arange(n_dp * room, dtype=jnp.int32)
    listed = jnp.max(
        jnp.where((pos[None, :] == wanted[:, None]) & is_first[None, :], local[None, :], -1), 1
    ).reshape(n_dp, 1, room)
    listed = jnp.pad(listed, ((0, 0), (0, 0), (0, 128 - room)), constant_values=-1)
    flag = jnp.broadcast_to(over.astype(jnp.int32), (n_dp, 7, 128))
    return pos, jnp.concatenate([listed, flag], 1)


def local(
    token_ids, seq_lengths, positives, embedding, attn_in, attn_out, ffn_in, ffn_out, norm_params,
    logit_scale, embed_m, embed_v, attn_in_m, attn_in_v, attn_out_m, attn_out_v, ffn_in_m, ffn_in_v,
    ffn_out_m, ffn_out_v, norm_m, norm_v, scale_m, scale_v,
):
    n_dp = lax.axis_size("dp")
    tower_idx = lax.axis_index("tower")
    data_idx = lax.axis_index("dp")
    model_idx = lax.axis_index("mp")
    slot_count = seq_lengths.shape[2]
    ids = token_ids[0]
    tok = ids.shape[0]
    half = tok // 2
    row_count, width = embedding.shape
    room = max(32, tok // n_dp)
    heads_cols = attn_out.shape[1]
    ff = ffn_out.shape[1]

    pos, lists = name_rows(ids, data_idx, n_dp, row_count, room)
    kinds = ("plain", "late", "late", "early", "late")
    shards = (
        attn_in.reshape(attn_in.shape[0], -1), attn_out, ffn_in[:, 0], ffn_in[:, 1], ffn_out,
    )
    rows, heard, flag, weights = fetch(embedding, lists, shards, kinds, room)
    w_qkv, w_out, w_gate, w_up, w_down = weights
    crowded = flag[1, 0] > 0

    def whole_table(_):
        table = lax.all_gather(embedding.astype(bf16), "dp", axis=0, tiled=True)
        mine = jnp.take(table, jnp.clip(ids, 0, table.shape[0] - 1), axis=0)
        both = lax.all_gather(mine, "mp", axis=0)
        extra = n_dp * room - tok
        both = jnp.pad(both, ((0, 0), (0, extra), (0, 0)))
        return both.reshape(rows.shape), jnp.arange(tok, dtype=jnp.int32)

    rows, pos_used = lax.cond(crowded, whole_table, lambda _: (rows, pos), None)
    shift = model_idx * half
    places = (jnp.arange(tok, dtype=jnp.int32) + shift) % tok
    pos_rel = jnp.where(
        model_idx == 0, pos_used, jnp.concatenate([pos_used[half:], pos_used[:half]])
    )
    pos_back = jnp.where(model_idx == 0, pos, jnp.concatenate([pos[half:], pos[:half]]))
    lengths_row = seq_lengths[tower_idx, data_idx]
    segment, positions = layout(lengths_row, places, slot_count)
    cosine, sine = rotary_tables(positions)
    seg_row, seg_col = segment[None, :], segment[:, None]
    emb, stream_zero, input_zero, query, key, value, lse, attended = forward_attention(
        rows, pos_rel[:, None], norm_params[0:2], w_qkv, cosine, sine, seg_row, seg_col
    )
    att = (attended[:half], swap(attended[half:]))

    sum_one = stream_zero + tdot(att[0], w_out[0]) + tdot(att[1], w_out[1])
    hat_one, scale_one = norm_parts(sum_one)
    stream_one = hat_one * norm_params[2] + norm_params[3]
    input_one = stream_one.astype(bf16)
    gates = [mdot(input_one, w_gate[j]) for j in range(2)]
    ups = [mdot(input_one, w_up[j]) for j in range(2)]
    hidden = [glu(gates[j], ups[j]).astype(bf16) for j in range(2)]
    sum_two = stream_one + tdot(hidden[0], w_down[0]) + tdot(hidden[1], w_down[1])
    hat_two, scale_two = norm_parts(sum_two)
    stream_two = hat_two * norm_params[4] + norm_params[5]

    member = (segment[None, :half] == jnp.arange(slot_count, dtype=jnp.int32)[:, None]).astype(f32)
    counts = jnp.maximum(lengths_row, 1).astype(f32)[:, None]
    part = jnp.dot(member, stream_two, precision=highest)
    doc_ok = (seq_lengths[1].reshape(1, -1) > 0).astype(f32)
    query_ok = (seq_lengths[0].reshape(-1, 1) > 0).astype(f32)
    grad_pool, stats = loss_step(
        part, counts, doc_ok, query_ok, positives.reshape(-1, 1), logit_scale.reshape(1, 1)
    )
    loss_sum, query_count, scale_grad = stats[0, 0], stats[1, 0], stats[2, 0]

    grad_two = jnp.dot(member.T, grad_pool, precision=highest)
    grad_sum_two, gain_two, bias_two = norm_back(grad_two, hat_two, scale_two, norm_params[4])
    ffn_low = grad_sum_two.astype(bf16)
    grad_down, grad_gate, grad_up = [], [], []
    grad_stream_one = grad_sum_two
    for j in range(2):
        grad_down.append(jnp.einsum("td,tf->df", ffn_low, hidden[j], preferred_element_type=f32).astype(bf16))
        grad_hidden = mdot(ffn_low, w_down[j])
        d_gate, d_up = jax.vjp(glu, gates[j], ups[j])[1](grad_hidden)
        d_gate, d_up = d_gate.astype(bf16), d_up.astype(bf16)
        grad_gate.append(jnp.einsum("td,tf->df", input_one, d_gate, preferred_element_type=f32).astype(bf16))
        grad_up.append(jnp.einsum("td,tf->df", input_one, d_up, preferred_element_type=f32).astype(bf16))
        grad_stream_one = grad_stream_one + tdot(d_gate, w_gate[j]) + tdot(d_up, w_up[j])
    grad_sum_one, gain_one, bias_one = norm_back(
        grad_stream_one, hat_one, scale_one, norm_params[2]
    )
    attn_low = grad_sum_one.astype(bf16)
    grad_out = [
        jnp.einsum("td,tf->df", attn_low, att[j], preferred_element_type=f32).astype(bf16) for j in range(2)
    ]
    grad_att = jnp.concatenate(
        [mdot(attn_low, w_out[0]).astype(bf16), swap(mdot(attn_low, w_out[1]).astype(bf16))], 0
    )
    grad_proj = backward_attention(
        query, key, value, grad_att, lse, cosine, sine, seg_row, seg_col
    )
    grad_qkv = jnp.einsum("td,tf->df", input_zero, grad_proj, preferred_element_type=f32).astype(bf16)
    back = tdot(grad_proj, w_qkv)
    grad_stream_zero = grad_sum_one + back[:half] + swap(back[half:].astype(bf16)).astype(f32)
    hat_zero, scale_zero = norm_parts(emb.astype(f32))
    grad_embed, gain_zero, bias_zero = norm_back(
        grad_stream_zero, hat_zero, scale_zero, norm_params[0]
    )
    embed_low = grad_embed.astype(bf16)
    norm_part = jnp.stack([gain_zero, bias_zero, gain_one, bias_one, gain_two, bias_two])
    norm_part = jnp.pad(norm_part, ((0, 2), (0, 0)))
    embed_grad, norm_sum = spread_rows(
        embed_low, pos_back[None, :], heard, norm_part, row_count, room
    )
    norm_grad = norm_sum[:6]

    def whole_grads(_):
        column = lax.dynamic_slice_in_dim(embed_low, model_idx * width, width, 1)
        theirs = lax.dynamic_slice_in_dim(embed_low, (1 - model_idx) * width, width, 1)
        theirs = swap(theirs)
        full = jnp.where(
            model_idx == 0,
            jnp.concatenate([column, theirs], 0),
            jnp.concatenate([theirs, column], 0),
        )
        all_ids = lax.all_gather(ids, ("tower", "dp"), axis=0, tiled=True)
        piece = all_ids - data_idx * row_count
        inside = (piece >= 0) & (piece < row_count)
        return jax.ops.segment_sum(
            lax.all_gather(full, ("tower", "dp"), axis=0, tiled=True).astype(f32),
            jnp.where(inside, piece, row_count),
            num_segments=row_count + 1,
        )[:row_count]

    embed_grad = lax.cond(crowded, whole_grads, lambda _: embed_grad, None)
    r_qkv, r_out, r_gate, r_up, r_down = reduce_grads(
        (grad_qkv, grad_out, grad_gate, grad_up, grad_down),
        ("plain", "late", "late", "early", "late"), 4,
    )
    r_qkv = r_qkv.reshape(attn_in.shape)
    r_ffn = jnp.stack([r_gate, r_up], 1)
    shard_grads = (r_qkv, r_out, r_ffn, r_down)
    local_sq = sum((jnp.sum(gradient * gradient) for gradient in shard_grads)) + 0.5 * jnp.sum(
        embed_grad * embed_grad
    )
    total_sq = (
        total_of(jnp.broadcast_to(local_sq, (8, 128)))[0, 0]
        + jnp.sum(norm_grad * norm_grad)
        + scale_grad * scale_grad
    )
    grad_norm = jnp.sqrt(total_sq)
    factor = jnp.minimum(1.0, clip_max / (grad_norm + 1e-06))
    step_num = float(STEP)
    embed_new = adamw(embedding, embed_grad, embed_m, embed_v, factor, step_num, learn_rate)
    qkv_new = adamw(attn_in, shard_grads[0], attn_in_m, attn_in_v, factor, step_num, learn_rate)
    out_new = adamw(attn_out, shard_grads[1], attn_out_m, attn_out_v, factor, step_num, out_rate)
    ffn_new = adamw(ffn_in, shard_grads[2], ffn_in_m, ffn_in_v, factor, step_num, learn_rate)
    down_new = adamw(ffn_out, shard_grads[3], ffn_out_m, ffn_out_v, factor, step_num, learn_rate)
    norms_new = adamw(norm_params, norm_grad, norm_m, norm_v, factor, step_num, norm_rate)
    scale_new = adamw(
        logit_scale, scale_grad.reshape(1), scale_m, scale_v, factor, step_num, learn_rate
    )
    return (
        *embed_new, *qkv_new, *out_new, *ffn_new, *down_new, *norms_new, *scale_new,
        loss_sum.reshape(1), query_count.reshape(1), grad_norm.reshape(1),
    )


def solution(mesh):
    table, rows3, rows2 = P("dp", "mp"), P(("tower", "dp"), None, "mp"), P(("tower", "dp"), "mp")
    weights = (table, rows3, rows2, rows3, rows2)
    moments = tuple(spec for spec in weights for _ in range(2))
    return jax.shard_map(
        local,
        mesh=mesh,
        in_specs=(P("tower", "dp"), P(), P()) + weights + (P(), P()) + moments + (P(),) * 4,
        out_specs=tuple(spec for spec in weights for _ in range(3)) + (P(),) * 9,
        check_vma=False,
    )
```

time: 1790 us -> 680 us (0.38)
  waiting for transfers between devices: 1090 us -> 3.35 us
  Pallas kernels: 0 us -> 483 us
  blocking collectives: 202 us -> 0 us
  other arithmetic: 216 us -> 51.3 us
  matrix products: 148 us -> 69.5 us
  local copies, waits for them, and re-layouts: 88.5 us -> 30.4 us
    all_gather x6 -> x0, waiting for transfers between devices: 655 us -> none  [the longest x1 450 us: local(): lax.all_gather(embedding.astype(jnp.bfloat16), 'dp', axis=0, tiled=True)]
    pallas_call x0 -> x7, Pallas kernels: none -> 483 us  [the longest x1 159 us: fetch(): pl.pallas_call(lambda *refs: fetch_body(kinds, room, *refs), out_shape=ou...]
    reduce_scatter x5 -> x0, waiting for transfers between devices: 269 us -> none  [the longest x1 114 us: local(): lax.psum_scatter(layer_grads[2], ('tower', 'dp'), scatter_dimension=0, ti...]
    psum x4 -> x0, waiting for transfers between devices: 168 us -> none  [model_total(): return lax.psum(values.astype(jnp.bfloat16), 'mp').astype(jnp.float32)]
    scatter-add x1 -> x0, other arithmetic: 109 us -> none  [local(): jax.ops.segment_sum(lax.all_gather(column_part, ('tower', 'dp'), axis=0,...]
    all_gather x3 -> x0, blocking collectives: 107 us -> none  [the longest x1 37.6 us: local(): lax.all_gather(attn_out.astype(jnp.bfloat16), ('tower', 'dp'), axis=0, ti...]
    psum x2 -> x0, blocking collectives: 95.7 us -> none  [the longest x1 58.1 us: local(): lax.psum((norm_grads, loss_part, scale_part), ('tower', 'dp'))]
    dot_general x31 -> x28, matrix products: 148 us -> 69.5 us  [the longest x8 24.1 us: mdot(): return jnp.dot(lhs, rhs, preferred_element_type=f32)]
  transfers between devices with their start and end apart: 15 -> 3, of which waited for: 13 -> 2; matrix products, arithmetic and copies ran while one was open for 4% -> 3% of each run, Pallas kernels for 0% -> 23%
where the time goes in v1:
time: 680 us; the launch traced here: 674 us
  Pallas kernels  483 us (71%)
  matrix products  69.5 us (10%)
  other arithmetic  51.3 us (8%)
  local copies, waits for them, and re-layouts  30.4 us (4%)
  between operations  29.5 us (4%)
    pallas_call x1, Pallas kernels, fetch(): pl.pallas_call(lambda *refs: fetch_body(kinds, room, *refs), out_shape=ou...  159 us
    pallas_call x1, Pallas kernels, reduce_grads(): pl.pallas_call(lambda *refs: reduce_body(kinds, sizes, *refs), out_shape=...  155 us
    pallas_call x1, Pallas kernels, spread_rows(): pl.pallas_call(body, out_shape=[sds((row_count, width), f32), sds(norm_gr...  59.3 us
    pallas_call x1, Pallas kernels, forward_attention(): pl.pallas_call(forward_body, out_shape=[sds((half, width), bf16), sds((ha...  34.2 us
    pallas_call x1, Pallas kernels, loss_step(): pl.pallas_call(loss_body, out_shape=[sds(part.shape, f32), sds((8, 128),...  32.8 us
    pallas_call x1, Pallas kernels, backward_attention(): pl.pallas_call(backward_body, out_shape=sds((tok, 3 * feats), bf16), in_s...  30.4 us
    dot_general x8, matrix products, mdot(): return jnp.dot(lhs, rhs, preferred_element_type=f32)  24.1 us
    sub x6, other arithmetic, adamw(): weight_in - rate * (first_hat / (jnp.sqrt(second_hat) + adam_eps) + decay...  19 us
  transfers between devices with their start and end apart: 3, of which 2 were waited for; matrix products, arithmetic and copies ran while one was open for 3% of the time, Pallas kernels for 23%

profile of v1, /device:TPU:1, one launch (start us, length us, event | category | flops | bytes accessed | tf_op | source)
XLA Modules:
  0.0 674.2 jit_solution(1596608834387585903)
XLA Ops:
  19.2 3.0 fusion.41
  25.4 159.1 %fetch.1 = (bf16[2,8,128,384]{3,2,1,0:T(8,128)(2,1)}, s32[8,8,128]{2,1,0:T(8,128)}, s32[8,128]{1,0:T(8,128)}, bf16[2,2,2,2,48,1152]{5,4,3,2,1,0:T(8,128)(2,1)}, ...) custom-call(f32[3816,384]{1,0:T(8,128)} %refs_0_.1, ...), custom_call_target="tpu_custom_call" | custom-call | tf_op jit(solution)/shard_map/fetch/pallas_call | solution.py:278
  186.4 5.3 conditional.2
  192.7 34.2 %forward.1 = (bf16[512,768]{1,0:T(8,128)(2,1)}, f32[512,768]{1,0:T(8,128)}, bf16[1024,768]{1,0:T(8,128)(2,1)}, bf16[1024,384]{1,0:T(8,128)(2,1)}, bf16[1024,384]...) custom-call(bf16[2,8,128,384]{3,2,1,0:T(8,128)(2,1)} %get-tuple-element.89.rows, ...), custom_call_target="tpu_custom_call" | custom-call | tf_op jit(solution)/shard_map/forward/pallas_call | solution.py:391
  227.0 1.9 slice.88
  235.3 1.8 fusion.39
  237.2 2.6 collective-permute-done.1
  248.3 3.2 multiply_convert_fusion.3
  253.7 3.2 multiply_convert_fusion.2
  260.4 32.8 %loss.1 = (f32[16,768]{1,0:T(8,128)}, f32[8,128]{1,0:T(8,128)}) custom-call(f32[16,768]{1,0:T(8,128)} %fusion.28.part, f32[16,1]{1,0:T(8,128)} %maximum_convert_fusion.counts, f32[1,128]{1,0:T(1,128)} %reshape.379.doc_ok, f32[128,1]{1,0:T(8,128)} %reshape.399.query_ok, s32[128,1]{1,0:T(8,128)} %reshape.400.target, f32[1,1]{1,0:T(1,128)} %bitcast.110.scale), custom_call_target="tpu_custom_call" | custom-call | tf_op jit(solution)/shard_map/loss/pallas_call | solution.py:532
  293.2 2.3 multiply_reduce_fusion.1
  298.1 2.5 fusion.10
  301.7 11.3 %multiply_convert_fusion = (bf16[512,1536]{1,0:T(8,128)(2,1)S(1)}, bf16[512,1536]{1,0:T(8,128)(2,1)S(1)}) fusion(f32[512,1536]{1,0:T(8,128)S(1)} %copy-done.45, f32[512,1536]{1,0:T(8,128)S(1)} %copy-done.52, bf16[512,768]{1,0:T(8,128)(2,1)S(1)} %get-tuple-element.278, bf16[768,1536]{1,0:T(8,128)(2,1)S(1)} %bitcast.160), kind=kOutput, calls=%fused_computation.41 | convolution fusion | flops 1218969600 | bytes 12582912 | tf_op jit(solution)/shard_map/dot_general | solution.py:84
  318.0 2.2 multiply_reduce_fusion.2
  323.9 2.8 convolution_convert_fusion.2
  326.7 2.8 convolution_convert_fusion.5
  329.6 2.8 convolution_convert_fusion
  332.4 2.9 convolution_convert_fusion.1
  335.3 2.9 convolution_convert_fusion.3
  339.1 2.4 convolution_convert_fusion.7
  344.2 3.1 convolution_convert_fusion.4
  349.0 30.4 %backward.1 = bf16[1024,1152]{1,0:T(8,128)(2,1)} custom-call(bf16[1024,384]{1,0:T(8,128)(2,1)} %get-tuple-element.104.query, bf16[1024,384]{1,0:T(8,128)(2,1)} %get-tuple-element.105.key, bf16[1024,384]{1,0:T(8,128)(2,1)} %get-tuple-element.106.value, bf16[1024,384]{1,0:T(8,128)(2,1)} %pad_maximum_fusion.grad_att, f32[6,1,1024]{2,1,0:T(1,128)} %get-tuple-element.107.lse, ...), custom_call_target="tpu_custom_call" | custom-call | tf_op jit(solution)/shard_map/backward/pallas_call | solution.py:453
  379.4 4.0 fusion.81
  386.0 3.5 convolution_convert_fusion.6
  389.5 155.4 %reduce.13 = (f32[48,1152]{1,0:T(8,128)}, f32[48,384]{1,0:T(8,128)}, f32[48,1536]{1,0:T(8,128)}, f32[48,1536]{1,0:T(8,128)}, f32[48,1536]{1,0:T(8,128)}) custom-call(bf16[2,2,2,2,48,1152]{5,4,3,2,1,0:T(8,128)(2,1)} %bitcast.121, bf16[2,2,2,2,48,384]{5,4,3,2,1,0:T(8,128)(2,1)} %bitcast.131, bf16[2,2,2,2,48,384]{5,4,3,2,1,0:T(8,128)(2,1)} %bitcast.132, ...), custom_call_target="tpu_custom_call" | custom-call | tf_op jit(solution)/shard_map/reduce/pallas_call | solution.py:700
  554.1 2.6 fusion.25
  557.9 59.3 %spread.1 = (f32[3816,384]{1,0:T(8,128)}, f32[8,768]{1,0:T(8,128)}) custom-call(bf16[512,768]{1,0:T(8,128)(2,1)S(1)} %fusion.24.grad, s32[1,1024]{1,0:T(1,128)} %get-tuple-element.273.pos, s32[8,8,128]{2,1,0:T(8,128)} %get-tuple-element.108.heard, f32[8,768]{1,0:T(8,128)} %pad.5.norm_grad), custom_call_target="tpu_custom_call" | custom-call | tf_op jit(solution)/shard_map/spread/pallas_call | solution.py:814
  618.7 4.9 multiply_reduce_fusion
  624.9 11.4 %total.1 = f32[8,128]{1,0:T(8,128)} custom-call(f32[8,128]{1,0:T(8,128)} %broadcast_in_dim.104.value), custom_call_target="tpu_custom_call" | custom-call | tf_op jit(solution)/shard_map/total/pallas_call | solution.py:863
  639.7 2.1 multiply_subtract_fusion.1
  647.9 2.2 multiply_subtract_fusion.2
  650.2 11.5 %multiply_subtract_fusion = (f32[3816,384]{1,0:T(8,128)}, f32[3816,384]{1,0:T(8,128)}, f32[3816,384]{1,0:T(8,128)}) fusion(f32[3816,384]{1,0:T(8,128)S(1)} %bitcast.112, f32[3816,384]{1,0:T(8,128)S(1)} %copy-done, f32[]{:T(128)} %min_shard_map.3, f32[3816,384]{1,0:T(8,128)} %param.38, f32[3816,384]{1,0:T(8,128)} %param.39), kind=kLoop, calls=%fused_computation.15 | loop fusion | flops 23445504 | bytes 41029636 | tf_op jit(solution)/shard_map/sub | solution.py:918
  (212 shorter events, 72.2 us)
Async XLA Ops:
  12.6 9.5 %copy-start.25 = (s32[1024]{0:T(1024)}, s32[1024]{0:T(1024)S(1)}, u32[]{:S(2)}) copy-start(s32[1024]{0:T(1024)S(1)} %convert_reduce_fusion.2) | copy-start | bytes 12292
  12.8 9.4 %copy-start.2 = (f32[48,2,1536]{2,1,0:T(2,128)S(1)}, f32[48,2,1536]{2,1,0:T(2,128)}, u32[]{:S(2)}) copy-start(f32[48,2,1536]{2,1,0:T(2,128)} %param.34) | copy-start | bytes 1769476
  25.4 161.0 %copy-start.22 = (s32[1,1024]{1,0:T(1,128)S(1)}, s32[1,1024]{1,0:T(1,128)}, u32[]{:S(2)}) copy-start(s32[1,1024]{1,0:T(1,128)} %param.28) | copy-start | bytes 12292
  192.7 36.7 %copy-start.26 = (s32[1024]{0:T(1024)S(1)}, s32[1024]{0:T(1024)}, u32[]{:S(2)}) copy-start(s32[1024]{0:T(1024)} %copy-done.25) | copy-start | bytes 12292
  192.7 36.7 %copy-start.31 = (s32[2,8,16]{2,1,0:T(8,128)S(1)}, s32[2,8,16]{2,1,0:T(8,128)}, u32[]{:S(2)}) copy-start(s32[2,8,16]{2,1,0:T(8,128)} %param.29) | copy-start | bytes 3076
  192.7 40.0 %copy-start.32 = (s32[8,16]{1,0:T(8,128)S(1)}, s32[8,16]{1,0:T(8,128)}, u32[]{:S(2)}) copy-start(s32[8,16]{1,0:T(8,128)} %param.30) | copy-start | bytes 1540
  227.0 7.8 %copy-start.1 = (bf16[512,768]{1,0:T(8,128)(2,1)S(1)}, bf16[512,768]{1,0:T(8,128)(2,1)}, u32[]{:S(2)}) copy-start(bf16[512,768]{1,0:T(8,128)(2,1)} %get-tuple-element.92) | copy-start | bytes 2359300
  227.0 8.2 %copy-start.28 = (f32[6,768]{1,0:T(8,128)S(1)}, f32[6,768]{1,0:T(8,128)}, u32[]{:S(2)}) copy-start(f32[6,768]{1,0:T(8,128)} %param.36) | copy-start | bytes 55300
  228.9 10.9 %collective-permute-start.1 = (bf16[512,384]{1,0:T(8,128)(2,1)}, bf16[512,384]{1,0:T(8,128)(2,1)}, u32[]{:S(2)}, u32[]{:S(2)}) collective-permute-start(bf16[512,384]{1,0:T(8,128)(2,1)} %slice.88), channel_id=1, source_target_pairs={{0,1},{1,0},{2,3},{3,2},{4,5},{5,4},{6,7},{7,6},{8,9},{9,8},{10,11... | collective-permute-start | bytes 1179656 | tf_op jit(solution)/shard_map/ppermute | solution.py:877
  234.8 4.9 copy-start.8
  234.9 4.9 copy-start.18
  242.1 10.8 %copy-start.15 = (bf16[512,768]{1,0:T(8,128)(2,1)}, bf16[512,768]{1,0:T(8,128)(2,1)S(1)}, u32[]{:S(2)}) copy-start(bf16[512,768]{1,0:T(8,128)(2,1)S(1)} %fusion.31) | copy-start | bytes 2359300
  245.1 7.8 %copy-start.44 = (f32[512,1536]{1,0:T(8,128)}, f32[512,1536]{1,0:T(8,128)S(1)}, u32[]{:S(2)}) copy-start(f32[512,1536]{1,0:T(8,128)S(1)} %fusion.77) | copy-start | bytes 9437188
  301.7 11.3 %copy-start.38 = (bf16[2,2,2,2,48,1536]{5,4,3,2,1,0:T(8,128)(2,1)S(1)}, bf16[2,2,2,2,48,1536]{5,4,3,2,1,0:T(8,128)(2,1)}, u32[]{:S(2)}) copy-start(bf16[2,2,2,2,48,1536]{5,4,3,2,1,0:T(8,128)(2,1)} %get-tuple-element.100) | copy-start | bytes 7077892
  338.1 9.9 %collective-permute-start.2 = (bf16[512,384]{1,0:T(8,128)(2,1)S(1)}, bf16[512,384]{1,0:T(8,128)(2,1)S(1)}, u32[]{:S(2)}, u32[]{:S(2)}) collective-permute-start(bf16[512,384]{1,0:T(8,128)(2,1)S(1)} %convolution_convert_fusion.9), channel_id=1, source_target_pairs={{0,1},{1,0},{2,3},{3,2},{4,5},{5,4},{6,7},{7,6},{8,9},{9,8},{10,11... | collective-permute-start | bytes 1179656 | tf_op jit(solution)/shard_map/ppermute | solution.py:877
  349.0 30.4 %copy-start.6 = (bf16[2,2,2,2,48,1152]{5,4,3,2,1,0:T(8,128)(2,1)S(1)}, bf16[2,2,2,2,48,1152]{5,4,3,2,1,0:T(8,128)(2,1)}, u32[]{:S(2)}) copy-start(bf16[2,2,2,2,48,1152]{5,4,3,2,1,0:T(8,128)(2,1)} %get-tuple-element.91) | copy-start | bytes 5308420
  379.4 6.0 copy-start.5
  383.4 6.1 copy-start.7
  384.4 169.7 %collective-permute-start.3 = (bf16[512,768]{1,0:T(8,128)(2,1)}, bf16[512,768]{1,0:T(8,128)(2,1)}, u32[]{:S(2)}, u32[]{:S(2)}) collective-permute-start(bf16[512,768]{1,0:T(8,128)(2,1)} %slice.137), channel_id=1, source_target_pairs={{0,1},{1,0},{2,3},{3,2},{4,5},{5,4},{6,7},{7,6},{8,9},{9,8},{10,11... | collective-permute-start | bytes 2359304 | tf_op jit(solution)/shard_map/ppermute | solution.py:877
  618.7 20.3 %copy-start.12 = (f32[48,1152]{1,0:T(8,128)S(1)}, f32[48,1152]{1,0:T(8,128)}, u32[]{:S(2)}) copy-start(f32[48,1152]{1,0:T(8,128)} %get-tuple-element.111) | copy-start | bytes 663556
  618.7 21.0 %copy-start.10 = (f32[48,1536]{1,0:T(8,128)S(1)}, f32[48,1536]{1,0:T(8,128)}, u32[]{:S(2)}) copy-start(f32[48,1536]{1,0:T(8,128)} %get-tuple-element.113) | copy-start | bytes 884740
  618.7 27.0 %copy-start.29 = (f32[6,768]{1,0:T(8,128)S(1)}, f32[6,768]{1,0:T(8,128)}, u32[]{:S(2)}) copy-start(f32[6,768]{1,0:T(8,128)} %param.48) | copy-start | bytes 55300
  618.7 27.0 %copy-start.30 = (f32[6,768]{1,0:T(8,128)S(1)}, f32[6,768]{1,0:T(8,128)}, u32[]{:S(2)}) copy-start(f32[6,768]{1,0:T(8,128)} %param.49) | copy-start | bytes 55300
  618.7 27.6 %copy-start.21 = (f32[48,384]{1,0:T(8,128)S(1)}, f32[48,384]{1,0:T(8,128)}, u32[]{:S(2)}) copy-start(f32[48,384]{1,0:T(8,128)} %refs_3_.1) | copy-start | bytes 221188
  618.7 31.4 %slice-start = ((s8[5861376]{0:T(1024)(128)(4,1)}), s8[1667072]{0:T(1024)(128)(4,1)S(1)}, s32[]{:S(2)}) async-start(s8[5861376]{0:T(1024)(128)(4,1)} %bitcast.111), calls=%async_computation.3 | async-start | bytes 3334144
  638.8 6.8 %copy-start.27 = (f32[8,768]{1,0:T(8,128)S(1)}, f32[8,768]{1,0:T(8,128)}, u32[]{:S(2)}) copy-start(f32[8,768]{1,0:T(8,128)} %get-tuple-element.116) | copy-start | bytes 73732
  639.7 10.4 %slice-start.1 = ((s8[5861376]{0:T(1024)(128)(4,1)}), s8[4194304]{0:T(1024)(128)(4,1)S(1)}, s32[]{:S(2)}) async-start(s8[5861376]{0:T(1024)(128)(4,1)} %bitcast.111), calls=%async_computation.4 | async-start | bytes 8388608
  641.8 6.1 copy-start.9
  641.8 8.3 %copy-start = (f32[3816,384]{1,0:T(8,128)S(1)}, f32[3816,384]{1,0:T(8,128)}, u32[]{:S(2)}) copy-start(f32[3816,384]{1,0:T(8,128)} %get-tuple-element.320) | copy-start | bytes 17584132
  650.1 11.6 %copy-start.11 = (f32[48,3,384]{2,0,1:T(8,128)S(1)}, f32[48,3,384]{2,0,1:T(8,128)}, u32[]{:S(2)}) copy-start(f32[48,3,384]{2,0,1:T(8,128)} %param.32) | copy-start | bytes 663556
  650.2 11.5 %copy-start.23 = (f32[48,3,384]{2,0,1:T(8,128)S(1)}, f32[48,3,384]{2,0,1:T(8,128)}, u32[]{:S(2)}) copy-start(f32[48,3,384]{2,0,1:T(8,128)} %param.40) | copy-start | bytes 663556
  650.2 11.5 %copy-start.24 = (f32[48,3,384]{2,0,1:T(8,128)S(1)}, f32[48,3,384]{2,0,1:T(8,128)}, u32[]{:S(2)}) copy-start(f32[48,3,384]{2,0,1:T(8,128)} %param.41) | copy-start | bytes 663556
  (27 other events, 64.6 us)

commit v2 on v0

--- a/solution.py
+++ b/solution.py
@@ -2,10 +2,11 @@
 import jax.numpy as jnp
 from jax import lax
 from jax.sharding import PartitionSpec as P
+from jax.experimental import pallas as pl
+from jax.experimental.pallas import tpu as pltpu
 
 HDIM = 64
 STEP = 5
-
 
 norm_eps = 1e-06
 cap_value = 3.4
@@ -19,6 +20,990 @@
 adam_eps = 1e-08
 neg_large = -1e30
 highest = lax.Precision.HIGHEST
+f32 = jnp.float32
+bf16 = jnp.bfloat16
+MESH = pl.DeviceIdType.MESH
+ANY = pl.BlockSpec(memory_space=pl.ANY)
+VM = pl.BlockSpec(memory_space=pltpu.VMEM)
+
+
+def sds(shape, dtype):
+    return jax.ShapeDtypeStruct(shape, dtype)
+
+
+def params(ident, limit=58):
+    return pltpu.CompilerParams(
+        collective_id=ident, has_side_effects=True, vmem_limit_bytes=limit << 20
+    )
+
+
+class Place:
+    def __init__(self):
+        self.n_dp = lax.axis_size("dp")
+        self.count = self.n_dp.bit_length() - 1
+        self.t = lax.axis_index("tower")
+        self.d = lax.axis_index("dp")
+        self.m = lax.axis_index("mp")
+        self.bits = [(self.d // (1 << (self.count - 1 - j))) % 2 for j in range(self.count)]
+
+    def across(self, dim):
+        if dim == "t":
+            return {"tower": 1 - self.t}
+        if dim == "y":
+            return {"mp": 1 - self.m}
+        step = 1 << (self.count - 1 - dim)
+        return {"dp": self.d + (1 - 2 * self.bits[dim]) * step}
+
+    def mixed(self, rel):
+        out = self.d
+        for j in range(self.count):
+            step = 1 << (self.count - 1 - j)
+            if rel & step:
+                out = out + (1 - 2 * self.bits[j]) * step
+        return out
+
+
+def remote(src, dst, send, recv, where):
+    return pltpu.make_async_remote_copy(
+        src_ref=src, dst_ref=dst, send_sem=send, recv_sem=recv, device_id=where, device_id_type=MESH
+    )
+
+
+def greet(peers):
+    barrier = pltpu.get_barrier_semaphore()
+    for where in peers:
+        pl.semaphore_signal(barrier, inc=1, device_id=where, device_id_type=MESH)
+    pl.semaphore_wait(barrier, len(peers))
+
+
+def tdot(lhs, rhs):
+    return lax.dot_general(lhs, rhs, (((1,), (1,)), ((), ())), preferred_element_type=f32)
+
+
+def mdot(lhs, rhs):
+    return jnp.dot(lhs, rhs, preferred_element_type=f32)
+
+
+def every(ndim, cols):
+    return (slice(None),) * (ndim - 1) + (cols,)
+
+
+class Gather:
+    def __init__(self, here, shard, full, other, order, cols, send, recv, local_sem):
+        self.here, self.shard, self.full, self.other = here, shard, full, other
+        self.order, self.cols, self.send, self.recv = order, cols, send, recv
+        self.local_sem = local_sem
+        self.last = len(order)
+        self.done = set()
+        self.live, self.sent = [], []
+        self.arrays = [full]
+        self.slot = 0
+
+    def view(self):
+        here = self.here
+        return (
+            (here.t,)
+            + tuple(slice(None) if j in self.done else here.bits[j] for j in range(here.count))
+            + (slice(None), self.cols)
+        )
+
+    def stage(self, step):
+        here = self.here
+        if step == 0:
+            self.place = pltpu.make_async_copy(
+                self.shard.at[:, self.cols], self.full.at[self.view()], self.local_sem
+            )
+            self.place.start()
+        for copy in self.live:
+            copy.wait_recv()
+        if step == 1:
+            self.place.wait()
+        self.sent += self.live
+        self.live = []
+        if step == self.last:
+            for copy in self.sent:
+                copy.wait_send()
+            return
+        dim = self.order[step]
+        if dim == "y":
+            pairs = [(self.full.at[self.view()], self.other.at[self.view()])]
+            self.arrays = [self.full, self.other]
+        elif step == 0:
+            pairs = [(self.shard.at[:, self.cols], self.full.at[self.view()])]
+        else:
+            pairs = [(ref.at[self.view()], ref.at[self.view()]) for ref in self.arrays]
+        for src, dst in pairs:
+            copy = remote(
+                src, dst, self.send.at[self.slot], self.recv.at[self.slot], here.across(dim)
+            )
+            copy.start()
+            self.live.append(copy)
+            self.slot += 1
+        if dim not in ("t", "y"):
+            self.done.add(dim)
+
+
+class Scatter:
+    def __init__(self, here, own, other, order, cols, held, landed, out, send, recv, local_sems):
+        self.here, self.order, self.cols = here, order, cols
+        self.source = [own] if other is None else [own, other]
+        self.held, self.landed, self.out = held, landed, out
+        self.send, self.recv, self.local_sems = send, recv, local_sems
+        self.last = len(order)
+        self.fixed = {}
+        self.live = []
+        self.slot = 0
+        self.arrays = list(range(len(self.source)))
+
+    def view(self, extra=None):
+        fixed = dict(self.fixed)
+        if extra:
+            fixed.update(extra)
+        return tuple(fixed.get(j, slice(None)) for j in range(self.here.count))
+
+    def start(self, src, where, index):
+        copy = remote(
+            src, self.landed[self.slot], self.send.at[self.slot], self.recv.at[self.slot], where
+        )
+        copy.start()
+        self.live.append((copy, self.slot, index))
+        self.slot += 1
+
+    def stage(self, step):
+        here = self.here
+        if step > 0:
+            self.finish(step - 1)
+        if step == self.last:
+            return
+        dim = self.order[step]
+        if dim == "t":
+            self.loads = []
+            tail = (slice(None),) * (here.count + 1) + (self.cols,)
+            for index in self.arrays:
+                load = pltpu.make_async_copy(
+                    self.source[index].at[(here.t,) + tail], self.held[index],
+                    self.local_sems.at[index],
+                )
+                load.start()
+                self.loads.append(load)
+                self.start(self.source[index].at[(1 - here.t,) + tail], here.across("t"), index)
+        elif dim == "y":
+            self.start(self.held[1].at[self.view()], here.across("y"), 0)
+            self.arrays = [0]
+        else:
+            far = self.view({dim: 1 - here.bits[dim]})
+            for index in self.arrays:
+                self.start(self.held[index].at[far], here.across(dim), index)
+
+    def finish(self, step):
+        here = self.here
+        dim = self.order[step]
+        if dim not in ("t", "y"):
+            self.fixed[dim] = here.bits[dim]
+        view = self.view()
+        if dim == "t":
+            for load in self.loads:
+                load.wait()
+        for copy, slot, index in self.live:
+            copy.wait()
+            total = self.held[index][view].astype(f32) + self.landed[slot][...].astype(f32)
+            if step == self.last - 1:
+                self.out[:, self.cols] = total
+            else:
+                self.held[index][view] = total.astype(bf16)
+        self.live = []
+
+
+class Runner:
+    def __init__(self, jobs, lags):
+        self.jobs, self.lags, self.tick = jobs, lags, 0
+        self.length = max(job.last + lag for job, lag in zip(jobs, lags)) + 1
+
+    def advance(self):
+        if self.tick < self.length:
+            for job, lag in zip(self.jobs, self.lags):
+                if 0 <= self.tick - lag <= job.last:
+                    job.stage(self.tick - lag)
+            self.tick += 1
+
+    def drain(self):
+        while self.tick < self.length:
+            self.advance()
+
+
+def gather_orders(count):
+    far, near = list(range(count - 1)), [count - 1]
+    return {
+        "plain": far + near + ["t"],
+        "late": far + near + ["y", "t"],
+        "early": far + ["y"] + near + ["t"],
+    }
+
+
+def scatter_orders(count):
+    near, far = [count - 1], list(range(count - 2, -1, -1))
+    return {
+        "plain": ["t"] + near + far,
+        "early": ["t", "y"] + near + far,
+        "late": ["t"] + near + ["y"] + far,
+    }
+
+
+def scatter_lands(order, count, pair, rows, cols):
+    shapes, free, live = [], count, 2 if pair else 1
+    for dim in order:
+        if dim == "y":
+            live = 1
+        elif dim != "t":
+            free -= 1
+        shapes += [(2,) * free + (rows, cols)] * live
+    return shapes
+
+
+def lists_body(lists, heard, flag, send, recv):
+    here = Place()
+    n = here.n_dp
+    peers = []
+    for rt in range(2):
+        for k in range(n):
+            if rt or k:
+                peers.append((rt, k, {"tower": here.t + rt * (1 - 2 * here.t), "dp": here.mixed(k)}))
+    greet([where for _, _, where in peers])
+    copies = []
+    for rt, k, where in peers:
+        copy = remote(lists.at[k], heard.at[rt, k], send.at[rt, k], recv.at[rt, k], where)
+        copy.start()
+        copies.append(copy)
+    heard[0, 0] = lists[0]
+    for copy in copies:
+        copy.wait()
+    flag[...] = jnp.max(heard[...].reshape((2 * n,) + flag.shape), axis=0)
+
+
+def exchange_lists(lists):
+    n = lists.shape[0]
+    dma = pltpu.SemaphoreType.DMA
+    return pl.pallas_call(
+        lists_body,
+        out_shape=[sds((2,) + lists.shape, jnp.int32), sds(lists.shape[1:], jnp.int32)],
+        in_specs=[VM],
+        out_specs=[VM, VM],
+        scratch_shapes=[dma((2, n)), dma((2, n))],
+        compiler_params=params(1),
+        name="lists",
+    )(lists)
+
+
+def turned(values):
+    lanes = lax.broadcasted_iota(jnp.int32, values.shape, 1) % HDIM
+    size = values.shape[1]
+    return jnp.where(
+        lanes < HDIM // 2,
+        -pltpu.roll(values, size - HDIM // 2, 1),
+        pltpu.roll(values, HDIM // 2, 1),
+    )
+
+
+def norm_parts(stream):
+    average = jnp.mean(stream, -1, keepdims=True)
+    centered = stream - average
+    variance = jnp.mean(centered * centered, -1, keepdims=True)
+    scale = lax.rsqrt(variance + norm_eps)
+    return centered * scale, scale
+
+
+def forward_body(room, kinds, pieces, *refs):
+    here = Place()
+    n, count = here.n_dp, here.count
+    table, heard, pos, norm_rows, cosine, sine, seg_row, seg_col = refs[:8]
+    shards = refs[8:13]
+    emb_out, zero_out, input_out, q_out, k_out, v_out, lse_out, att_own, att_other = refs[13:22]
+    fulls, at = [], 22
+    for kind in kinds:
+        width = 1 if kind == "plain" else 2
+        fulls.append((refs[at], None) if width == 1 else (refs[at], refs[at + 1]))
+        at += width
+    low_table, served, rows, vt, att_far = refs[at : at + 5]
+    lows = refs[at + 5 : at + 10]
+    rsem, ysem, asem, wsend, wrecv, wlocal = refs[at + 10 :]
+    tok = pos.shape[0]
+    half = tok // 2
+    width = rows.shape[3]
+    slots = n * room
+    feats = q_out.shape[1]
+    groups = feats // 128
+    block = 256
+
+    greet(
+        [{"dp": here.mixed(k)} for k in range(1, n)] + [here.across("t"), here.across("y")]
+    )
+    orders = gather_orders(count)
+    for low, shard in zip(lows, shards):
+        low[...] = shard[...].astype(bf16)
+    jobs, lags = [], []
+    for number, (which, kind, start, size, lag) in enumerate(pieces):
+        jobs.append(
+            Gather(
+                here, lows[which], fulls[which][0], fulls[which][1], orders[kind],
+                pl.ds(start, size), wsend.at[number], wrecv.at[number], wlocal.at[number],
+            )
+        )
+        lags.append(lag)
+    runner = Runner(jobs, lags)
+    first_ticks = jobs[0].last + 1
+    runner.advance()
+    low_table[...] = table[...].astype(bf16)
+    row_count = table.shape[0]
+    out_copies, y_copies = [], []
+
+    def pass_on(k):
+        copy = remote(
+            rows.at[here.m, k], rows.at[here.m, k], ysem.at[0, k], ysem.at[1, k], here.across("y")
+        )
+        copy.start()
+        y_copies.append(copy)
+
+    for k in list(range(1, n)) + [0]:
+        column = jnp.transpose(heard[k])[:room, 0:1]
+        hot = (lax.broadcasted_iota(jnp.int32, (room, row_count), 1) == column).astype(f32)
+        found = mdot(hot.astype(bf16), low_table[...]).astype(bf16)
+        if k == 0:
+            rows[here.m, 0] = found
+            pass_on(0)
+        else:
+            served[k] = found
+            copy = remote(
+                served.at[k], rows.at[here.m, k], rsem.at[0, k], rsem.at[1, k],
+                {"dp": here.mixed(k)},
+            )
+            copy.start()
+            out_copies.append(copy)
+            if k == n // 2:
+                runner.advance()
+    for k in range(1, n):
+        out_copies[k - 1].wait_recv()
+        pass_on(k)
+    while runner.tick < first_ticks:
+        runner.advance()
+    for copy in out_copies:
+        copy.wait_send()
+    for copy in y_copies:
+        copy.wait()
+
+    w_qkv = fulls[0][0]
+    for i in range(tok // block):
+        at = slice(i * block, (i + 1) * block)
+        hot = (lax.broadcasted_iota(jnp.int32, (block, slots), 1) == pos[at, :]).astype(f32)
+        hot = hot.astype(bf16)
+        emb = jnp.concatenate([mdot(hot, rows[h].reshape(slots, width)) for h in range(2)], 1)
+        hat, _scale = norm_parts(emb)
+        stream = hat * norm_rows[0:1, :] + norm_rows[1:2, :]
+        low = stream.astype(bf16)
+        input_out[at, :] = low
+        if (i + 1) * block <= half:
+            emb_out[at, :] = emb.astype(bf16)
+            zero_out[at, :] = stream
+        cos, sin = cosine[at, :], sine[at, :]
+        proj = mdot(low, w_qkv[...].reshape(2 * width, 3 * feats))
+        for c in range(3):
+            for g in range(groups):
+                cols = slice(g * 128, (g + 1) * 128)
+                part = proj[:, c * feats + g * 128 : c * feats + (g + 1) * 128]
+                if c < 2:
+                    part = part * cos + turned(part) * sin
+                part = part.astype(bf16)
+                if c == 0:
+                    q_out[at, cols] = part * bf16(HDIM**-0.5)
+                elif c == 1:
+                    k_out[at, cols] = part
+                else:
+                    v_out[at, cols] = part
+        runner.advance()
+
+    lane = lax.broadcasted_iota(jnp.int32, (1, 128), 1)
+    att_copies = []
+    for g in range(groups):
+        cols = slice(g * 128, (g + 1) * 128)
+        vt[...] = jnp.transpose(v_out[:, cols].astype(f32)).astype(bf16)
+        keys = [jnp.where((lane // HDIM) == h, k_out[:, cols], bf16(0)) for h in range(2)]
+        for i in list(range(tok // block // 2, tok // block)) + list(range(tok // block // 2)):
+            at = slice(i * block, (i + 1) * block)
+            query = q_out[at, cols]
+            same = seg_col[...] == seg_row[:, at]
+            outs = []
+            for h in range(2):
+                scores = jnp.where(same, tdot(keys[h], query), neg_large)
+                peak = jnp.max(scores, 0, keepdims=True)
+                soft = jnp.exp(scores - peak)
+                total = jnp.sum(soft, 0, keepdims=True)
+                lse_out[2 * g + h, :, at] = peak + jnp.log(total)
+                soft = (soft * (1.0 / total)).astype(bf16)
+                outs.append(mdot(vt[h * HDIM : (h + 1) * HDIM, :], soft))
+            found = jnp.transpose(jnp.concatenate(outs, 0)).astype(bf16)
+            if i * block < half:
+                att_own[at, cols] = found
+            else:
+                att_far[slice(i * block - half, (i + 1) * block - half), cols] = found
+                if (i + 1) * block == tok:
+                    copy = remote(
+                        att_far.at[:, cols], att_other.at[:, cols], asem.at[0, g], asem.at[1, g],
+                        here.across("y"),
+                    )
+                    copy.start()
+                    att_copies.append(copy)
+            runner.advance()
+    runner.drain()
+    for copy in att_copies:
+        copy.wait()
+
+
+def forward_pass(table, heard, pos, norm_rows, cosine, sine, seg_row, seg_col, shards, kinds, pieces):
+    n_dp, room = heard.shape[0], max(32, pos.shape[0] // heard.shape[0])
+    count = n_dp.bit_length() - 1
+    halves = (2,) * (count + 1)
+    tok = pos.shape[0]
+    half = tok // 2
+    width = table.shape[1]
+    feats = shards[0].shape[1] // 3
+    outs = [
+        sds((half, 2 * width), bf16),
+        sds((half, 2 * width), f32),
+        sds((tok, 2 * width), bf16),
+        sds((tok, feats), bf16),
+        sds((tok, feats), bf16),
+        sds((tok, feats), bf16),
+        sds((feats // HDIM, 1, tok), f32),
+        sds((half, feats), bf16),
+        sds((half, feats), bf16),
+    ]
+    specs = [VM] * len(outs)
+    for shard, kind in zip(shards, kinds):
+        full = sds(halves + shard.shape, bf16)
+        outs += [full] if kind == "plain" else [full, full]
+        specs += [VM] if kind == "plain" else [ANY, ANY]
+    dma = pltpu.SemaphoreType.DMA
+    steps = count + 6
+    scratch = (
+        [
+            pltpu.VMEM(table.shape, bf16),
+            pltpu.VMEM((n_dp, room, width), bf16),
+            pltpu.VMEM((2, n_dp, room, width), bf16),
+            pltpu.VMEM((128, tok), bf16),
+            pltpu.VMEM((half, feats), bf16),
+        ]
+        + [pltpu.VMEM(shard.shape, bf16) for shard in shards]
+        + [dma((2, n_dp)), dma((2, n_dp)), dma((2, feats // 128))]
+        + [dma((len(pieces), steps)), dma((len(pieces), steps)), dma((len(pieces),))]
+    )
+    out = pl.pallas_call(
+        lambda *refs: forward_body(room, kinds, pieces, *refs),
+        out_shape=outs,
+        in_specs=[VM] * (8 + len(shards)),
+        out_specs=specs,
+        scratch_shapes=scratch,
+        compiler_params=params(2),
+        name="forward",
+    )(table, heard, pos, norm_rows, cosine, sine, seg_row, seg_col, *shards)
+    weights, at = [], 9
+    for shard, kind in zip(shards, kinds):
+        whole = (2 * n_dp * shard.shape[0], shard.shape[1])
+        if kind == "plain":
+            weights.append(out[at].reshape(whole))
+            at += 1
+        else:
+            weights.append((out[at].reshape(whole), out[at + 1].reshape(whole)))
+            at += 2
+    return out[:9], weights
+
+
+def make_scatters(here, grads, kinds, pieces, outs, held, landed, send, recv, loads):
+    orders = scatter_orders(here.count)
+    jobs, lags = [], []
+    held, landed = list(held), list(landed)
+    for number, (which, kind, start, size, lag) in enumerate(pieces):
+        own, other = grads[which]
+        pair = other is not None
+        mine = [held.pop(0) for _ in range(2 if pair else 1)]
+        amount = len(scatter_lands(orders[kind], here.count, pair, 1, 1))
+        lands = [landed.pop(0) for _ in range(amount)]
+        jobs.append(
+            Scatter(
+                here, own, other, orders[kind], pl.ds(start, size), mine, lands, outs[which],
+                send.at[number], recv.at[number], loads.at[number],
+            )
+        )
+        lags.append(lag)
+    return Runner(jobs, lags)
+
+
+def scatter_scratch(count, rows, pairs, pieces):
+    orders = scatter_orders(count)
+    held, landed = [], []
+    for which, kind, _start, size, _lag in pieces:
+        pair = pairs[which]
+        held += [pltpu.VMEM((2,) * count + (rows, size), bf16)] * (2 if pair else 1)
+        landed += [
+            pltpu.VMEM(shape, bf16)
+            for shape in scatter_lands(orders[kind], count, pair, rows, size)
+        ]
+    dma = pltpu.SemaphoreType.DMA
+    steps = 2 * count + 6
+    sems = [dma((len(pieces), steps)), dma((len(pieces), steps)), dma((len(pieces), 2))]
+    return held, landed, sems
+
+
+def square_sum(values):
+    return jnp.sum(jnp.sum(values * values, 0, keepdims=True), 1, keepdims=True)
+
+
+def backward_body(pieces, sizes, *refs):
+    here = Place()
+    (low, out_own, out_other, query, key, value, lse, cosine, sine, seg_row, seg_col, residual,
+     emb, norm_rows, w_qkv) = refs[:15]
+    grads = [(refs[15 + 2 * j], refs[16 + 2 * j]) for j in range(3)]
+    grad_proj, low_out, norms_out = refs[21:24]
+    outs = refs[24:27]
+    squares = refs[27]
+    kt, dq, dk, dv, grad_att, far_att, far_send, far_recv = refs[28:36]
+    at = 36
+    held = refs[at : at + sizes[0]]
+    landed = refs[at + sizes[0] : at + sizes[0] + sizes[1]]
+    asem, bsem, send, recv, loads = refs[at + sizes[0] + sizes[1] :]
+    tok, feats = query.shape
+    half = tok // 2
+    groups = feats // 128
+    block = 256
+    greet([here.across("t"), here.across("y")] + [here.across(j) for j in range(here.count)])
+    runner = make_scatters(here, grads, None, pieces, outs, held, landed, send, recv, loads)
+    runner.advance()
+    att_copies = []
+    far_att[...] = mdot(low[...], out_other[...]).astype(bf16)
+    for g in range(groups):
+        cols = slice(g * 128, (g + 1) * 128)
+        copy = remote(
+            far_att.at[:, cols], grad_att.at[half:, cols], asem.at[0, g], asem.at[1, g],
+            here.across("y"),
+        )
+        copy.start()
+        att_copies.append(copy)
+    grad_att[:half, :] = mdot(low[...], out_own[...]).astype(bf16)
+    lane = lax.broadcasted_iota(jnp.int32, (1, 128), 1)
+    for g in range(groups):
+        cols = slice(g * 128, (g + 1) * 128)
+        kt[...] = jnp.transpose(key[:, cols].astype(f32)).astype(bf16)
+        keys = [jnp.where((lane // HDIM) == h, key[:, cols], bf16(0)) for h in range(2)]
+        values = [jnp.where((lane // HDIM) == h, value[:, cols], bf16(0)) for h in range(2)]
+        for i in range(tok // block):
+            if i * block == half:
+                att_copies[g].wait_recv()
+            rows = slice(i * block, (i + 1) * block)
+            q_part = query[rows, cols]
+            g_part = grad_att[rows, cols]
+            same = seg_col[...] == seg_row[:, rows]
+            turns = []
+            add_k, add_v = None, None
+            for h in range(2):
+                mine = (lane // HDIM) == h
+                scores = jnp.where(same, tdot(keys[h], q_part), neg_large)
+                soft = jnp.exp(scores - lse[2 * g + h, :, rows])
+                grad_soft = tdot(values[h], g_part)
+                inner = jnp.sum(soft * grad_soft, 0, keepdims=True)
+                grad_scores = (soft * (grad_soft - inner)).astype(bf16)
+                part_v = mdot(soft.astype(bf16), jnp.where(mine, g_part, bf16(0)))
+                part_k = mdot(grad_scores, jnp.where(mine, q_part, bf16(0)))
+                add_v = part_v if h == 0 else add_v + part_v
+                add_k = part_k if h == 0 else add_k + part_k
+                turns.append(mdot(kt[h * HDIM : (h + 1) * HDIM, :], grad_scores))
+            dq[rows, :] = jnp.transpose(jnp.concatenate(turns, 0)) * (HDIM**-0.5)
+            if i == 0:
+                dv[...] = add_v
+                dk[...] = add_k
+            else:
+                dv[...] += add_v
+                dk[...] += add_k
+            if i % 2:
+                runner.advance()
+        cos, sin = cosine[...], sine[...]
+        for c, grad in ((0, dq), (1, dk)):
+            whole = grad[...]
+            back = whole * cos - turned(whole) * sin
+            grad_proj[:, c * feats + g * 128 : c * feats + (g + 1) * 128] = back.astype(bf16)
+        grad_proj[:, 2 * feats + g * 128 : 2 * feats + (g + 1) * 128] = dv[...].astype(bf16)
+    for copy in att_copies:
+        copy.wait_send()
+    far_copies = []
+    for i in range(half // block):
+        rows = slice(i * block, (i + 1) * block)
+        far = grad_proj[half + i * block : half + (i + 1) * block, :]
+        far_send[rows, :] = tdot(far, w_qkv[...]).astype(bf16)
+        copy = remote(
+            far_send.at[rows, :], far_recv.at[rows, :], bsem.at[0, i], bsem.at[1, i],
+            here.across("y"),
+        )
+        copy.start()
+        far_copies.append(copy)
+    norms_out[...] = jnp.zeros_like(norms_out)
+    for i in range(half // block):
+        rows = slice(i * block, (i + 1) * block)
+        near = residual[rows, :] + tdot(grad_proj[rows, :], w_qkv[...])
+        far_copies[i].wait()
+        near = near + far_recv[rows, :].astype(f32)
+        hat, scale = norm_parts(emb[rows, :].astype(f32))
+        grad_hat = near * norm_rows[0:1, :]
+        first = jnp.mean(grad_hat, -1, keepdims=True)
+        second = jnp.mean(grad_hat * hat, -1, keepdims=True)
+        low_out[rows, :] = (scale * (grad_hat - first - hat * second)).astype(bf16)
+        norms_out[0:1, :] += jnp.sum(near * hat, 0, keepdims=True)
+        norms_out[1:2, :] += jnp.sum(near, 0, keepdims=True)
+        runner.advance()
+    runner.drain()
+    total = square_sum(outs[0][...]) + square_sum(outs[1][...]) + square_sum(outs[2][...])
+    squares[...] = jnp.broadcast_to(total, squares.shape)
+
+
+def blocks_of(grad, n_dp):
+    count = n_dp.bit_length() - 1
+    rows = grad.shape[0] // (2 * n_dp)
+    return grad.reshape((2,) * (count + 1) + (rows, grad.shape[1]))
+
+
+def backward_pass(low, w_out, query, key, value, lse, cosine, sine, seg_row, seg_col, residual,
+                  emb, norm_rows, w_qkv, grads, pieces):
+    n_dp = lax.axis_size("dp")
+    count = n_dp.bit_length() - 1
+    tok, feats = query.shape
+    half, width = low.shape
+    rows, cols = grads[0][0].shape[0] // (2 * n_dp), grads[0][0].shape[1]
+    held, landed, sems = scatter_scratch(count, rows, [True] * 3, pieces)
+    flat = [blocks_of(g, n_dp) for pair in grads for g in pair]
+    dma = pltpu.SemaphoreType.DMA
+    vmem = pltpu.VMEM
+    return pl.pallas_call(
+        lambda *refs: backward_body(pieces, (len(held), len(landed)), *refs),
+        out_shape=[
+            sds((tok, 3 * feats), bf16), sds((half, width), bf16), sds((8, width), f32),
+            sds((rows, cols), f32), sds((rows, cols), f32), sds((rows, cols), f32),
+            sds((8, 128), f32),
+        ],
+        in_specs=[VM] * 15 + [ANY] * 6,
+        out_specs=[VM] * 7,
+        scratch_shapes=[
+            vmem((128, tok), bf16), vmem((tok, 128), f32), vmem((tok, 128), f32),
+            vmem((tok, 128), f32), vmem((tok, feats), bf16), vmem((half, feats), bf16),
+            vmem((half, width), bf16), vmem((half, width), bf16),
+        ] + held + landed + [dma((2, feats // 128)), dma((2, max(1, half // 256)))] + sems,
+        compiler_params=params(4),
+        name="backward",
+    )(low, w_out[0], w_out[1], query, key, value, lse, cosine, sine, seg_row, seg_col, residual,
+      emb, norm_rows, w_qkv, *flat)
+
+
+def spread_body(room, pieces, sizes, *refs):
+    here = Place()
+    n = here.n_dp
+    grad, pos, heard, norm_grad, squares = refs[:5]
+    grads = [(refs[5], None), (refs[6], refs[7])]
+    out, norms_out, out_qkv, out_proj, total_out = refs[8:13]
+    other, packed, mine, theirs, norms, parts, own_part, gathered = refs[13:21]
+    at = 21
+    held = refs[at : at + sizes[0]]
+    landed = refs[at + sizes[0] : at + sizes[0] + sizes[1]]
+    ysem, rsem, csem, nsem, tsem, send, recv, loads = refs[at + sizes[0] + sizes[1] :]
+    width = grad.shape[1] // 2
+    slots = n * room
+    peers = []
+    for rt in range(2):
+        for rd in range(n):
+            for rm in range(2):
+                if rt or rd or rm:
+                    where = {
+                        "tower": here.t + rt * (1 - 2 * here.t),
+                        "dp": here.mixed(rd),
+                        "mp": here.m + rm * (1 - 2 * here.m),
+                    }
+                    peers.append(((rt * n + rd) * 2 + rm, where))
+    greet([where for _, where in peers])
+    theirs_at = pl.ds(pl.multiple_of((1 - here.m) * width, 128), width)
+    mine_at = pl.ds(pl.multiple_of(here.m * width, 128), width)
+    swapped = remote(grad.at[:, theirs_at], other, ysem.at[0], ysem.at[1], here.across("y"))
+    swapped.start()
+    runner = make_scatters(
+        here, grads, None, pieces, (out_qkv, out_proj), held, landed, send, recv, loads
+    )
+    runner.advance()
+    me = (here.t * n + here.d) * 2 + here.m
+    norm_copies = []
+    for rel, where in peers:
+        copy = remote(norm_grad, norms.at[me], nsem.at[0, rel], nsem.at[1, rel], where)
+        copy.start()
+        norm_copies.append(copy)
+    norms[me] = norm_grad[...]
+    runner.advance()
+    swapped.wait()
+    both = jnp.concatenate([grad[:, mine_at], other[...]], 0)
+    copies = []
+    for k in list(range(1, n)) + [0]:
+        hot = (
+            lax.broadcasted_iota(jnp.int32, (room, pos.shape[1]), 0) + k * room == pos[...]
+        ).astype(f32)
+        packed[k] = mdot(hot.astype(bf16), both).astype(bf16)
+        if k:
+            copy = remote(
+                packed.at[k], mine.at[k], rsem.at[0, k], rsem.at[1, k], {"dp": here.mixed(k)}
+            )
+        else:
+            mine[0] = packed[0]
+            copy = remote(mine.at[0], theirs.at[0], csem.at[0, 0], csem.at[1, 0], here.across("t"))
+        copy.start()
+        copies.append(copy)
+    passed = [copies.pop()]
+    runner.advance()
+    for k in range(1, n):
+        copies[k - 1].wait_recv()
+        copy = remote(mine.at[k], theirs.at[k], csem.at[0, k], csem.at[1, k], here.across("t"))
+        copy.start()
+        passed.append(copy)
+    runner.advance()
+    for copy in copies:
+        copy.wait_send()
+    for copy in passed:
+        copy.wait()
+    row_count = out.shape[0]
+    block = row_count
+    for size in range(512, 255, -8):
+        if row_count % size == 0:
+            block = size
+            break
+    gathered[0:slots, :] = mine[...].reshape(slots, width)
+    gathered[slots:, :] = theirs[...].reshape(slots, width)
+    own_part[...] = jnp.zeros_like(own_part)
+
+    @pl.loop(0, row_count // block)
+    def _(i):
+        rows = pl.ds(pl.multiple_of(i * block, 8) if block != row_count else 0, block)
+        base = lax.broadcasted_iota(jnp.int32, (block, room), 0) + i * block
+        hots = []
+        for source in range(2):
+            for k in range(n):
+                hots.append((base == heard[source, k, 0:1, :room]).astype(f32).astype(bf16))
+        found = mdot(jnp.concatenate(hots, 1), gathered[...])
+        out[rows, :] = found
+        own_part[0:1, :] += jnp.sum(found * found, 0, keepdims=True)
+
+    runner.drain()
+    for copy in norm_copies:
+        copy.wait()
+    total = norms[0]
+    for j in range(1, 4 * n):
+        total = total + norms[j]
+    norms_out[...] = total
+    local_sq = (
+        squares[0:1, 0:1]
+        + 0.5 * jnp.sum(own_part[...], 1, keepdims=True)[0:1]
+        + square_sum(out_qkv[...])
+        + square_sum(out_proj[...])
+    )
+    parts[me] = jnp.broadcast_to(local_sq, parts.shape[1:])
+    copies = []
+    for rel, where in peers:
+        copy = remote(parts.at[me], parts.at[me], tsem.at[0, rel], tsem.at[1, rel], where)
+        copy.start()
+        copies.append(copy)
+    for copy in copies:
+        copy.wait()
+    total_out[...] = jnp.sum(parts[...], 0) + square_sum(norms_out[...])
+
+
+def spread_pass(grad, pos_row, heard, norm_grad, squares, grad_qkv, grad_out, row_count, pieces):
+    n_dp = lax.axis_size("dp")
+    count = n_dp.bit_length() - 1
+    half, width = grad.shape[0], grad.shape[1] // 2
+    room = max(32, 2 * half // n_dp)
+    rows = grad_qkv.shape[0] // (2 * n_dp)
+    held, landed, sems = scatter_scratch(count, rows, [False, True], pieces)
+    flat = [blocks_of(g, n_dp) for g in (grad_qkv, grad_out[0], grad_out[1])]
+    dma = pltpu.SemaphoreType.DMA
+    vmem = pltpu.VMEM
+    return pl.pallas_call(
+        lambda *refs: spread_body(room, pieces, (len(held), len(landed)), *refs),
+        out_shape=[
+            sds((row_count, width), f32), sds(norm_grad.shape, f32),
+            sds((rows, grad_qkv.shape[1]), f32), sds((rows, grad_out[0].shape[1]), f32),
+            sds((8, 128), f32),
+        ],
+        in_specs=[VM] * 5 + [ANY] * 3,
+        out_specs=[VM] * 5,
+        scratch_shapes=[
+            vmem((half, width), bf16),
+            vmem((n_dp, room, width), bf16),
+            vmem((n_dp, room, width), bf16),
+            vmem((n_dp, room, width), bf16),
+            vmem((4 * n_dp,) + norm_grad.shape, f32),
+            vmem((4 * n_dp, 8, 128), f32),
+            vmem((8, width), f32),
+            vmem((2 * n_dp * room, width), bf16),
+        ] + held + landed
+        + [dma((2,)), dma((2, n_dp)), dma((2, n_dp)), dma((2, 4 * n_dp)), dma((2, 4 * n_dp))] + sems,
+        compiler_params=params(5),
+        name="spread",
+    )(grad, pos_row, heard, norm_grad, squares, *flat)
+
+
+def loss_body(part, counts, doc_ok, query_ok, target, scale, grad_out, stats, other, low_all, turn,
+              psend, precv, esend, erecv):
+    here = Place()
+    n = here.n_dp
+    slots, width = part.shape
+    peers = []
+    for rt in range(2):
+        for rd in range(n):
+            if rt or rd:
+                peers.append(
+                    (rt * n + rd, {"tower": here.t + rt * (1 - 2 * here.t), "dp": here.mixed(rd)})
+                )
+    greet([where for _, where in peers] + [here.across("y")])
+    copy = remote(part, other, psend, precv, here.across("y"))
+    copy.start()
+    copy.wait()
+    pooled = (part[...] + other[...]) / counts[...]
+    scale_row = lax.rsqrt(jnp.sum(pooled * pooled, 1, keepdims=True) + 1e-06)
+    unit = pooled * scale_row
+    low_all[here.t, here.d] = unit.astype(bf16)
+    copies = []
+    for rel, where in peers:
+        copy = remote(
+            low_all.at[here.t, here.d], low_all.at[here.t, here.d], esend.at[rel], erecv.at[rel], where
+        )
+        copy.start()
+        copies.append(copy)
+    for copy in copies:
+        copy.wait()
+    total = n * slots
+    queries = low_all[0].reshape(total, width)
+    documents = low_all[1].reshape(total, width)
+    cosines = tdot(queries, documents)
+    factor = jnp.exp(jnp.minimum(scale[...], cap_value))
+    logits = jnp.where(doc_ok[...] > 0, factor * cosines, neg_large)
+    peak = jnp.max(logits, 1, keepdims=True)
+    log_total = peak + jnp.log(jnp.sum(jnp.exp(logits - peak), 1, keepdims=True))
+    soft = jnp.exp(logits - log_total)
+    mask = lax.broadcasted_iota(jnp.int32, (total, total), 1) == target[...]
+    picked = jnp.sum(jnp.where(mask, logits, 0.0), 1, keepdims=True)
+    valid = query_ok[...] > 0
+    query_count = jnp.sum(valid.astype(f32), axis=0, keepdims=True)
+    loss_sum = jnp.sum(jnp.where(valid, log_total - picked, 0.0), axis=0, keepdims=True)
+    grad_logits = jnp.where(valid, soft - mask.astype(f32), 0.0) / query_count
+    by_row = jnp.sum(grad_logits * cosines, 1, keepdims=True)
+    grad_scale = (
+        jnp.sum(by_row, 0, keepdims=True) * factor * (scale[...] < cap_value).astype(f32)
+    )
+    grad_cos = factor * grad_logits
+    at = pl.ds(pl.multiple_of(here.d * slots, slots), slots)
+    turn[0] = grad_cos
+    turn[1] = jnp.transpose(grad_cos)
+    left = turn[here.t, at, :].astype(bf16)
+    right = low_all[1 - here.t].reshape(total, width)
+    grad_unit = mdot(left, right)
+    grad_pooled = scale_row * (
+        grad_unit - unit * jnp.sum(unit * grad_unit, 1, keepdims=True)
+    )
+    grad_out[...] = grad_pooled / counts[...]
+    row = lax.broadcasted_iota(jnp.int32, stats.shape, 0)
+    stats[...] = jnp.where(row == 0, loss_sum, jnp.where(row == 1, query_count, grad_scale))
+
+
+def loss_step(part, counts, doc_ok, query_ok, target, scale):
+    n_dp = lax.axis_size("dp")
+    slots, width = part.shape
+    total = n_dp * slots
+    dma = pltpu.SemaphoreType.DMA
+    return pl.pallas_call(
+        loss_body,
+        out_shape=[sds(part.shape, f32), sds((8, 128), f32)],
+        in_specs=[VM] * 6,
+        out_specs=[VM] * 2,
+        scratch_shapes=[
+            pltpu.VMEM(part.shape, f32),
+            pltpu.VMEM((2, n_dp, slots, width), bf16),
+            pltpu.VMEM((2, total, total), f32),
+            dma, dma, dma((2 * n_dp,)), dma((2 * n_dp,)),
+        ],
+        compiler_params=params(3),
+        name="loss",
+    )(part, counts, doc_ok, query_ok, target, scale)
+
+
+def rotary_tables(positions):
+    half_dim = HDIM // 2
+    inverse = 1000.0 ** (-2.0 * jnp.arange(half_dim, dtype=f32) / HDIM)
+    angles = positions.astype(f32)[:, None] * inverse[None, :]
+    angles = jnp.concatenate([angles] * 4, 1)
+    return jnp.cos(angles), jnp.sin(angles)
+
+
+def layout(lengths, places, slot_count):
+    end_points = jnp.cumsum(lengths)
+    segment = jnp.sum((places[:, None] >= end_points[None, :]).astype(jnp.int32), 1)
+    starts = jnp.concatenate([jnp.zeros((1,), jnp.int32), end_points])
+    slot_ids = jnp.arange(slot_count + 1, dtype=jnp.int32)
+    segment_start = jnp.sum(jnp.where(segment[:, None] == slot_ids[None, :], starts[None, :], 0), 1)
+    return segment, places - segment_start
+
+
+def norm_back(grad, hat, scale, gain):
+    grad_hat = grad * gain
+    first = jnp.mean(grad_hat, -1, keepdims=True)
+    second = jnp.mean(grad_hat * hat, -1, keepdims=True)
+    return (
+        scale * (grad_hat - first - hat * second),
+        jnp.sum(grad * hat, 0),
+        jnp.sum(grad, 0),
+    )
+
+
+def glu(gate_vals, up_vals):
+    return jax.nn.silu(gate_vals) * up_vals
+
+
+def adamw(weight_in, gradient, first_mom, second, factor, step_num, rate):
+    gradient = gradient * factor
+    first_new = beta_one * first_mom + (1.0 - beta_one) * gradient
+    second_new = beta_two * second + (1.0 - beta_two) * gradient * gradient
+    first_hat = first_new / (1.0 - beta_one**step_num)
+    second_hat = second_new / (1.0 - beta_two**step_num)
+    weight_new = weight_in - rate * (
+        first_hat / (jnp.sqrt(second_hat) + adam_eps) + decay_rate * weight_in
+    )
+    return (weight_new, first_new, second_new)
+
+
+def name_rows(ids, d, n_dp, row_count, room):
+    tok = ids.shape[0]
+    owner = ids // row_count
+    local = ids - owner * row_count
+    order = jnp.bitwise_xor(owner, d)
+    places = jnp.arange(tok, dtype=jnp.int32)
+    first_at = jnp.min(
+        jnp.where(ids[:, None] == ids[None, :], places[None, :], tok), 1
+    )
+    is_first = first_at == places
+    slot = jnp.sum(
+        (
+            (places[None, :] < first_at[:, None])
+            & is_first[None, :]
+            & (owner[None, :] == owner[:, None])
+        ).astype(jnp.int32),
+        1,
+    )
+    over = jnp.max(slot) >= room
+    pos = order * room + slot
+    wanted = jnp.arange(n_dp * room, dtype=jnp.int32)
+    listed = jnp.max(
+        jnp.where((pos[None, :] == wanted[:, None]) & is_first[None, :], local[None, :], -1), 1
+    ).reshape(n_dp, 1, room)
+    listed = jnp.pad(listed, ((0, 0), (0, 0), (0, 128 - room)), constant_values=-1)
+    flag = jnp.broadcast_to(over.astype(jnp.int32), (n_dp, 7, 128))
+    return pos, jnp.concatenate([listed, flag], 1)
 
 
 def layer_norm(stream, gain_row, bias_row):
@@ -34,7 +1019,7 @@
     return values * cosine + turned * sine_table
 
 
-def rotary_tables(positions, head_dim):
+def plain_rotary_tables(positions, head_dim):
     half_dim = head_dim // 2
     inverse = 1000.0 ** (-2.0 * jnp.arange(half_dim, dtype=jnp.float32) / head_dim)
     angles = positions.astype(jnp.float32)[:, None] * inverse[None, :]
@@ -42,7 +1027,7 @@
     return (jnp.cos(angles), jnp.sin(angles))
 
 
-def layout(lengths, tok_count, slot_count):
+def plain_layout(lengths, tok_count, slot_count):
     end_points = jnp.cumsum(lengths)
     places = jnp.arange(tok_count, dtype=jnp.int32)
     segment = jnp.sum((places[:, None] >= end_points[None, :]).astype(jnp.int32), 1)
@@ -52,7 +1037,7 @@
     return (segment, places - segment_start)
 
 
-def glu(gate_vals, up_vals):
+def plain_glu(gate_vals, up_vals):
     return jax.nn.silu(gate_vals) * up_vals
 
 
@@ -151,7 +1136,7 @@
     input_zero = stream_zero.astype(jnp.bfloat16)
     projected = jnp.einsum("td,dcf->tcf", input_zero, w_qkv, preferred_element_type=jnp.float32)
     heads_view = projected.reshape(tok_count, 3, heads_local, HDIM)
-    cosine, sine_table = rotary_tables(positions, HDIM)
+    cosine, sine_table = plain_rotary_tables(positions, HDIM)
     query_low = rotate(heads_view[:, 0], cosine, sine_table).astype(jnp.bfloat16)
     key_low = rotate(heads_view[:, 1], cosine, sine_table).astype(jnp.bfloat16)
     value_low = heads_view[:, 2].astype(jnp.bfloat16)
@@ -164,7 +1149,7 @@
     stream_one = layer_norm(sum_one, norm_rows[2], norm_rows[3])
     input_one = stream_one.astype(jnp.bfloat16)
     gate_up = jnp.einsum("td,dcf->tcf", input_one, w_ffn, preferred_element_type=jnp.float32)
-    hidden_low = glu(gate_up[:, 0], gate_up[:, 1]).astype(jnp.bfloat16)
+    hidden_low = plain_glu(gate_up[:, 0], gate_up[:, 1]).astype(jnp.bfloat16)
     ffn_branch = model_total(
         jnp.einsum("tf,df->td", hidden_low, w_down, preferred_element_type=jnp.float32)
     )
@@ -210,7 +1195,7 @@
     ffn_low = grad_sum_two.astype(jnp.bfloat16)
     grad_down = jnp.einsum("td,tf->df", ffn_low, hidden_low, preferred_element_type=jnp.float32)
     grad_hidden = jnp.einsum("td,df->tf", ffn_low, w_down, preferred_element_type=jnp.float32)
-    grad_gate, grad_up = jax.vjp(glu, gate_up[:, 0], gate_up[:, 1])[1](grad_hidden)
+    grad_gate, grad_up = jax.vjp(plain_glu, gate_up[:, 0], gate_up[:, 1])[1](grad_hidden)
     gate_grads = jnp.stack([grad_gate, grad_up], 1).astype(jnp.bfloat16)
     grad_ffn = jnp.einsum("td,tcf->dcf", input_one, gate_grads, preferred_element_type=jnp.float32)
     grad_stream_one = grad_sum_two + model_total(
@@ -232,7 +1217,7 @@
         log_total,
         segment,
     )
-    cosine, sine_table = rotary_tables(positions, head_dim)
+    cosine, sine_table = plain_rotary_tables(positions, head_dim)
     turn_back = jax.vjp(lambda values: rotate(values, cosine, sine_table), grad_query)[1]
     grad_projected = jnp.stack([turn_back(grad_query)[0], turn_back(grad_key)[0], grad_value], 1)
     grad_projected = grad_projected.reshape(tok_count, 3, heads_local * head_dim).astype(
@@ -251,7 +1236,7 @@
     return (grad_embed, (grad_qkv, grad_out, grad_ffn, grad_down), norm_grads)
 
 
-def adamw(weight_in, gradient, first_mom, second, factor, step_num, rate):
+def plain_adamw(weight_in, gradient, first_mom, second, factor, step_num, rate):
     gradient = gradient * factor
     first_new = beta_one * first_mom + (1.0 - beta_one) * gradient
     second_new = beta_two * second + (1.0 - beta_two) * gradient * gradient
@@ -263,7 +1248,7 @@
     return (weight_new, first_new, second_new)
 
 
-def local(
+def plain_step(
     token_ids,
     seq_lengths,
     positives,
@@ -313,7 +1298,7 @@
         jnp.float32
     )
     lengths_row = seq_lengths[tower_idx, data_idx]
-    segment, positions = layout(lengths_row, tok_count, slot_count)
+    segment, positions = plain_layout(lengths_row, tok_count, slot_count)
     stream_two, kept_vals = layer_forward(embed_rows, segment, positions, weights, norm_params)
     member = (segment[None, :] == jnp.arange(slot_count, dtype=jnp.int32)[:, None]).astype(
         jnp.float32
@@ -394,13 +1379,13 @@
     grad_norm = jnp.sqrt(total_sq)
     factor = jnp.minimum(1.0, clip_max / (grad_norm + 1e-06))
     step_num = float(STEP)
-    embed_new = adamw(embedding, embed_grad, embed_m, embed_v, factor, step_num, learn_rate)
-    qkv_new = adamw(attn_in, shard_grads[0], attn_in_m, attn_in_v, factor, step_num, learn_rate)
-    out_new = adamw(attn_out, shard_grads[1], attn_out_m, attn_out_v, factor, step_num, out_rate)
-    ffn_new = adamw(ffn_in, shard_grads[2], ffn_in_m, ffn_in_v, factor, step_num, learn_rate)
-    down_new = adamw(ffn_out, shard_grads[3], ffn_out_m, ffn_out_v, factor, step_num, learn_rate)
-    norms_new = adamw(norm_params, norm_grad, norm_m, norm_v, factor, step_num, norm_rate)
-    scale_new = adamw(
+    embed_new = plain_adamw(embedding, embed_grad, embed_m, embed_v, factor, step_num, learn_rate)
+    qkv_new = plain_adamw(attn_in, shard_grads[0], attn_in_m, attn_in_v, factor, step_num, learn_rate)
+    out_new = plain_adamw(attn_out, shard_grads[1], attn_out_m, attn_out_v, factor, step_num, out_rate)
+    ffn_new = plain_adamw(ffn_in, shard_grads[2], ffn_in_m, ffn_in_v, factor, step_num, learn_rate)
+    down_new = plain_adamw(ffn_out, shard_grads[3], ffn_out_m, ffn_out_v, factor, step_num, learn_rate)
+    norms_new = plain_adamw(norm_params, norm_grad, norm_m, norm_v, factor, step_num, norm_rate)
+    scale_new = plain_adamw(
         logit_scale, scale_grad.reshape(1), scale_m, scale_v, factor, step_num, learn_rate
     )
     return (
@@ -431,61 +1416,151 @@
     )
 
 
+def lean_step(args, pos, heard):
+    (
+        token_ids, seq_lengths, positives, embedding, attn_in, attn_out, ffn_in, ffn_out,
+        norm_params, logit_scale, embed_m, embed_v, attn_in_m, attn_in_v, attn_out_m, attn_out_v,
+        ffn_in_m, ffn_in_v, ffn_out_m, ffn_out_v, norm_m, norm_v, scale_m, scale_v,
+    ) = args
+    tower_idx = lax.axis_index("tower")
+    data_idx = lax.axis_index("dp")
+    model_idx = lax.axis_index("mp")
+    slot_count = seq_lengths.shape[2]
+    tok = token_ids.shape[1]
+    half = tok // 2
+    row_count = embedding.shape[0]
+    feats = attn_out.shape[1]
+    ff = ffn_out.shape[1]
+    part_ff = ff // 2
+
+    shards = (
+        attn_in.reshape(attn_in.shape[0], -1), attn_out, ffn_in[:, 0], ffn_in[:, 1], ffn_out,
+    )
+    kinds = ("plain", "late", "late", "late", "late")
+    gather_pieces = [(0, "plain", 0, 3 * feats, 0), (1, "late", 0, feats, 1)]
+    for turn, which in enumerate((2, 3, 4)):
+        gather_pieces.append((which, "late", 0, part_ff, 1 + turn))
+        gather_pieces.append((which, "early", part_ff, part_ff, 1 + turn))
+    places = (jnp.arange(tok, dtype=jnp.int32) + model_idx * half) % tok
+    pos_rel = jnp.where(model_idx == 0, pos, jnp.concatenate([pos[half:], pos[:half]]))
+    lengths_row = seq_lengths[tower_idx, data_idx]
+    segment, positions = layout(lengths_row, places, slot_count)
+    cosine, sine = rotary_tables(positions)
+    seg_row, seg_col = segment[None, :], segment[:, None]
+    kept, weights = forward_pass(
+        embedding, heard[0], pos_rel[:, None], norm_params[0:2], cosine, sine, seg_row, seg_col,
+        shards, kinds, gather_pieces,
+    )
+    emb, stream_zero, input_zero, query, key, value, lse = kept[:7]
+    att = kept[7:9]
+    w_qkv, w_out, w_gate, w_up, w_down = weights
+
+    sum_one = stream_zero + tdot(att[0], w_out[0]) + tdot(att[1], w_out[1])
+    hat_one, scale_one = norm_parts(sum_one)
+    stream_one = hat_one * norm_params[2] + norm_params[3]
+    input_one = stream_one.astype(bf16)
+    gates = [mdot(input_one, w_gate[j]) for j in range(2)]
+    ups = [mdot(input_one, w_up[j]) for j in range(2)]
+    hidden = [glu(gates[j], ups[j]).astype(bf16) for j in range(2)]
+    sum_two = stream_one + tdot(hidden[0], w_down[0]) + tdot(hidden[1], w_down[1])
+    hat_two, scale_two = norm_parts(sum_two)
+    stream_two = hat_two * norm_params[4] + norm_params[5]
+
+    member = (segment[None, :half] == jnp.arange(slot_count, dtype=jnp.int32)[:, None]).astype(f32)
+    counts = jnp.maximum(lengths_row, 1).astype(f32)[:, None]
+    part = jnp.dot(member, stream_two, precision=highest)
+    doc_ok = (seq_lengths[1].reshape(1, -1) > 0).astype(f32)
+    query_ok = (seq_lengths[0].reshape(-1, 1) > 0).astype(f32)
+    grad_pool, stats = loss_step(
+        part, counts, doc_ok, query_ok, positives.reshape(-1, 1), logit_scale.reshape(1, 1)
+    )
+    loss_sum, query_count, scale_grad = stats[0, 0], stats[1, 0], stats[2, 0]
+
+    grad_two = jnp.dot(member.T, grad_pool, precision=highest)
+    grad_sum_two, gain_two, bias_two = norm_back(grad_two, hat_two, scale_two, norm_params[4])
+    ffn_low = grad_sum_two.astype(bf16)
+
+    def weight_grad(left, right):
+        return jnp.einsum("td,tf->df", left, right, preferred_element_type=f32).astype(bf16)
+
+    grad_down, grad_gate, grad_up = [], [], []
+    grad_stream_one = grad_sum_two
+    for j in range(2):
+        grad_down.append(weight_grad(ffn_low, hidden[j]))
+        grad_hidden = mdot(ffn_low, w_down[j])
+        d_gate, d_up = jax.vjp(glu, gates[j], ups[j])[1](grad_hidden)
+        d_gate, d_up = d_gate.astype(bf16), d_up.astype(bf16)
+        grad_gate.append(weight_grad(input_one, d_gate))
+        grad_up.append(weight_grad(input_one, d_up))
+        grad_stream_one = grad_stream_one + tdot(d_gate, w_gate[j]) + tdot(d_up, w_up[j])
+    grad_sum_one, gain_one, bias_one = norm_back(
+        grad_stream_one, hat_one, scale_one, norm_params[2]
+    )
+    attn_low = grad_sum_one.astype(bf16)
+    grad_out = [weight_grad(attn_low, att[j]) for j in range(2)]
+    pieces = []
+    for turn, which in enumerate((2, 0, 1)):
+        pieces.append((which, "early", 0, part_ff, turn))
+        pieces.append((which, "late", part_ff, part_ff, turn))
+    grad_proj, embed_low, zero_norms, r_gate, r_up, r_down, squares = backward_pass(
+        attn_low, w_out, query, key, value, lse, cosine, sine, seg_row, seg_col, grad_sum_one,
+        emb, norm_params[0:2], w_qkv, (grad_gate, grad_up, grad_down), pieces,
+    )
+    grad_qkv = weight_grad(input_zero, grad_proj)
+    norm_part = jnp.concatenate(
+        [zero_norms[0:2], jnp.stack([gain_one, bias_one, gain_two, bias_two]), zero_norms[2:4]]
+    )
+    pieces = [(0, "plain", 0, 2 * feats, 0), (0, "plain", 2 * feats, feats, 1), (1, "late", 0, feats, 1)]
+    embed_grad, norm_sum, r_qkv, r_out, total = spread_pass(
+        embed_low, pos_rel[None, :], heard, norm_part, squares, grad_qkv, grad_out, row_count,
+        pieces,
+    )
+    norm_grad = norm_sum[:6]
+    r_qkv = r_qkv.reshape(attn_in.shape)
+    total_sq = total[0, 0] + scale_grad * scale_grad
+    grad_norm = jnp.sqrt(total_sq)
+    factor = jnp.minimum(1.0, clip_max / (grad_norm + 1e-06))
+    step_num = float(STEP)
+    embed_new = adamw(embedding, embed_grad, embed_m, embed_v, factor, step_num, learn_rate)
+    qkv_new = adamw(attn_in, r_qkv, attn_in_m, attn_in_v, factor, step_num, learn_rate)
+    out_new = adamw(attn_out, r_out, attn_out_m, attn_out_v, factor, step_num, out_rate)
+    r_ffn = jnp.stack([r_gate, r_up], 1)
+    ffn_new = adamw(ffn_in, r_ffn, ffn_in_m, ffn_in_v, factor, step_num, learn_rate)
+    down_new = adamw(ffn_out, r_down, ffn_out_m, ffn_out_v, factor, step_num, learn_rate)
+    norms_new = adamw(norm_params, norm_grad, norm_m, norm_v, factor, step_num, norm_rate)
+    scale_new = adamw(
+        logit_scale, scale_grad.reshape(1), scale_m, scale_v, factor, step_num, learn_rate
+    )
+    return (
+        *embed_new, *qkv_new, *out_new, *ffn_new, *down_new, *norms_new, *scale_new,
+        loss_sum.reshape(1), query_count.reshape(1), grad_norm.reshape(1),
+    )
+
+
+def local(*args):
+    token_ids, embedding = args[0], args[3]
+    n_dp = lax.axis_size("dp")
+    room = max(32, token_ids.shape[1] // n_dp)
+    pos, lists = name_rows(
+        token_ids[0], lax.axis_index("dp"), n_dp, embedding.shape[0], room
+    )
+    heard, flag = exchange_lists(lists)
+    return lax.cond(
+        flag[1, 0] > 0,
+        lambda values: plain_step(*values),
+        lambda values: lean_step(values, pos, heard),
+        args,
+    )
+
+
 def solution(mesh):
+    table, rows3, rows2 = P("dp", "mp"), P(("tower", "dp"), None, "mp"), P(("tower", "dp"), "mp")
+    weights = (table, rows3, rows2, rows3, rows2)
+    moments = tuple(spec for spec in weights for _ in range(2))
     return jax.shard_map(
         local,
         mesh=mesh,
-        in_specs=(
-            P("tower", "dp"),
-            P(),
-            P(),
-            P("dp", "mp"),
-            P(("tower", "dp"), None, "mp"),
-            P(("tower", "dp"), "mp"),
-            P(("tower", "dp"), None, "mp"),
-            P(("tower", "dp"), "mp"),
-            P(),
-            P(),
-            P("dp", "mp"),
-            P("dp", "mp"),
-            P(("tower", "dp"), None, "mp"),
-            P(("tower", "dp"), None, "mp"),
-            P(("tower", "dp"), "mp"),
-            P(("tower", "dp"), "mp"),
-            P(("tower", "dp"), None, "mp"),
-            P(("tower", "dp"), None, "mp"),
-            P(("tower", "dp"), "mp"),
-            P(("tower", "dp"), "mp"),
-            P(),
-            P(),
-            P(),
-            P(),
-        ),
-        out_specs=(
-            P("dp", "mp"),
-            P("dp", "mp"),
-            P("dp", "mp"),
-            P(("tower", "dp"), None, "mp"),
-            P(("tower", "dp"), None, "mp"),
-            P(("tower", "dp"), None, "mp"),
-            P(("tower", "dp"), "mp"),
-            P(("tower", "dp"), "mp"),
-            P(("tower", "dp"), "mp"),
-            P(("tower", "dp"), None, "mp"),
-            P(("tower", "dp"), None, "mp"),
-            P(("tower", "dp"), None, "mp"),
-            P(("tower", "dp"), "mp"),
-            P(("tower", "dp"), "mp"),
-            P(("tower", "dp"), "mp"),
-            P(),
-            P(),
-            P(),
-            P(),
-            P(),
-            P(),
-            P(),
-            P(),
-            P(),
-        ),
+        in_specs=(P("tower", "dp"), P(), P()) + weights + (P(), P()) + moments + (P(),) * 4,
+        out_specs=tuple(spec for spec in weights for _ in range(3)) + (P(),) * 9,
         check_vma=False,
     )

time: 1790 us -> 526 us (0.29)
  waiting for transfers between devices: 1090 us -> 0 us
  Pallas kernels: 0 us -> 365 us
  blocking collectives: 202 us -> 0 us
  other arithmetic: 216 us -> 32.9 us
  matrix products: 148 us -> 56 us
  local copies, waits for them, and re-layouts: 88.5 us -> 30.6 us
    all_gather x6 -> x0, waiting for transfers between devices: 655 us -> none  [the longest x1 450 us: local(): lax.all_gather(embedding.astype(jnp.bfloat16), 'dp', axis=0, tiled=True)]
    pallas_call x0 -> x5, Pallas kernels: none -> 365 us  [the longest x1 154 us: forward_pass(): pl.pallas_call(lambda *refs: forward_body(room, kinds, pieces, *refs), ou...]
    reduce_scatter x5 -> x0, waiting for transfers between devices: 269 us -> none  [the longest x1 114 us: local(): lax.psum_scatter(layer_grads[2], ('tower', 'dp'), scatter_dimension=0, ti...]
    psum x4 -> x0, waiting for transfers between devices: 168 us -> none  [model_total(): return lax.psum(values.astype(jnp.bfloat16), 'mp').astype(jnp.float32)]
    scatter-add x1 -> x0, other arithmetic: 109 us -> none  [local(): jax.ops.segment_sum(lax.all_gather(column_part, ('tower', 'dp'), axis=0,...]
    all_gather x3 -> x0, blocking collectives: 107 us -> none  [the longest x1 37.6 us: local(): lax.all_gather(attn_out.astype(jnp.bfloat16), ('tower', 'dp'), axis=0, ti...]
    psum x2 -> x0, blocking collectives: 95.7 us -> none  [the longest x1 58.1 us: local(): lax.psum((norm_grads, loss_part, scale_part), ('tower', 'dp'))]
    dot_general x31 -> x25, matrix products: 148 us -> 56 us  [the longest x9 24.9 us: weight_grad(): jnp.einsum('td,tf->df', left, right, preferred_element_type=f32)]
  transfers between devices with their start and end apart: 15 -> 0, of which waited for: 13 -> 0; matrix products, arithmetic and copies ran while one was open for 4% -> 0% of each run, Pallas kernels for 0% -> 0%
where the time goes in v2:
time: 526 us; the launch traced here: 520 us
  Pallas kernels  365 us (69%)
  matrix products  56 us (11%)
  other arithmetic  32.9 us (6%)
  local copies, waits for them, and re-layouts  30.6 us (6%)
  between operations  20.2 us (4%)
  loops' own time  15.4 us (3%)
    pallas_call x1, Pallas kernels, forward_pass(): pl.pallas_call(lambda *refs: forward_body(room, kinds, pieces, *refs), ou...  154 us
    pallas_call x1, Pallas kernels, backward_pass(): pl.pallas_call(lambda *refs: backward_body(pieces, (len(held), len(landed...  106 us
    pallas_call x1, Pallas kernels, spread_pass(): pl.pallas_call(lambda *refs: spread_body(room, pieces, (len(held), len(la...  77 us
    dot_general x9, matrix products, weight_grad(): jnp.einsum('td,tf->df', left, right, preferred_element_type=f32)  24.9 us
    pallas_call x1, Pallas kernels, loss_step(): pl.pallas_call(loss_body, out_shape=[sds(part.shape, f32), sds((8, 128),...  17.9 us
    sub x6, other arithmetic, adamw(): weight_in - rate * (first_hat / (jnp.sqrt(second_hat) + adam_eps) + decay...  17.9 us
    another operation x1, loops' own time, local(): lax.cond(flag[1, 0] > 0, lambda values: plain_step(*values), lambda value...  15.4 us
    dot_general x6, matrix products, mdot(): return jnp.dot(lhs, rhs, preferred_element_type=f32)  14.1 us

profile of v2, /device:TPU:1, one launch (start us, length us, event | category | flops | bytes accessed | tf_op | source)
XLA Modules:
  0.0 519.9 jit_solution(15360933528286270083)
XLA Ops:
  7.2 1.5 select_reduce_fusion.5
  10.2 1.5 convert_reduce_fusion.4
  14.6 9.9 %lists.1 = (s32[2,8,8,128]{3,2,1,0:T(8,128)S(1)}, s32[8,128]{1,0:T(8,128)}) custom-call(s32[8,8,128]{2,1,0:T(8,128)} %concatenate.50.lists), custom_call_target="tpu_custom_call" | custom-call | tf_op jit(solution)/shard_map/lists/pallas_call | solution.py:286
  26.4 481.9 %conditional.1 = (f32[3816,384]{1,0:T(8,128)}, f32[3816,384]{1,0:T(8,128)}, f32[3816,384]{1,0:T(8,128)}, f32[48,3,384]{2,0,1:T(8,128)}, f32[48,3,384]{2,0,1:T(8,...) conditional(s32[]{:T(128)} %bitcast.74, ...), branch_computations={%region_4.20_spmd, %region_20.77_spmd} | conditional | flops 32450023424 | bytes 1181347840 | solution.py:1548
  36.6 1.6 copy.278
  40.5 3.0 fusion.53
  44.5 153.6 %forward.1 = (bf16[512,768]{1,0:T(8,128)(2,1)}, f32[512,768]{1,0:T(8,128)}, bf16[1024,768]{1,0:T(8,128)(2,1)}, bf16[1024,384]{1,0:T(8,128)(2,1)}, bf16[1024,384]...) custom-call(f32[3816,384]{1,0:T(8,128)} %get-tuple-element.174.refs_, ...), custom_call_target="tpu_custom_call" | custom-call | tf_op jit(solution)/shard_map/cond/branch_0_fun/forward/pallas_call | solution.py:498
  198.1 1.9 fusion.202
  200.0 1.9 fusion.198
  208.3 3.2 multiply_convert_fusion.4
  213.7 3.2 multiply_convert_fusion.3
  216.9 1.6 fusion.199
  218.9 1.5 fusion.43.part
  220.4 17.9 %loss.1 = (f32[16,768]{1,0:T(8,128)}, f32[8,128]{1,0:T(8,128)}) custom-call(f32[16,768]{1,0:T(8,128)} %fusion.43.part, f32[16,1]{1,0:T(8,128)} %maximum_convert_fusion.counts, f32[1,128]{1,0:T(1,128)} %reshape.738.doc_ok, f32[128,1]{1,0:T(8,128)} %reshape.781.query_ok, s32[128,1]{1,0:T(8,128)} %reshape.782.target, f32[1,1]{1,0:T(1,128)} %bitcast.15.scale), custom_call_target="tpu_custom_call" | custom-call | tf_op jit(solution)/shard_map/cond/branch_0_fun/loss/pallas_call | solution.py:920
  240.9 2.3 multiply_reduce_fusion.1
  245.9 2.5 fusion.37
  249.4 2.5 multiply_convert_fusion.1
  255.3 1.4 fusion.206
  256.9 2.1 multiply_reduce_fusion.2
  259.1 1.6 fusion.182
  263.6 2.8 convolution_convert_fusion.3
  266.4 2.8 convolution_convert_fusion.6
  269.2 2.8 convolution_convert_fusion.1
  272.0 2.8 convolution_convert_fusion.2
  274.9 2.8 convolution_convert_fusion.4
  277.7 2.8 convolution_convert_fusion.5
  280.5 106.4 %backward.1 = (bf16[1024,1152]{1,0:T(8,128)(2,1)}, bf16[512,768]{1,0:T(8,128)(2,1)}, f32[8,768]{1,0:T(8,128)}, f32[48,1536]{1,0:T(8,128)}, f32[48,1536]{1,0:T(8,...) custom-call(bf16[512,768]{1,0:T(8,128)(2,1)} %copy-done.29, bf16[768,384]{1,0:T(8,128)(2,1)} %bitcast.299, ...), custom_call_target="tpu_custom_call" | custom-call | tf_op jit(solution)/shard_map/cond/branch_0_fun/backward/pallas_call | solution.py:681
  388.3 5.1 convolution_convert_fusion
  393.5 77.0 %spread.1 = (f32[3816,384]{1,0:T(8,128)}, f32[8,768]{1,0:T(8,128)}, f32[48,1152]{1,0:T(8,128)}, f32[48,384]{1,0:T(8,128)}, f32[8,128]{1,0:T(8,128)}) custom-call(bf16[512,768]{1,0:T(8,128)(2,1)} %get-tuple-element.204.refs_0_, s32[1,1024]{1,0:T(1,128)} %bitcast.323, s32[2,8,8,128]{3,2,1,0:T(8,128)S(1)} %get-tuple-element.176.refs_2_, ...), custom_call_target="tpu_custom_call" | custom-call | tf_op jit(solution)/shard_map/cond/branch_0_fun/spread/pallas_call | solution.py:827
  476.4 1.8 multiply_subtract_fusion.3
  478.2 1.8 copy_subtract_fusion
  487.7 11.2 %multiply_subtract_fusion = (f32[3816,384]{1,0:T(8,128)}, f32[3816,384]{1,0:T(8,128)}, f32[3816,384]{1,0:T(8,128)}) fusion(f32[3816,384]{1,0:T(8,128)S(1)} %bitcast.277, f32[3816,384]{1,0:T(8,128)S(1)} %copy-done.22, f32[]{:T(128)} %bitcast.27, f32[3816,384]{1,0:T(8,128)} %get-tuple-element.175, f32[3816,384]{1,0:T(8,128)} %get-tuple-element.212), kind=kLoop, calls=%fused_computation.51 | loop fusion | flops 23445504 | bytes 41029636 | tf_op jit(solution)/shard_map/cond/branch_0_fun/sub | solution.py:974
  (169 shorter events, 49.4 us)
Async XLA Ops:
  26.4 17.1 %copy-start.15 = (f32[48,2,1536]{2,1,0:T(2,128)S(1)}, f32[48,2,1536]{2,1,0:T(2,128)}, u32[]{:S(2)}) copy-start(f32[48,2,1536]{2,1,0:T(2,128)} %get-tuple-element.727) | copy-start | bytes 1769476 | tf_op jit(solution)/shard_map/cond
  29.2 15.3 %copy-start.105 = (s32[1024]{0:T(1024)}, s32[1024]{0:T(1024)S(1)}, u32[]{:S(2)}) copy-start(s32[1024]{0:T(1024)S(1)} %add_select_fusion.1) | copy-start | bytes 12292 | tf_op jit(solution)/shard_map/cond
  31.2 13.3 %copy-start.23 = (f32[48,1536]{1,0:T(8,128)S(1)}, f32[48,1536]{1,0:T(8,128)}, u32[]{:S(2)}) copy-start(f32[48,1536]{1,0:T(8,128)} %get-tuple-element.183.refs_12_) | copy-start | bytes 884740 | tf_op jit(solution)/shard_map/cond
  31.2 13.3 %copy-start.43 = (f32[48,384]{1,0:T(8,128)S(1)}, f32[48,384]{1,0:T(8,128)}, u32[]{:S(2)}) copy-start(f32[48,384]{1,0:T(8,128)} %get-tuple-element.181.refs_9_) | copy-start | bytes 221188 | tf_op jit(solution)/shard_map/cond
  31.5 13.0 %copy-start.89 = (s32[1024]{0:T(1024)}, s32[1024]{0:T(1024)S(1)}, u32[]{:S(2)}) copy-start(s32[1024]{0:T(1024)S(1)} %convert_reduce_fusion) | copy-start | bytes 12292 | tf_op jit(solution)/shard_map/cond
  203.5 9.6 %copy-start.62 = (bf16[512,768]{1,0:T(8,128)(2,1)}, bf16[512,768]{1,0:T(8,128)(2,1)S(1)}, u32[]{:S(2)}) copy-start(bf16[512,768]{1,0:T(8,128)(2,1)S(1)} %fusion.46) | copy-start | bytes 2359300 | tf_op jit(solution)/shard_map/cond
  205.5 7.6 %copy-start.137 = (f32[512,1536]{1,0:T(8,128)}, f32[512,1536]{1,0:T(8,128)S(1)}, u32[]{:S(2)}) copy-start(f32[512,1536]{1,0:T(8,128)S(1)} %fusion.205) | copy-start | bytes 9437188 | tf_op jit(solution)/shard_map/cond
  208.3 3.2 copy-start.139
  208.3 3.4 copy-start.134
  213.7 3.2 copy-start.132
  240.9 2.9 copy-start.148
  245.9 3.5 copy-start.147
  259.1 3.1 copy-start.66
  260.7 5.7 %copy-start.29 = (bf16[512,768]{1,0:T(8,128)(2,1)}, bf16[512,768]{1,0:T(8,128)(2,1)S(1)}, u32[]{:S(2)}) copy-start(bf16[512,768]{1,0:T(8,128)(2,1)S(1)} %get-tuple-element.890.refs_0_) | copy-start | bytes 2359300 | tf_op jit(solution)/shard_map/cond
  260.7 2.9 copy-start.63
  266.4 2.8 copy-start.144
  269.2 2.8 copy-start.146
  280.5 107.8 %copy-start.136 = (bf16[1024,768]{1,0:T(8,128)(2,1)S(1)}, bf16[1024,768]{1,0:T(8,128)(2,1)}, u32[]{:S(2)}) copy-start(bf16[1024,768]{1,0:T(8,128)(2,1)} %get-tuple-element.207) | copy-start | bytes 4718596 | tf_op jit(solution)/shard_map/cond
  393.4 80.5 %copy-start.72 = (f32[6,768]{1,0:T(8,128)S(1)}, f32[6,768]{1,0:T(8,128)}, u32[]{:S(2)}) copy-start(f32[6,768]{1,0:T(8,128)} %get-tuple-element.178) | copy-start | bytes 55300 | tf_op jit(solution)/shard_map/cond
  393.4 80.5 %copy-start.92 = (f32[6,768]{1,0:T(8,128)S(1)}, f32[6,768]{1,0:T(8,128)}, u32[]{:S(2)}) copy-start(f32[6,768]{1,0:T(8,128)} %get-tuple-element.226) | copy-start | bytes 55300 | tf_op jit(solution)/shard_map/cond
  393.4 80.5 %copy-start.94 = (f32[6,768]{1,0:T(8,128)S(1)}, f32[6,768]{1,0:T(8,128)}, u32[]{:S(2)}) copy-start(f32[6,768]{1,0:T(8,128)} %get-tuple-element.228) | copy-start | bytes 55300 | tf_op jit(solution)/shard_map/cond
  393.4 84.8 %copy-start.26 = (f32[48,3,384]{2,0,1:T(8,128)S(1)}, f32[48,3,384]{2,0,1:T(8,128)}, u32[]{:S(2)}) copy-start(f32[48,3,384]{2,0,1:T(8,128)} %get-tuple-element.726) | copy-start | bytes 663556 | tf_op jit(solution)/shard_map/cond
  470.5 11.6 %copy-start.46 = (f32[48,1536]{1,0:T(8,128)S(1)}, f32[48,1536]{1,0:T(8,128)}, u32[]{:S(2)}) copy-start(f32[48,1536]{1,0:T(8,128)} %get-tuple-element.223) | copy-start | bytes 884740 | tf_op jit(solution)/shard_map/cond
  470.5 11.6 %copy-start.48 = (f32[48,1536]{1,0:T(8,128)S(1)}, f32[48,1536]{1,0:T(8,128)}, u32[]{:S(2)}) copy-start(f32[48,1536]{1,0:T(8,128)} %get-tuple-element.225) | copy-start | bytes 884740 | tf_op jit(solution)/shard_map/cond
  476.3 6.9 %copy-start.33 = (f32[48,2,1536]{2,1,0:T(2,128)S(1)}, f32[48,2,1536]{2,1,0:T(2,128)}, u32[]{:S(2)}) copy-start(f32[48,2,1536]{2,1,0:T(2,128)} %get-tuple-element.738) | copy-start | bytes 1769476 | tf_op jit(solution)/shard_map/cond
  476.3 6.9 %copy-start.35 = (f32[48,2,1536]{2,1,0:T(2,128)S(1)}, f32[48,2,1536]{2,1,0:T(2,128)}, u32[]{:S(2)}) copy-start(f32[48,2,1536]{2,1,0:T(2,128)} %get-tuple-element.739) | copy-start | bytes 1769476 | tf_op jit(solution)/shard_map/cond
  476.4 5.8 %copy-start.77 = (f32[48,1536]{1,0:T(8,128)S(1)}, f32[48,1536]{1,0:T(8,128)}, u32[]{:S(2)}) copy-start(f32[48,1536]{1,0:T(8,128)} %get-tuple-element.224) | copy-start | bytes 884740 | tf_op jit(solution)/shard_map/cond
  476.4 6.8 %copy-start.75 = (f32[48,1536]{1,0:T(8,128)S(1)}, f32[48,1536]{1,0:T(8,128)}, u32[]{:S(2)}) copy-start(f32[48,1536]{1,0:T(8,128)} %get-tuple-element.220) | copy-start | bytes 884740 | tf_op jit(solution)/shard_map/cond
  476.4 6.8 %copy-start.76 = (f32[48,1536]{1,0:T(8,128)S(1)}, f32[48,1536]{1,0:T(8,128)}, u32[]{:S(2)}) copy-start(f32[48,1536]{1,0:T(8,128)} %get-tuple-element.221) | copy-start | bytes 884740 | tf_op jit(solution)/shard_map/cond
  478.2 9.4 %copy-start.22 = (f32[3816,384]{1,0:T(8,128)S(1)}, f32[3816,384]{1,0:T(8,128)}, u32[]{:S(2)}) copy-start(f32[3816,384]{1,0:T(8,128)} %get-tuple-element.209) | copy-start | bytes 17584132 | tf_op jit(solution)/shard_map/cond
  480.7 6.9 %slice-start = ((s8[5861376]{0:T(1024)(128)(4,1)}), s8[4194304]{0:T(1024)(128)(4,1)S(1)}, s32[]{:S(2)}) async-start(s8[5861376]{0:T(1024)(128)(4,1)} %bitcast.276), calls=%async_computation.20 | async-start | bytes 8388608 | tf_op jit(solution)/shard_map/cond
  483.2 4.4 slice-start.1
  (16 other events, 32.2 us)

commit v3 on v2

--- a/solution.py
+++ b/solution.py
@@ -214,16 +214,35 @@
         self.live = []
 
 
+class Total:
+    def __init__(self, here, value, landed, send, recv):
+        self.here, self.value, self.landed, self.send, self.recv = here, value, landed, send, recv
+        self.order = ["t", "y"] + list(range(here.count))
+        self.last = len(self.order)
+
+    def stage(self, step):
+        if step > 0:
+            self.copy.wait()
+            self.value[...] += self.landed[step - 1]
+        if step < self.last:
+            self.copy = remote(
+                self.value, self.landed.at[step], self.send.at[step], self.recv.at[step],
+                self.here.across(self.order[step]),
+            )
+            self.copy.start()
+
+
 class Runner:
-    def __init__(self, jobs, lags):
-        self.jobs, self.lags, self.tick = jobs, lags, 0
-        self.length = max(job.last + lag for job, lag in zip(jobs, lags)) + 1
+    def __init__(self, jobs, lags, stride=1):
+        self.jobs, self.lags, self.stride, self.tick = jobs, lags, stride, 0
+        self.length = max(job.last * stride + lag for job, lag in zip(jobs, lags)) + 1
 
     def advance(self):
         if self.tick < self.length:
             for job, lag in zip(self.jobs, self.lags):
-                if 0 <= self.tick - lag <= job.last:
-                    job.stage(self.tick - lag)
+                since = self.tick - lag
+                if since % self.stride == 0 and 0 <= since // self.stride <= job.last:
+                    job.stage(since // self.stride)
             self.tick += 1
 
     def drain(self):
@@ -280,6 +299,10 @@
     flag[...] = jnp.max(heard[...].reshape((2 * n,) + flag.shape), axis=0)
 
 
+def heard_room(tok, n_dp):
+    return max(32, tok // n_dp)
+
+
 def exchange_lists(lists):
     n = lists.shape[0]
     dma = pltpu.SemaphoreType.DMA
@@ -312,7 +335,7 @@
     return centered * scale, scale
 
 
-def forward_body(room, kinds, pieces, *refs):
+def forward_body(room, kinds, pieces, stride, every, *refs):
     here = Place()
     n, count = here.n_dp, here.count
     table, heard, pos, norm_rows, cosine, sine, seg_row, seg_col = refs[:8]
@@ -349,8 +372,9 @@
             )
         )
         lags.append(lag)
-    runner = Runner(jobs, lags)
-    first_ticks = jobs[0].last + 1
+    first = Runner(jobs[:1], lags[:1])
+    runner = Runner(jobs[1:], lags[1:], stride)
+    first.advance()
     runner.advance()
     low_table[...] = table[...].astype(bf16)
     row_count = table.shape[0]
@@ -363,7 +387,7 @@
         copy.start()
         y_copies.append(copy)
 
-    for k in list(range(1, n)) + [0]:
+    for k in list(range(n - 1, 0, -1)) + [0]:
         column = jnp.transpose(heard[k])[:room, 0:1]
         hot = (lax.broadcasted_iota(jnp.int32, (room, row_count), 1) == column).astype(f32)
         found = mdot(hot.astype(bf16), low_table[...]).astype(bf16)
@@ -378,13 +402,17 @@
             )
             copy.start()
             out_copies.append(copy)
-            if k == n // 2:
+            if k % 2:
                 runner.advance()
-    for k in range(1, n):
-        out_copies[k - 1].wait_recv()
+        if k == n // 2:
+            first.advance()
+    first.advance()
+    for k in range(n - 1, 0, -1):
+        out_copies[n - 1 - k].wait_recv()
         pass_on(k)
-    while runner.tick < first_ticks:
-        runner.advance()
+        if k % 3 == 1:
+            runner.advance()
+    first.drain()
     for copy in out_copies:
         copy.wait_send()
     for copy in y_copies:
@@ -418,7 +446,8 @@
                     k_out[at, cols] = part
                 else:
                     v_out[at, cols] = part
-        runner.advance()
+        if i % every == every - 1:
+            runner.advance()
 
     lane = lax.broadcasted_iota(jnp.int32, (1, 128), 1)
     att_copies = []
@@ -451,14 +480,17 @@
                     )
                     copy.start()
                     att_copies.append(copy)
-            runner.advance()
+            if i % every == every - 1:
+                runner.advance()
     runner.drain()
     for copy in att_copies:
         copy.wait()
 
 
-def forward_pass(table, heard, pos, norm_rows, cosine, sine, seg_row, seg_col, shards, kinds, pieces):
-    n_dp, room = heard.shape[0], max(32, pos.shape[0] // heard.shape[0])
+def forward_pass(table, heard, pos, norm_rows, cosine, sine, seg_row, seg_col, shards, kinds, pieces,
+                 stride=2, every=1):
+    n_dp = heard.shape[0]
+    room = heard_room(pos.shape[0], n_dp)
     count = n_dp.bit_length() - 1
     halves = (2,) * (count + 1)
     tok = pos.shape[0]
@@ -496,7 +528,7 @@
         + [dma((len(pieces), steps)), dma((len(pieces), steps)), dma((len(pieces),))]
     )
     out = pl.pallas_call(
-        lambda *refs: forward_body(room, kinds, pieces, *refs),
+        lambda *refs: forward_body(room, kinds, pieces, stride, every, *refs),
         out_shape=outs,
         in_specs=[VM] * (8 + len(shards)),
         out_specs=specs,
@@ -516,7 +548,9 @@
     return out[:9], weights
 
 
-def make_scatters(here, grads, kinds, pieces, outs, held, landed, send, recv, loads):
+def make_scatters(
+    here, grads, kinds, pieces, outs, held, landed, send, recv, loads, stride=1
+):
     orders = scatter_orders(here.count)
     jobs, lags = [], []
     held, landed = list(held), list(landed)
@@ -533,7 +567,7 @@
             )
         )
         lags.append(lag)
-    return Runner(jobs, lags)
+    return Runner(jobs, lags, stride)
 
 
 def scatter_scratch(count, rows, pairs, pieces):
@@ -556,25 +590,174 @@
     return jnp.sum(jnp.sum(values * values, 0, keepdims=True), 1, keepdims=True)
 
 
-def backward_body(pieces, sizes, *refs):
+def store_blocks(ref, values, count, start):
+    rows, cols = ref.shape[-2], values.shape[1]
+    for number in range(2 ** (count + 1)):
+        at = tuple((number >> (count - j)) & 1 for j in range(count + 1))
+        ref[at + (slice(None), slice(start, start + cols))] = values[
+            number * rows : (number + 1) * rows, :
+        ].astype(bf16)
+
+
+def hidden_body(pieces, sizes, stride, *refs):
     here = Place()
+    count = here.count
+    (grad_pool, seg, hat_two, scale_two, norm_rows, low_one, hat_one, scale_one,
+     att_own, att_other, hidden_own, hidden_other) = refs[:12]
+    weights = refs[12:18]
+    residual, low_out, norms_out, wout_own, wout_other = refs[18:23]
+    later = refs[23:27]
+    out_down, squares = refs[27:29]
+    loaded, down, low_two, turned_one, turned_two, total = refs[29:35]
+    held = refs[35 : 35 + sizes[0]]
+    landed = refs[35 + sizes[0] : 35 + sizes[0] + sizes[1]]
+    wsem, send, recv, loads = refs[35 + sizes[0] + sizes[1] :]
+    half, width = low_one.shape
+    part = weights[0].shape[1] // 2
+    copies = {}
+
+    def load(c, j):
+        for w in range(3):
+            copies[c, j, w] = pltpu.make_async_copy(
+                weights[2 * w + j].at[:, pl.ds(c * part, part)], loaded.at[j * 3 + w],
+                wsem.at[(c * 2 + j) * 3 + w],
+            )
+            copies[c, j, w].start()
+
+    load(0, 0)
+    load(0, 1)
+    greet([here.across("t"), here.across("y")] + [here.across(j) for j in range(count)])
+    grads = [(down.at[0], down.at[1])]
+    runner = make_scatters(
+        here, grads, None, pieces, (out_down,), held, landed, send, recv, loads, stride
+    )
+    slots = grad_pool.shape[0]
+    hot = (lax.broadcasted_iota(jnp.int32, (half, slots), 1) == seg[...]).astype(f32)
+    grad_two = jnp.dot(hot, grad_pool[...], precision=highest, preferred_element_type=f32)
+    hat = hat_two[...]
+    grad_hat = grad_two * norm_rows[4:5, :]
+    first = jnp.mean(grad_hat, -1, keepdims=True)
+    second = jnp.mean(grad_hat * hat, -1, keepdims=True)
+    grad_sum = scale_two[...] * (grad_hat - first - hat * second)
+    low_two[...] = grad_sum.astype(bf16)
+    turned_two[...] = jnp.transpose(grad_sum).astype(bf16)
+    for c in range(2):
+        for j, hidden in enumerate((hidden_own, hidden_other)):
+            cols = slice(c * part, (c + 1) * part)
+            store_blocks(down.at[j], mdot(turned_two[...], hidden[:, cols]), count, c * part)
+        runner.advance()
+    norms_out[...] = jnp.zeros_like(norms_out)
+    norms_out[4:5, :] = jnp.sum(grad_two * hat, 0, keepdims=True)
+    norms_out[5:6, :] = jnp.sum(grad_two, 0, keepdims=True)
+    turned_one[...] = jnp.transpose(low_one[...].astype(f32)).astype(bf16)
+    total[...] = grad_sum
+    runner.advance()
+    for c in range(2):
+        for j in range(2):
+            number = j * 3
+            for w in range(3):
+                copies[c, j, w].wait()
+            gate = mdot(low_one[...], loaded[number])
+            up = mdot(low_one[...], loaded[number + 1])
+            share = 1.0 / (1.0 + jnp.exp(-gate))
+            grad_hidden = mdot(low_two[...], loaded[number + 2])
+            grad_up = (grad_hidden * (gate * share)).astype(bf16)
+            grad_gate = (
+                grad_hidden * up * (share * (1.0 + gate * (1.0 - share)))
+            ).astype(bf16)
+            runner.advance()
+            store_blocks(later[j], mdot(turned_one[...], grad_gate), count, c * part)
+            store_blocks(later[2 + j], mdot(turned_one[...], grad_up), count, c * part)
+            total[...] += tdot(grad_gate, loaded[number]) + tdot(grad_up, loaded[number + 1])
+            if c == 0:
+                load(1, j)
+            runner.advance()
+    hat = hat_one[...]
+    grad_one = total[...]
+    grad_hat = grad_one * norm_rows[2:3, :]
+    first = jnp.mean(grad_hat, -1, keepdims=True)
+    second = jnp.mean(grad_hat * hat, -1, keepdims=True)
+    grad_sum = scale_one[...] * (grad_hat - first - hat * second)
+    norms_out[2:3, :] = jnp.sum(grad_one * hat, 0, keepdims=True)
+    norms_out[3:4, :] = jnp.sum(grad_one, 0, keepdims=True)
+    residual[...] = grad_sum
+    low_out[...] = grad_sum.astype(bf16)
+    runner.advance()
+    turned_two[...] = jnp.transpose(grad_sum).astype(bf16)
+    wout_own[...] = mdot(turned_two[...], att_own[...]).astype(bf16)
+    runner.advance()
+    wout_other[...] = mdot(turned_two[...], att_other[...]).astype(bf16)
+    runner.drain()
+    squares[...] = jnp.broadcast_to(square_sum(out_down[...]), squares.shape)
+
+
+def hidden_back(grad_pool, seg, hat_two, scale_two, norm_rows, low_one, hat_one, scale_one, att,
+                hidden, w_gate, w_up, w_down, pieces, stride=1):
+    n_dp = lax.axis_size("dp")
+    count = n_dp.bit_length() - 1
+    half, width = low_one.shape
+    feats = att[0].shape[1]
+    cols = w_gate[0].shape[1]
+    rows = width // (2 * n_dp)
+    blocks = (2,) * (count + 1) + (rows, cols)
+    held, landed, sems = scatter_scratch(count, rows, [True], pieces)
+    vmem = pltpu.VMEM
+    return pl.pallas_call(
+        lambda *refs: hidden_body(pieces, (len(held), len(landed)), stride, *refs),
+        out_shape=[
+            sds((half, width), f32), sds((half, width), bf16), sds((8, width), f32),
+            sds((width, feats), bf16), sds((width, feats), bf16),
+        ] + [sds(blocks, bf16)] * 4 + [sds((rows, cols), f32), sds((8, 128), f32)],
+        in_specs=[VM] * 12 + [ANY] * 6,
+        out_specs=[VM] * 11,
+        scratch_shapes=[
+            vmem((6, width, cols // 2), bf16), vmem((2,) + blocks, bf16), vmem((half, width), bf16),
+            vmem((width, half), bf16), vmem((width, half), bf16), vmem((half, width), f32),
+        ] + held + landed + [pltpu.SemaphoreType.DMA((12,))] + sems,
+        compiler_params=params(6),
+        name="hidden",
+    )(grad_pool, seg, hat_two, scale_two, norm_rows, low_one, hat_one, scale_one, *att, *hidden,
+      *w_gate, *w_up, *w_down)
+
+
+def backward_body(room, pieces, late_pieces, sizes, stride, every, *refs):
+    here = Place()
+    n, count = here.n_dp, here.count
     (low, out_own, out_other, query, key, value, lse, cosine, sine, seg_row, seg_col, residual,
-     emb, norm_rows, w_qkv) = refs[:15]
-    grads = [(refs[15 + 2 * j], refs[16 + 2 * j]) for j in range(3)]
-    grad_proj, low_out, norms_out = refs[21:24]
-    outs = refs[24:27]
-    squares = refs[27]
-    kt, dq, dk, dv, grad_att, far_att, far_send, far_recv = refs[28:36]
-    at = 36
-    held = refs[at : at + sizes[0]]
-    landed = refs[at + sizes[0] : at + sizes[0] + sizes[1]]
-    asem, bsem, send, recv, loads = refs[at + sizes[0] + sizes[1] :]
+     emb, norm_rows, w_qkv, norms_in, before, inputs, pos, heard) = refs[:20]
+    grads = [(refs[20 + 2 * j], refs[21 + 2 * j]) for j in range(3)]
+    (table_out, norms_out, out_gate, out_up, out_proj, out_qkv, total_out) = refs[26:33]
+    (kt, dq, dk, dv, grad_att, far_att, far_send, far_recv, grad_proj, turned_in, grad_qkv,
+     low_out, norm_part, other, packed, mine, theirs, norms, parts, own_part) = refs[33:53]
+    at = 53
+    cuts = []
+    for size in sizes:
+        cuts.append(refs[at : at + size])
+        at += size
+    held, landed, late_held, late_landed = cuts
+    (asem, bsem, ysem, rsem, csem, nsem, tsem, send, recv, loads, late_send, late_recv,
+     late_loads) = refs[at:]
     tok, feats = query.shape
-    half = tok // 2
+    half, width = tok // 2, table_out.shape[1]
     groups = feats // 128
     block = 256
-    greet([here.across("t"), here.across("y")] + [here.across(j) for j in range(here.count)])
-    runner = make_scatters(here, grads, None, pieces, outs, held, landed, send, recv, loads)
+    peers = []
+    for rt in range(2):
+        for rd in range(n):
+            for rm in range(2):
+                if rt or rd or rm:
+                    where = {
+                        "tower": here.t + rt * (1 - 2 * here.t),
+                        "dp": here.mixed(rd),
+                        "mp": here.m + rm * (1 - 2 * here.m),
+                    }
+                    peers.append(((rt * n + rd) * 2 + rm, where))
+    me = (here.t * n + here.d) * 2 + here.m
+    greet([where for _, where in peers])
+    runner = make_scatters(
+        here, grads, None, pieces, (out_gate, out_up, out_proj), held, landed, send, recv, loads,
+        stride,
+    )
     runner.advance()
     att_copies = []
     far_att[...] = mdot(low[...], out_other[...]).astype(bf16)
@@ -587,6 +770,10 @@
         copy.start()
         att_copies.append(copy)
     grad_att[:half, :] = mdot(low[...], out_own[...]).astype(bf16)
+    for i in range(tok // block):
+        rows = slice(i * block, (i + 1) * block)
+        turned_in[:, rows] = jnp.transpose(inputs[rows, :].astype(f32)).astype(bf16)
+    runner.advance()
     lane = lax.broadcasted_iota(jnp.int32, (1, 128), 1)
     for g in range(groups):
         cols = slice(g * 128, (g + 1) * 128)
@@ -603,14 +790,14 @@
             turns = []
             add_k, add_v = None, None
             for h in range(2):
-                mine = (lane // HDIM) == h
+                inside = (lane // HDIM) == h
                 scores = jnp.where(same, tdot(keys[h], q_part), neg_large)
                 soft = jnp.exp(scores - lse[2 * g + h, :, rows])
                 grad_soft = tdot(values[h], g_part)
                 inner = jnp.sum(soft * grad_soft, 0, keepdims=True)
                 grad_scores = (soft * (grad_soft - inner)).astype(bf16)
-                part_v = mdot(soft.astype(bf16), jnp.where(mine, g_part, bf16(0)))
-                part_k = mdot(grad_scores, jnp.where(mine, q_part, bf16(0)))
+                part_v = mdot(soft.astype(bf16), jnp.where(inside, g_part, bf16(0)))
+                part_k = mdot(grad_scores, jnp.where(inside, q_part, bf16(0)))
                 add_v = part_v if h == 0 else add_v + part_v
                 add_k = part_k if h == 0 else add_k + part_k
                 turns.append(mdot(kt[h * HDIM : (h + 1) * HDIM, :], grad_scores))
@@ -621,7 +808,7 @@
             else:
                 dv[...] += add_v
                 dk[...] += add_k
-            if i % 2:
+            if i % every == every - 1:
                 runner.advance()
         cos, sin = cosine[...], sine[...]
         for c, grad in ((0, dq), (1, dk)):
@@ -642,10 +829,26 @@
         )
         copy.start()
         far_copies.append(copy)
-    norms_out[...] = jnp.zeros_like(norms_out)
+    late = make_scatters(
+        here, [(grad_qkv, None)], None, late_pieces, (out_qkv,), late_held, late_landed, late_send,
+        late_recv, late_loads, 1,
+    )
+    jobs = late.jobs
+    step = feats if grad_qkv.shape[-2] % 16 == 0 else 128
+    for start in range(0, 3 * feats, step):
+        cols = slice(start, start + step)
+        store_blocks(grad_qkv, mdot(turned_in[...], grad_proj[:, cols]), count, start)
+    late.advance()
+    runner.advance()
+    theirs_at = pl.ds(pl.multiple_of((1 - here.m) * width, 128), width)
+    mine_at = pl.ds(pl.multiple_of(here.m * width, 128), width)
+    norm_part[...] = norms_in[...]
+    swaps = []
     for i in range(half // block):
         rows = slice(i * block, (i + 1) * block)
         near = residual[rows, :] + tdot(grad_proj[rows, :], w_qkv[...])
+        if i == 0:
+            runner.advance()
         far_copies[i].wait()
         near = near + far_recv[rows, :].astype(f32)
         hat, scale = norm_parts(emb[rows, :].astype(f32))
@@ -653,96 +856,24 @@
         first = jnp.mean(grad_hat, -1, keepdims=True)
         second = jnp.mean(grad_hat * hat, -1, keepdims=True)
         low_out[rows, :] = (scale * (grad_hat - first - hat * second)).astype(bf16)
-        norms_out[0:1, :] += jnp.sum(near * hat, 0, keepdims=True)
-        norms_out[1:2, :] += jnp.sum(near, 0, keepdims=True)
-        runner.advance()
-    runner.drain()
-    total = square_sum(outs[0][...]) + square_sum(outs[1][...]) + square_sum(outs[2][...])
-    squares[...] = jnp.broadcast_to(total, squares.shape)
-
-
-def blocks_of(grad, n_dp):
-    count = n_dp.bit_length() - 1
-    rows = grad.shape[0] // (2 * n_dp)
-    return grad.reshape((2,) * (count + 1) + (rows, grad.shape[1]))
-
-
-def backward_pass(low, w_out, query, key, value, lse, cosine, sine, seg_row, seg_col, residual,
-                  emb, norm_rows, w_qkv, grads, pieces):
-    n_dp = lax.axis_size("dp")
-    count = n_dp.bit_length() - 1
-    tok, feats = query.shape
-    half, width = low.shape
-    rows, cols = grads[0][0].shape[0] // (2 * n_dp), grads[0][0].shape[1]
-    held, landed, sems = scatter_scratch(count, rows, [True] * 3, pieces)
-    flat = [blocks_of(g, n_dp) for pair in grads for g in pair]
-    dma = pltpu.SemaphoreType.DMA
-    vmem = pltpu.VMEM
-    return pl.pallas_call(
-        lambda *refs: backward_body(pieces, (len(held), len(landed)), *refs),
-        out_shape=[
-            sds((tok, 3 * feats), bf16), sds((half, width), bf16), sds((8, width), f32),
-            sds((rows, cols), f32), sds((rows, cols), f32), sds((rows, cols), f32),
-            sds((8, 128), f32),
-        ],
-        in_specs=[VM] * 15 + [ANY] * 6,
-        out_specs=[VM] * 7,
-        scratch_shapes=[
-            vmem((128, tok), bf16), vmem((tok, 128), f32), vmem((tok, 128), f32),
-            vmem((tok, 128), f32), vmem((tok, feats), bf16), vmem((half, feats), bf16),
-            vmem((half, width), bf16), vmem((half, width), bf16),
-        ] + held + landed + [dma((2, feats // 128)), dma((2, max(1, half // 256)))] + sems,
-        compiler_params=params(4),
-        name="backward",
-    )(low, w_out[0], w_out[1], query, key, value, lse, cosine, sine, seg_row, seg_col, residual,
-      emb, norm_rows, w_qkv, *flat)
-
-
-def spread_body(room, pieces, sizes, *refs):
-    here = Place()
-    n = here.n_dp
-    grad, pos, heard, norm_grad, squares = refs[:5]
-    grads = [(refs[5], None), (refs[6], refs[7])]
-    out, norms_out, out_qkv, out_proj, total_out = refs[8:13]
-    other, packed, mine, theirs, norms, parts, own_part, gathered = refs[13:21]
-    at = 21
-    held = refs[at : at + sizes[0]]
-    landed = refs[at + sizes[0] : at + sizes[0] + sizes[1]]
-    ysem, rsem, csem, nsem, tsem, send, recv, loads = refs[at + sizes[0] + sizes[1] :]
-    width = grad.shape[1] // 2
-    slots = n * room
-    peers = []
-    for rt in range(2):
-        for rd in range(n):
-            for rm in range(2):
-                if rt or rd or rm:
-                    where = {
-                        "tower": here.t + rt * (1 - 2 * here.t),
-                        "dp": here.mixed(rd),
-                        "mp": here.m + rm * (1 - 2 * here.m),
-                    }
-                    peers.append(((rt * n + rd) * 2 + rm, where))
-    greet([where for _, where in peers])
-    theirs_at = pl.ds(pl.multiple_of((1 - here.m) * width, 128), width)
-    mine_at = pl.ds(pl.multiple_of(here.m * width, 128), width)
-    swapped = remote(grad.at[:, theirs_at], other, ysem.at[0], ysem.at[1], here.across("y"))
-    swapped.start()
-    runner = make_scatters(
-        here, grads, None, pieces, (out_qkv, out_proj), held, landed, send, recv, loads
-    )
+        copy = remote(
+            low_out.at[rows, theirs_at], other.at[rows, :], ysem.at[0, i], ysem.at[1, i],
+            here.across("y"),
+        )
+        copy.start()
+        swaps.append(copy)
+        norm_part[0:1, :] += jnp.sum(near * hat, 0, keepdims=True)
+        norm_part[1:2, :] += jnp.sum(near, 0, keepdims=True)
+    jobs.append(Total(here, norm_part, norms, nsem.at[0], nsem.at[1]))
+    late.lags.append(late.tick)
+    late.length = max(late.length, late.tick + jobs[-1].last + 1)
+    late.advance()
     runner.advance()
-    me = (here.t * n + here.d) * 2 + here.m
-    norm_copies = []
-    for rel, where in peers:
-        copy = remote(norm_grad, norms.at[me], nsem.at[0, rel], nsem.at[1, rel], where)
-        copy.start()
-        norm_copies.append(copy)
-    norms[me] = norm_grad[...]
-    runner.advance()
-    swapped.wait()
-    both = jnp.concatenate([grad[:, mine_at], other[...]], 0)
+    for copy in swaps:
+        copy.wait()
+    both = jnp.concatenate([low_out[:, mine_at], other[...]], 0)
     copies = []
-    for k in list(range(1, n)) + [0]:
+    for k in list(range(n - 1, 0, -1)) + [0]:
         hot = (
             lax.broadcasted_iota(jnp.int32, (room, pos.shape[1]), 0) + k * room == pos[...]
         ).astype(f32)
@@ -757,51 +888,49 @@
         copy.start()
         copies.append(copy)
     passed = [copies.pop()]
+    late.advance()
     runner.advance()
-    for k in range(1, n):
-        copies[k - 1].wait_recv()
+    for k in range(n - 1, 0, -1):
+        copies[n - 1 - k].wait_recv()
         copy = remote(mine.at[k], theirs.at[k], csem.at[0, k], csem.at[1, k], here.across("t"))
         copy.start()
         passed.append(copy)
+        if k == n // 2:
+            late.advance()
+            runner.advance()
+    late.advance()
     runner.advance()
     for copy in copies:
         copy.wait_send()
     for copy in passed:
         copy.wait()
-    row_count = out.shape[0]
-    block = row_count
-    for size in range(512, 255, -8):
-        if row_count % size == 0:
-            block = size
-            break
-    gathered[0:slots, :] = mine[...].reshape(slots, width)
-    gathered[slots:, :] = theirs[...].reshape(slots, width)
+    slots = n * room
+    row_count = table_out.shape[0]
+    size = 424 * 1024 // max(slots, 1024) // 8 * 8
     own_part[...] = jnp.zeros_like(own_part)
-
-    @pl.loop(0, row_count // block)
-    def _(i):
-        rows = pl.ds(pl.multiple_of(i * block, 8) if block != row_count else 0, block)
-        base = lax.broadcasted_iota(jnp.int32, (block, room), 0) + i * block
-        hots = []
-        for source in range(2):
-            for k in range(n):
-                hots.append((base == heard[source, k, 0:1, :room]).astype(f32).astype(bf16))
-        found = mdot(jnp.concatenate(hots, 1), gathered[...])
-        out[rows, :] = found
+    for part in range(-(-row_count // size)):
+        rows = slice(part * size, min((part + 1) * size, row_count))
+        block_rows = rows.stop - rows.start
+        base = lax.broadcasted_iota(jnp.int32, (block_rows, slots), 0) + part * size
+        found = 0.0
+        for source, sums in ((0, mine), (1, theirs)):
+            hot = (base == heard[source]).astype(f32).astype(bf16)
+            found = found + mdot(hot, sums[...].reshape(slots, width))
+        table_out[rows, :] = found
         own_part[0:1, :] += jnp.sum(found * found, 0, keepdims=True)
-
+        if part % 2:
+            late.advance()
+            runner.advance()
+    late.drain()
     runner.drain()
-    for copy in norm_copies:
-        copy.wait()
-    total = norms[0]
-    for j in range(1, 4 * n):
-        total = total + norms[j]
-    norms_out[...] = total
+    norms_out[...] = norm_part[...]
     local_sq = (
-        squares[0:1, 0:1]
+        before[0:1, 0:1]
         + 0.5 * jnp.sum(own_part[...], 1, keepdims=True)[0:1]
         + square_sum(out_qkv[...])
         + square_sum(out_proj[...])
+        + square_sum(out_gate[...])
+        + square_sum(out_up[...])
     )
     parts[me] = jnp.broadcast_to(local_sq, parts.shape[1:])
     copies = []
@@ -814,39 +943,55 @@
     total_out[...] = jnp.sum(parts[...], 0) + square_sum(norms_out[...])
 
 
-def spread_pass(grad, pos_row, heard, norm_grad, squares, grad_qkv, grad_out, row_count, pieces):
+def blocks_of(grad, n_dp):
+    count = n_dp.bit_length() - 1
+    rows = grad.shape[0] // (2 * n_dp)
+    return grad.reshape((2,) * (count + 1) + (rows, grad.shape[1]))
+
+
+def backward_pass(low, w_out, query, key, value, lse, cosine, sine, seg_row, seg_col, residual,
+                  emb, norm_rows, w_qkv, norms, before, inputs, pos_row, heard, grads, grad_out,
+                  row_count, pieces, late_pieces, stride=2, every=1):
     n_dp = lax.axis_size("dp")
     count = n_dp.bit_length() - 1
-    half, width = grad.shape[0], grad.shape[1] // 2
-    room = max(32, 2 * half // n_dp)
-    rows = grad_qkv.shape[0] // (2 * n_dp)
-    held, landed, sems = scatter_scratch(count, rows, [False, True], pieces)
-    flat = [blocks_of(g, n_dp) for g in (grad_qkv, grad_out[0], grad_out[1])]
+    tok, feats = query.shape
+    half, width = low.shape
+    rows, cols = grads[0].shape[-2:]
+    room = heard_room(tok, n_dp)
+    held, landed, sems = scatter_scratch(count, rows, [True] * 3, pieces)
+    late_held, late_landed, late_sems = scatter_scratch(count, rows, [False], late_pieces)
+    flat = list(grads) + [blocks_of(g, n_dp) for g in grad_out]
     dma = pltpu.SemaphoreType.DMA
     vmem = pltpu.VMEM
+    sizes = (len(held), len(landed), len(late_held), len(late_landed))
+    steps = max(1, half // 256)
+    part = width // 2
     return pl.pallas_call(
-        lambda *refs: spread_body(room, pieces, (len(held), len(landed)), *refs),
+        lambda *refs: backward_body(room, pieces, late_pieces, sizes, stride, every, *refs),
         out_shape=[
-            sds((row_count, width), f32), sds(norm_grad.shape, f32),
-            sds((rows, grad_qkv.shape[1]), f32), sds((rows, grad_out[0].shape[1]), f32),
-            sds((8, 128), f32),
+            sds((row_count, part), f32), sds((8, width), f32),
+            sds((rows, cols), f32), sds((rows, cols), f32), sds((rows, feats), f32),
+            sds((rows, 3 * feats), f32), sds((8, 128), f32),
         ],
-        in_specs=[VM] * 5 + [ANY] * 3,
-        out_specs=[VM] * 5,
+        in_specs=[VM] * 20 + [ANY] * 6,
+        out_specs=[VM] * 7,
         scratch_shapes=[
-            vmem((half, width), bf16),
-            vmem((n_dp, room, width), bf16),
-            vmem((n_dp, room, width), bf16),
-            vmem((n_dp, room, width), bf16),
-            vmem((4 * n_dp,) + norm_grad.shape, f32),
-            vmem((4 * n_dp, 8, 128), f32),
-            vmem((8, width), f32),
-            vmem((2 * n_dp * room, width), bf16),
-        ] + held + landed
-        + [dma((2,)), dma((2, n_dp)), dma((2, n_dp)), dma((2, 4 * n_dp)), dma((2, 4 * n_dp))] + sems,
-        compiler_params=params(5),
-        name="spread",
-    )(grad, pos_row, heard, norm_grad, squares, *flat)
+            vmem((128, tok), bf16), vmem((tok, 128), f32), vmem((tok, 128), f32),
+            vmem((tok, 128), f32), vmem((tok, feats), bf16), vmem((half, feats), bf16),
+            vmem((half, width), bf16), vmem((half, width), bf16),
+            vmem((tok, 3 * feats), bf16), vmem((width, tok), bf16),
+            vmem((2,) * (count + 1) + (rows, 3 * feats), bf16),
+            vmem((half, width), bf16), vmem((8, width), f32), vmem((half, part), bf16),
+            vmem((n_dp, room, part), bf16), vmem((n_dp, room, part), bf16),
+            vmem((n_dp, room, part), bf16), vmem((count + 2, 8, width), f32),
+            vmem((4 * n_dp, 8, 128), f32), vmem((8, part), f32),
+        ] + held + landed + late_held + late_landed
+        + [dma((2, feats // 128)), dma((2, steps)), dma((2, steps)), dma((2, n_dp)),
+           dma((2, n_dp)), dma((2, count + 2)), dma((2, 4 * n_dp))] + sems + late_sems,
+        compiler_params=params(4, 60),
+        name="backward",
+    )(low, w_out[0], w_out[1], query, key, value, lse, cosine, sine, seg_row, seg_col, residual,
+      emb, norm_rows, w_qkv, norms, before, inputs, pos_row, heard, *flat)
 
 
 def loss_body(part, counts, doc_ok, query_ok, target, scale, grad_out, stats, other, low_all, turn,
@@ -1437,16 +1582,20 @@
         attn_in.reshape(attn_in.shape[0], -1), attn_out, ffn_in[:, 0], ffn_in[:, 1], ffn_out,
     )
     kinds = ("plain", "late", "late", "late", "late")
-    gather_pieces = [(0, "plain", 0, 3 * feats, 0), (1, "late", 0, feats, 1)]
+    gather_pieces = [(0, "plain", 0, 3 * feats, 0)]
+    quarter = ff // 4
     for turn, which in enumerate((2, 3, 4)):
-        gather_pieces.append((which, "late", 0, part_ff, 1 + turn))
-        gather_pieces.append((which, "early", part_ff, part_ff, 1 + turn))
+        for c in range(4):
+            kind = ("late", "early")[c % 2]
+            gather_pieces.append((which, kind, c * quarter, quarter, 4 * turn + c))
+    gather_pieces.append((1, "late", 0, feats, 6))
     places = (jnp.arange(tok, dtype=jnp.int32) + model_idx * half) % tok
     pos_rel = jnp.where(model_idx == 0, pos, jnp.concatenate([pos[half:], pos[:half]]))
     lengths_row = seq_lengths[tower_idx, data_idx]
     segment, positions = layout(lengths_row, places, slot_count)
     cosine, sine = rotary_tables(positions)
     seg_row, seg_col = segment[None, :], segment[:, None]
+    named = heard[:, :, 0, : heard_room(tok, heard.shape[1])].reshape(2, 1, -1)
     kept, weights = forward_pass(
         embedding, heard[0], pos_rel[:, None], norm_params[0:2], cosine, sine, seg_row, seg_col,
         shards, kinds, gather_pieces,
@@ -1476,44 +1625,24 @@
     )
     loss_sum, query_count, scale_grad = stats[0, 0], stats[1, 0], stats[2, 0]
 
-    grad_two = jnp.dot(member.T, grad_pool, precision=highest)
-    grad_sum_two, gain_two, bias_two = norm_back(grad_two, hat_two, scale_two, norm_params[4])
-    ffn_low = grad_sum_two.astype(bf16)
-
     def weight_grad(left, right):
         return jnp.einsum("td,tf->df", left, right, preferred_element_type=f32).astype(bf16)
 
-    grad_down, grad_gate, grad_up = [], [], []
-    grad_stream_one = grad_sum_two
-    for j in range(2):
-        grad_down.append(weight_grad(ffn_low, hidden[j]))
-        grad_hidden = mdot(ffn_low, w_down[j])
-        d_gate, d_up = jax.vjp(glu, gates[j], ups[j])[1](grad_hidden)
-        d_gate, d_up = d_gate.astype(bf16), d_up.astype(bf16)
-        grad_gate.append(weight_grad(input_one, d_gate))
-        grad_up.append(weight_grad(input_one, d_up))
-        grad_stream_one = grad_stream_one + tdot(d_gate, w_gate[j]) + tdot(d_up, w_up[j])
-    grad_sum_one, gain_one, bias_one = norm_back(
-        grad_stream_one, hat_one, scale_one, norm_params[2]
-    )
-    attn_low = grad_sum_one.astype(bf16)
-    grad_out = [weight_grad(attn_low, att[j]) for j in range(2)]
-    pieces = []
-    for turn, which in enumerate((2, 0, 1)):
-        pieces.append((which, "early", 0, part_ff, turn))
-        pieces.append((which, "late", part_ff, part_ff, turn))
-    grad_proj, embed_low, zero_norms, r_gate, r_up, r_down, squares = backward_pass(
+    pieces = [(0, ("early", "late")[c % 2], c * quarter, quarter, c) for c in range(4)]
+    out = hidden_back(
+        grad_pool, seg_col[:half], hat_two, scale_two, norm_params, input_one, hat_one, scale_one,
+        att, hidden, w_gate, w_up, w_down, pieces, 2,
+    )
+    grad_sum_one, attn_low, norms = out[:3]
+    grad_out, later, r_down, squares = out[3:5], out[5:9], out[9], out[10]
+    pieces = [
+        (c // 4, ("early", "late")[c % 2], (c % 4) * quarter, quarter, c) for c in range(8)
+    ] + [(2, "late", 0, feats, 8)]
+    late_pieces = [(0, "plain", 0, 2 * feats, 0), (0, "plain", 2 * feats, feats, 0)]
+    embed_grad, norm_sum, r_gate, r_up, r_out, r_qkv, total = backward_pass(
         attn_low, w_out, query, key, value, lse, cosine, sine, seg_row, seg_col, grad_sum_one,
-        emb, norm_params[0:2], w_qkv, (grad_gate, grad_up, grad_down), pieces,
-    )
-    grad_qkv = weight_grad(input_zero, grad_proj)
-    norm_part = jnp.concatenate(
-        [zero_norms[0:2], jnp.stack([gain_one, bias_one, gain_two, bias_two]), zero_norms[2:4]]
-    )
-    pieces = [(0, "plain", 0, 2 * feats, 0), (0, "plain", 2 * feats, feats, 1), (1, "late", 0, feats, 1)]
-    embed_grad, norm_sum, r_qkv, r_out, total = spread_pass(
-        embed_low, pos_rel[None, :], heard, norm_part, squares, grad_qkv, grad_out, row_count,
-        pieces,
+        emb, norm_params[0:2], w_qkv, norms, squares, input_zero, pos_rel[None, :], named,
+        later, grad_out, row_count, pieces, late_pieces,
     )
     norm_grad = norm_sum[:6]
     r_qkv = r_qkv.reshape(attn_in.shape)
@@ -1540,7 +1669,7 @@
 def local(*args):
     token_ids, embedding = args[0], args[3]
     n_dp = lax.axis_size("dp")
-    room = max(32, token_ids.shape[1] // n_dp)
+    room = heard_room(token_ids.shape[1], n_dp)
     pos, lists = name_rows(
         token_ids[0], lax.axis_index("dp"), n_dp, embedding.shape[0], room
     )

time: 526 us -> 473 us (0.90)
  matrix products: 56 us -> 14.2 us
  Pallas kernels: 365 us -> 357 us
    dot_general x10 -> x0, matrix products: 27.2 us -> none  [the longest x9 24.9 us: weight_grad(): jnp.einsum('td,tf->df', left, right, preferred_element_type=f32)]
    pallas_call x3, Pallas kernels: 337 us -> 327 us  [the longest x1 142 us: backward_pass(): pl.pallas_call(lambda *refs: backward_body(room, pieces, late_pieces, siz...]
    dot_general x6 -> x4, matrix products: 14.1 us -> 6.11 us  [mdot(): return jnp.dot(lhs, rhs, preferred_element_type=f32)]
    dot_general x8 -> x4, matrix products: 13.2 us -> 6.77 us  [tdot(): lax.dot_general(lhs, rhs, (((1,), (1,)), ((), ())), preferred_element_typ...]
where the time goes in v3:
time: 473 us; the launch traced here: 467 us
  Pallas kernels  357 us (75%)
  other arithmetic  30.2 us (6%)
  local copies, waits for them, and re-layouts  29.8 us (6%)
  between operations  20.2 us (4%)
  loops' own time  15.4 us (3%)
  matrix products  14.2 us (3%)
    pallas_call x1, Pallas kernels, backward_pass(): pl.pallas_call(lambda *refs: backward_body(room, pieces, late_pieces, siz...  142 us
    pallas_call x1, Pallas kernels, forward_pass(): pl.pallas_call(lambda *refs: forward_body(room, kinds, pieces, stride, ev...  135 us
    pallas_call x1, Pallas kernels, hidden_back(): pl.pallas_call(lambda *refs: hidden_body(pieces, (len(held), len(landed))...  50.3 us
    pallas_call x1, Pallas kernels, loss_step(): pl.pallas_call(loss_body, out_shape=[sds(part.shape, f32), sds((8, 128),...  20 us
    sub x6, other arithmetic, adamw(): weight_in - rate * (first_hat / (jnp.sqrt(second_hat) + adam_eps) + decay...  17 us
    another operation x1, loops' own time, local(): lax.cond(flag[1, 0] > 0, lambda values: plain_step(*values), lambda value...  15.4 us
    pallas_call x1, Pallas kernels, exchange_lists(): pl.pallas_call(lists_body, out_shape=[sds((2,) + lists.shape, jnp.int32),...  9.92 us

profile of v3, /device:TPU:1, one launch (start us, length us, event | category | flops | bytes accessed | tf_op | source)
XLA Modules:
  0.0 467.1 jit_solution(11252124183199690126)
XLA Ops:
  7.2 1.5 select_reduce_fusion.5
  10.2 1.5 convert_reduce_fusion.4
  14.6 9.9 %lists.1 = (s32[2,8,8,128]{3,2,1,0:T(8,128)S(1)}, s32[8,128]{1,0:T(8,128)}) custom-call(s32[8,8,128]{2,1,0:T(8,128)} %concatenate.47.lists), custom_call_target="tpu_custom_call" | custom-call | tf_op jit(solution)/shard_map/lists/pallas_call | solution.py:309
  24.6 1.2 slice.128
  26.4 428.1 %conditional.1 = (f32[3816,384]{1,0:T(8,128)}, f32[3816,384]{1,0:T(8,128)}, f32[3816,384]{1,0:T(8,128)}, f32[48,3,384]{2,0,1:T(8,128)}, f32[48,3,384]{2,0,1:T(8,...) conditional(s32[]{:T(128)} %bitcast.71, ...), branch_computations={%region_4.12_spmd, %region_12.69_spmd} | conditional | flops 32450023424 | bytes 1183283200 | solution.py:1677
  29.2 1.3 slice.92.refs_3_.refs_13_
  35.8 1.4 reshape.772.target
  37.3 1.6 copy.287
  42.1 2.9 fusion.45
  46.0 135.0 %forward.1 = (bf16[512,768]{1,0:T(8,128)(2,1)}, f32[512,768]{1,0:T(8,128)}, bf16[1024,768]{1,0:T(8,128)(2,1)}, bf16[1024,384]{1,0:T(8,128)(2,1)}, bf16[1024,384]...) custom-call(f32[3816,384]{1,0:T(8,128)} %get-tuple-element.174.refs_, ...), custom_call_target="tpu_custom_call" | custom-call | tf_op jit(solution)/shard_map/cond/branch_0_fun/forward/pallas_call | solution.py:530
  181.0 1.9 fusion.189
  182.9 1.9 fusion.185
  186.3 2.1 copy-done.44
  188.5 1.4 fusion.192
  190.2 1.6 fusion.36.refs_11_
  191.8 1.4 fusion.190
  194.1 1.8 fusion.35.refs_10_
  195.9 1.4 fusion.191
  198.1 1.6 fusion.186
  200.2 1.4 fusion.37.part
  201.6 20.0 %loss.1 = (f32[16,768]{1,0:T(8,128)}, f32[8,128]{1,0:T(8,128)}) custom-call(f32[16,768]{1,0:T(8,128)} %fusion.37.part, f32[16,1]{1,0:T(8,128)} %maximum_convert_fusion.counts, f32[1,128]{1,0:T(1,128)} %reshape.728.doc_ok, f32[128,1]{1,0:T(8,128)} %reshape.771.query_ok, s32[128,1]{1,0:T(8,128)} %reshape.772.target, f32[1,1]{1,0:T(1,128)} %bitcast.15.scale), custom_call_target="tpu_custom_call" | custom-call | tf_op jit(solution)/shard_map/cond/branch_0_fun/loss/pallas_call | solution.py:1065
  221.6 1.3 fusion.183
  225.1 50.3 %hidden.1 = (f32[512,768]{1,0:T(8,128)}, bf16[512,768]{1,0:T(8,128)(2,1)}, f32[8,768]{1,0:T(8,128)}, bf16[768,384]{1,0:T(8,128)(2,1)}, bf16[768,384]{1,0:T(8,128...) custom-call(f32[16,768]{1,0:T(8,128)} %get-tuple-element.197.refs_0_, ...), custom_call_target="tpu_custom_call" | custom-call | tf_op jit(solution)/shard_map/cond/branch_0_fun/hidden/pallas_call | solution.py:705
  275.4 142.1 %backward.1 = (f32[3816,384]{1,0:T(8,128)}, f32[8,768]{1,0:T(8,128)}, f32[48,1536]{1,0:T(8,128)}, f32[48,1536]{1,0:T(8,128)}, f32[48,384]{1,0:T(8,128)}, /*index=5*/f32[48,1152]{1,0:T(8,128)}, f32[8,128]{1,0:T(8,128)}) custom-call(bf16[512,768]{1,0:T(8,128)(2,1)} %get-tuple-element.198.refs_0_, bf16[768,384]{1,0:T(8,128)(2,1)} %bitcast.258, ...), custom_call_target="tpu_custom_call" | custom-call | tf_op jit(solution)/shard_map/cond/branch_0_fun/backward/pallas_call | solution.py:969
  417.5 1.2 slice.103
  420.9 1.4 multiply_subtract_fusion.4
  423.3 1.8 multiply_subtract_fusion.3
  425.1 1.8 copy_subtract_fusion
  430.0 1.3 copy.242
  431.3 1.3 copy.244
  432.5 1.3 copy.246
  433.8 11.2 %multiply_subtract_fusion = (f32[3816,384]{1,0:T(8,128)}, f32[3816,384]{1,0:T(8,128)}, f32[3816,384]{1,0:T(8,128)}) fusion(f32[3816,384]{1,0:T(8,128)S(1)} %bitcast.244, f32[3816,384]{1,0:T(8,128)S(1)} %copy-done.24, f32[]{:T(128)} %bitcast.24, f32[3816,384]{1,0:T(8,128)} %get-tuple-element.175, f32[3816,384]{1,0:T(8,128)} %get-tuple-element.218), kind=kLoop, calls=%fused_computation.51 | loop fusion | flops 23445504 | bytes 41029636 | tf_op jit(solution)/shard_map/cond/branch_0_fun/sub | solution.py:1119
  (119 shorter events, 23.7 us)
Async XLA Ops:
  26.4 18.6 %copy-start.16 = (f32[48,2,1536]{2,1,0:T(2,128)S(1)}, f32[48,2,1536]{2,1,0:T(2,128)}, u32[]{:S(2)}) copy-start(f32[48,2,1536]{2,1,0:T(2,128)} %get-tuple-element.733) | copy-start | bytes 1769476 | tf_op jit(solution)/shard_map/cond
  29.2 16.8 %copy-start.115 = (s32[1024]{0:T(1024)}, s32[1024]{0:T(1024)S(1)}, u32[]{:S(2)}) copy-start(s32[1024]{0:T(1024)S(1)} %add_select_fusion.1) | copy-start | bytes 12292 | tf_op jit(solution)/shard_map/cond
  31.5 14.5 %copy-start.97 = (s32[1024]{0:T(1024)}, s32[1024]{0:T(1024)S(1)}, u32[]{:S(2)}) copy-start(s32[1024]{0:T(1024)S(1)} %convert_reduce_fusion) | copy-start | bytes 12292 | tf_op jit(solution)/shard_map/cond
  35.8 10.1 %copy-start.25 = (f32[48,1536]{1,0:T(8,128)S(1)}, f32[48,1536]{1,0:T(8,128)}, u32[]{:S(2)}) copy-start(f32[48,1536]{1,0:T(8,128)} %get-tuple-element.183.refs_12_) | copy-start | bytes 884740 | tf_op jit(solution)/shard_map/cond
  35.8 10.1 %copy-start.52 = (f32[48,384]{1,0:T(8,128)S(1)}, f32[48,384]{1,0:T(8,128)}, u32[]{:S(2)}) copy-start(f32[48,384]{1,0:T(8,128)} %get-tuple-element.181.refs_9_) | copy-start | bytes 221188 | tf_op jit(solution)/shard_map/cond
  181.0 1.9 copy-start.49
  186.0 2.5 copy-start.44
  186.3 6.9 %copy-start.34 = (bf16[512,768]{1,0:T(8,128)(2,1)}, bf16[512,768]{1,0:T(8,128)(2,1)S(1)}, u32[]{:S(2)}) copy-start(bf16[512,768]{1,0:T(8,128)(2,1)S(1)} %get-tuple-element.888.refs_5_) | copy-start | bytes 2359300 | tf_op jit(solution)/shard_map/cond
  186.3 11.0 %copy-start.23 = (f32[512,768]{1,0:T(8,128)}, f32[512,768]{1,0:T(8,128)S(1)}, u32[]{:S(2)}) copy-start(f32[512,768]{1,0:T(8,128)S(1)} %get-tuple-element.889.refs_6_) | copy-start | bytes 4718596 | tf_op jit(solution)/shard_map/cond
  188.5 1.7 copy-start.46
  190.2 1.7 copy-start.43
  191.8 5.5 %copy-start.50 = (bf16[512,1536]{1,0:T(8,128)(2,1)}, bf16[512,1536]{1,0:T(8,128)(2,1)S(1)}, u32[]{:S(2)}) copy-start(bf16[512,1536]{1,0:T(8,128)(2,1)S(1)} %fusion.36.refs_11_) | copy-start | bytes 4718596 | tf_op jit(solution)/shard_map/cond
  191.8 2.2 copy-start.45
  194.1 1.8 copy-start.47
  195.8 1.5 copy-start.51
  195.9 2.2 copy-start.48
  199.7 25.4 %copy-start.73 = (f32[6,768]{1,0:T(8,128)S(1)}, f32[6,768]{1,0:T(8,128)}, u32[]{:S(2)}) copy-start(f32[6,768]{1,0:T(8,128)} %get-tuple-element.179.refs_4_) | copy-start | bytes 55300 | tf_op jit(solution)/shard_map/cond
  200.2 24.9 %copy-start.14 = (f32[512,768]{1,0:T(8,128)}, f32[512,768]{1,0:T(8,128)S(1)}, u32[]{:S(2)}) copy-start(f32[512,768]{1,0:T(8,128)S(1)} %subtract_multiply_fusion.refs_2_) | copy-start | bytes 4718596 | tf_op jit(solution)/shard_map/cond
  275.3 145.5 %copy-start.100 = (f32[6,768]{1,0:T(8,128)S(1)}, f32[6,768]{1,0:T(8,128)}, u32[]{:S(2)}) copy-start(f32[6,768]{1,0:T(8,128)} %get-tuple-element.232) | copy-start | bytes 55300 | tf_op jit(solution)/shard_map/cond
  275.3 145.5 %copy-start.102 = (f32[6,768]{1,0:T(8,128)S(1)}, f32[6,768]{1,0:T(8,128)}, u32[]{:S(2)}) copy-start(f32[6,768]{1,0:T(8,128)} %get-tuple-element.234) | copy-start | bytes 55300 | tf_op jit(solution)/shard_map/cond
  275.4 149.8 %copy-start.28 = (f32[48,3,384]{2,0,1:T(8,128)S(1)}, f32[48,3,384]{2,0,1:T(8,128)}, u32[]{:S(2)}) copy-start(f32[48,3,384]{2,0,1:T(8,128)} %get-tuple-element.732) | copy-start | bytes 663556 | tf_op jit(solution)/shard_map/cond
  417.4 11.6 %copy-start.55 = (f32[48,1536]{1,0:T(8,128)S(1)}, f32[48,1536]{1,0:T(8,128)}, u32[]{:S(2)}) copy-start(f32[48,1536]{1,0:T(8,128)} %get-tuple-element.229) | copy-start | bytes 884740 | tf_op jit(solution)/shard_map/cond
  417.4 11.6 %copy-start.57 = (f32[48,1536]{1,0:T(8,128)S(1)}, f32[48,1536]{1,0:T(8,128)}, u32[]{:S(2)}) copy-start(f32[48,1536]{1,0:T(8,128)} %get-tuple-element.231) | copy-start | bytes 884740 | tf_op jit(solution)/shard_map/cond
  423.2 6.1 %copy-start.35 = (f32[48,2,1536]{2,1,0:T(2,128)S(1)}, f32[48,2,1536]{2,1,0:T(2,128)}, u32[]{:S(2)}) copy-start(f32[48,2,1536]{2,1,0:T(2,128)} %get-tuple-element.744) | copy-start | bytes 1769476 | tf_op jit(solution)/shard_map/cond
  423.2 6.1 %copy-start.37 = (f32[48,2,1536]{2,1,0:T(2,128)S(1)}, f32[48,2,1536]{2,1,0:T(2,128)}, u32[]{:S(2)}) copy-start(f32[48,2,1536]{2,1,0:T(2,128)} %get-tuple-element.745) | copy-start | bytes 1769476 | tf_op jit(solution)/shard_map/cond
  423.3 5.8 %copy-start.80 = (f32[48,1536]{1,0:T(8,128)S(1)}, f32[48,1536]{1,0:T(8,128)}, u32[]{:S(2)}) copy-start(f32[48,1536]{1,0:T(8,128)} %get-tuple-element.230) | copy-start | bytes 884740 | tf_op jit(solution)/shard_map/cond
  423.3 6.0 %copy-start.81 = (f32[48,1536]{1,0:T(8,128)S(1)}, f32[48,1536]{1,0:T(8,128)}, u32[]{:S(2)}) copy-start(f32[48,1536]{1,0:T(8,128)} %get-tuple-element.226) | copy-start | bytes 884740 | tf_op jit(solution)/shard_map/cond
  423.3 6.0 %copy-start.82 = (f32[48,1536]{1,0:T(8,128)S(1)}, f32[48,1536]{1,0:T(8,128)}, u32[]{:S(2)}) copy-start(f32[48,1536]{1,0:T(8,128)} %get-tuple-element.227) | copy-start | bytes 884740 | tf_op jit(solution)/shard_map/cond
  425.1 8.7 %copy-start.24 = (f32[3816,384]{1,0:T(8,128)S(1)}, f32[3816,384]{1,0:T(8,128)}, u32[]{:S(2)}) copy-start(f32[3816,384]{1,0:T(8,128)} %get-tuple-element.215) | copy-start | bytes 17584132 | tf_op jit(solution)/shard_map/cond
  427.7 6.1 %slice-start = ((s8[5861376]{0:T(1024)(128)(4,1)}), s8[4194304]{0:T(1024)(128)(4,1)S(1)}, s32[]{:S(2)}) async-start(s8[5861376]{0:T(1024)(128)(4,1)} %bitcast.243), calls=%async_computation.20 | async-start | bytes 8388608 | tf_op jit(solution)/shard_map/cond
  429.4 4.4 slice-start.1
  454.5 0.9 copy-start.85
  (2 other events, 1.5 us)

commit v4 on v3

--- a/solution.py
+++ b/solution.py
@@ -208,7 +208,7 @@
             copy.wait()
             total = self.held[index][view].astype(f32) + self.landed[slot][...].astype(f32)
             if step == self.last - 1:
-                self.out[:, self.cols] = total
+                self.out(self.cols, total)
             else:
                 self.held[index][view] = total.astype(bf16)
         self.live = []
@@ -256,6 +256,7 @@
         "plain": far + near + ["t"],
         "late": far + near + ["y", "t"],
         "early": far + ["y"] + near + ["t"],
+        "cross": far[:-1] + near + ["y"] + far[-1:] + ["t"],
     }
 
 
@@ -265,6 +266,7 @@
         "plain": ["t"] + near + far,
         "early": ["t", "y"] + near + far,
         "late": ["t"] + near + ["y"] + far,
+        "cross": ["t"] + far[:1] + ["y"] + near + far[1:],
     }
 
 
@@ -339,9 +341,9 @@
     here = Place()
     n, count = here.n_dp, here.count
     table, heard, pos, norm_rows, cosine, sine, seg_row, seg_col = refs[:8]
-    shards = refs[8:13]
-    emb_out, zero_out, input_out, q_out, k_out, v_out, lse_out, att_own, att_other = refs[13:22]
-    fulls, at = [], 22
+    attn_in, attn_out, ffn_in, ffn_out = refs[8:12]
+    emb_out, zero_out, input_out, q_out, k_out, v_out, lse_out, att_own, att_other = refs[12:21]
+    fulls, at = [], 21
     for kind in kinds:
         width = 1 if kind == "plain" else 2
         fulls.append((refs[at], None) if width == 1 else (refs[at], refs[at + 1]))
@@ -361,8 +363,12 @@
         [{"dp": here.mixed(k)} for k in range(1, n)] + [here.across("t"), here.across("y")]
     )
     orders = gather_orders(count)
-    for low, shard in zip(lows, shards):
-        low[...] = shard[...].astype(bf16)
+    for c in range(3):
+        lows[0][:, c * feats : (c + 1) * feats] = attn_in[:, c, :].astype(bf16)
+    lows[1][...] = attn_out[...].astype(bf16)
+    for c in range(2):
+        lows[2 + c][...] = ffn_in[:, c, :].astype(bf16)
+    lows[4][...] = ffn_out[...].astype(bf16)
     jobs, lags = [], []
     for number, (which, kind, start, size, lag) in enumerate(pieces):
         jobs.append(
@@ -388,7 +394,7 @@
         y_copies.append(copy)
 
     for k in list(range(n - 1, 0, -1)) + [0]:
-        column = jnp.transpose(heard[k])[:room, 0:1]
+        column = jnp.transpose(heard[0, k])[:room, 0:1]
         hot = (lax.broadcasted_iota(jnp.int32, (room, row_count), 1) == column).astype(f32)
         found = mdot(hot.astype(bf16), low_table[...]).astype(bf16)
         if k == 0:
@@ -487,9 +493,15 @@
         copy.wait()
 
 
-def forward_pass(table, heard, pos, norm_rows, cosine, sine, seg_row, seg_col, shards, kinds, pieces,
-                 stride=2, every=1):
-    n_dp = heard.shape[0]
+def forward_pass(table, heard, pos, norm_rows, cosine, sine, seg_row, seg_col, raw, kinds, pieces,
+                 stride=3, every=1):
+    n_dp = heard.shape[1]
+    attn_in, attn_out, ffn_in, ffn_out = raw
+    rows = attn_in.shape[0]
+    shards = (
+        sds((rows, 3 * attn_in.shape[2]), f32), sds(attn_out.shape, f32),
+        sds(ffn_out.shape, f32), sds(ffn_out.shape, f32), sds(ffn_out.shape, f32),
+    )
     room = heard_room(pos.shape[0], n_dp)
     count = n_dp.bit_length() - 1
     halves = (2,) * (count + 1)
@@ -530,12 +542,12 @@
     out = pl.pallas_call(
         lambda *refs: forward_body(room, kinds, pieces, stride, every, *refs),
         out_shape=outs,
-        in_specs=[VM] * (8 + len(shards)),
+        in_specs=[VM] * 12,
         out_specs=specs,
         scratch_shapes=scratch,
         compiler_params=params(2),
         name="forward",
-    )(table, heard, pos, norm_rows, cosine, sine, seg_row, seg_col, *shards)
+    )(table, heard, pos, norm_rows, cosine, sine, seg_row, seg_col, *raw)
     weights, at = [], 9
     for shard, kind in zip(shards, kinds):
         whole = (2 * n_dp * shard.shape[0], shard.shape[1])
@@ -546,6 +558,16 @@
             weights.append((out[at].reshape(whole), out[at + 1].reshape(whole)))
             at += 2
     return out[:9], weights
+
+
+def writer(ref, kind=None):
+    def store(cols, values):
+        if kind is None:
+            ref[:, cols] = values
+        else:
+            ref[:, kind, cols] = values
+
+    return store
 
 
 def make_scatters(
@@ -602,16 +624,16 @@
 def hidden_body(pieces, sizes, stride, *refs):
     here = Place()
     count = here.count
-    (grad_pool, seg, hat_two, scale_two, norm_rows, low_one, hat_one, scale_one,
-     att_own, att_other, hidden_own, hidden_other) = refs[:12]
-    weights = refs[12:18]
-    residual, low_out, norms_out, wout_own, wout_other = refs[18:23]
-    later = refs[23:27]
-    out_down, squares = refs[27:29]
-    loaded, down, low_two, turned_one, turned_two, total = refs[29:35]
-    held = refs[35 : 35 + sizes[0]]
-    landed = refs[35 + sizes[0] : 35 + sizes[0] + sizes[1]]
-    wsem, send, recv, loads = refs[35 + sizes[0] + sizes[1] :]
+    (grad_pool, seg, sum_two, norm_rows, low_one, sum_one,
+     att_own, att_other, hidden_own, hidden_other) = refs[:10]
+    weights = refs[10:16]
+    residual, low_out, norms_out, wout_own, wout_other = refs[16:21]
+    later = refs[21:25]
+    out_down, squares = refs[25:27]
+    loaded, down, low_two, turned_one, turned_two, total = refs[27:33]
+    held = refs[33 : 33 + sizes[0]]
+    landed = refs[33 + sizes[0] : 33 + sizes[0] + sizes[1]]
+    wsem, send, recv, loads = refs[33 + sizes[0] + sizes[1] :]
     half, width = low_one.shape
     part = weights[0].shape[1] // 2
     copies = {}
@@ -629,16 +651,16 @@
     greet([here.across("t"), here.across("y")] + [here.across(j) for j in range(count)])
     grads = [(down.at[0], down.at[1])]
     runner = make_scatters(
-        here, grads, None, pieces, (out_down,), held, landed, send, recv, loads, stride
+        here, grads, None, pieces, (writer(out_down),), held, landed, send, recv, loads, stride
     )
     slots = grad_pool.shape[0]
-    hot = (lax.broadcasted_iota(jnp.int32, (half, slots), 1) == seg[...]).astype(f32)
+    hot = (lax.broadcasted_iota(jnp.int32, (half, slots), 1) == seg[0:half, :]).astype(f32)
     grad_two = jnp.dot(hot, grad_pool[...], precision=highest, preferred_element_type=f32)
-    hat = hat_two[...]
+    hat, scale = norm_parts(sum_two[...])
     grad_hat = grad_two * norm_rows[4:5, :]
     first = jnp.mean(grad_hat, -1, keepdims=True)
     second = jnp.mean(grad_hat * hat, -1, keepdims=True)
-    grad_sum = scale_two[...] * (grad_hat - first - hat * second)
+    grad_sum = scale * (grad_hat - first - hat * second)
     low_two[...] = grad_sum.astype(bf16)
     turned_two[...] = jnp.transpose(grad_sum).astype(bf16)
     for c in range(2):
@@ -672,12 +694,12 @@
             if c == 0:
                 load(1, j)
             runner.advance()
-    hat = hat_one[...]
+    hat, scale = norm_parts(sum_one[...])
     grad_one = total[...]
     grad_hat = grad_one * norm_rows[2:3, :]
     first = jnp.mean(grad_hat, -1, keepdims=True)
     second = jnp.mean(grad_hat * hat, -1, keepdims=True)
-    grad_sum = scale_one[...] * (grad_hat - first - hat * second)
+    grad_sum = scale * (grad_hat - first - hat * second)
     norms_out[2:3, :] = jnp.sum(grad_one * hat, 0, keepdims=True)
     norms_out[3:4, :] = jnp.sum(grad_one, 0, keepdims=True)
     residual[...] = grad_sum
@@ -691,8 +713,8 @@
     squares[...] = jnp.broadcast_to(square_sum(out_down[...]), squares.shape)
 
 
-def hidden_back(grad_pool, seg, hat_two, scale_two, norm_rows, low_one, hat_one, scale_one, att,
-                hidden, w_gate, w_up, w_down, pieces, stride=1):
+def hidden_back(grad_pool, seg, sum_two, norm_rows, low_one, sum_one, att, hidden, w_gate, w_up,
+                w_down, pieces, stride=1):
     n_dp = lax.axis_size("dp")
     count = n_dp.bit_length() - 1
     half, width = low_one.shape
@@ -708,7 +730,7 @@
             sds((half, width), f32), sds((half, width), bf16), sds((8, width), f32),
             sds((width, feats), bf16), sds((width, feats), bf16),
         ] + [sds(blocks, bf16)] * 4 + [sds((rows, cols), f32), sds((8, 128), f32)],
-        in_specs=[VM] * 12 + [ANY] * 6,
+        in_specs=[VM] * 10 + [ANY] * 6,
         out_specs=[VM] * 11,
         scratch_shapes=[
             vmem((6, width, cols // 2), bf16), vmem((2,) + blocks, bf16), vmem((half, width), bf16),
@@ -716,7 +738,7 @@
         ] + held + landed + [pltpu.SemaphoreType.DMA((12,))] + sems,
         compiler_params=params(6),
         name="hidden",
-    )(grad_pool, seg, hat_two, scale_two, norm_rows, low_one, hat_one, scale_one, *att, *hidden,
+    )(grad_pool, seg, sum_two, norm_rows, low_one, sum_one, *att, *hidden,
       *w_gate, *w_up, *w_down)
 
 
@@ -726,7 +748,8 @@
     (low, out_own, out_other, query, key, value, lse, cosine, sine, seg_row, seg_col, residual,
      emb, norm_rows, w_qkv, norms_in, before, inputs, pos, heard) = refs[:20]
     grads = [(refs[20 + 2 * j], refs[21 + 2 * j]) for j in range(3)]
-    (table_out, norms_out, out_gate, out_up, out_proj, out_qkv, total_out) = refs[26:33]
+    (table_out, norms_out, out_ffn, out_proj, out_qkv, total_out) = refs[26:32]
+    refs = refs[:26] + (None,) + refs[26:]
     (kt, dq, dk, dv, grad_att, far_att, far_send, far_recv, grad_proj, turned_in, grad_qkv,
      low_out, norm_part, other, packed, mine, theirs, norms, parts, own_part) = refs[33:53]
     at = 53
@@ -755,8 +778,8 @@
     me = (here.t * n + here.d) * 2 + here.m
     greet([where for _, where in peers])
     runner = make_scatters(
-        here, grads, None, pieces, (out_gate, out_up, out_proj), held, landed, send, recv, loads,
-        stride,
+        here, grads, None, pieces, (writer(out_ffn, 0), writer(out_ffn, 1), writer(out_proj)), held,
+        landed, send, recv, loads, stride,
     )
     runner.advance()
     att_copies = []
@@ -829,15 +852,20 @@
         )
         copy.start()
         far_copies.append(copy)
+    grad_parts = [grad_qkv.at[c] for c in range(3)]
     late = make_scatters(
-        here, [(grad_qkv, None)], None, late_pieces, (out_qkv,), late_held, late_landed, late_send,
-        late_recv, late_loads, 1,
+        here, [(part, None) for part in grad_parts], None, late_pieces,
+        [writer(out_qkv, c) for c in range(3)], late_held, late_landed, late_send, late_recv,
+        late_loads, 1,
     )
     jobs = late.jobs
     step = feats if grad_qkv.shape[-2] % 16 == 0 else 128
     for start in range(0, 3 * feats, step):
         cols = slice(start, start + step)
-        store_blocks(grad_qkv, mdot(turned_in[...], grad_proj[:, cols]), count, start)
+        store_blocks(
+            grad_parts[start // feats], mdot(turned_in[...], grad_proj[:, cols]), count,
+            start % feats,
+        )
     late.advance()
     runner.advance()
     theirs_at = pl.ds(pl.multiple_of((1 - here.m) * width, 128), width)
@@ -927,10 +955,9 @@
     local_sq = (
         before[0:1, 0:1]
         + 0.5 * jnp.sum(own_part[...], 1, keepdims=True)[0:1]
-        + square_sum(out_qkv[...])
         + square_sum(out_proj[...])
-        + square_sum(out_gate[...])
-        + square_sum(out_up[...])
+        + sum(square_sum(out_qkv[:, c, :]) for c in range(3))
+        + sum(square_sum(out_ffn[:, c, :]) for c in range(2))
     )
     parts[me] = jnp.broadcast_to(local_sq, parts.shape[1:])
     copies = []
@@ -951,7 +978,7 @@
 
 def backward_pass(low, w_out, query, key, value, lse, cosine, sine, seg_row, seg_col, residual,
                   emb, norm_rows, w_qkv, norms, before, inputs, pos_row, heard, grads, grad_out,
-                  row_count, pieces, late_pieces, stride=2, every=1):
+                  row_count, pieces, late_pieces, stride=3, every=1):
     n_dp = lax.axis_size("dp")
     count = n_dp.bit_length() - 1
     tok, feats = query.shape
@@ -959,7 +986,7 @@
     rows, cols = grads[0].shape[-2:]
     room = heard_room(tok, n_dp)
     held, landed, sems = scatter_scratch(count, rows, [True] * 3, pieces)
-    late_held, late_landed, late_sems = scatter_scratch(count, rows, [False], late_pieces)
+    late_held, late_landed, late_sems = scatter_scratch(count, rows, [False] * 3, late_pieces)
     flat = list(grads) + [blocks_of(g, n_dp) for g in grad_out]
     dma = pltpu.SemaphoreType.DMA
     vmem = pltpu.VMEM
@@ -970,17 +997,17 @@
         lambda *refs: backward_body(room, pieces, late_pieces, sizes, stride, every, *refs),
         out_shape=[
             sds((row_count, part), f32), sds((8, width), f32),
-            sds((rows, cols), f32), sds((rows, cols), f32), sds((rows, feats), f32),
-            sds((rows, 3 * feats), f32), sds((8, 128), f32),
+            sds((rows, 2, cols), f32), sds((rows, feats), f32), sds((rows, 3, feats), f32),
+            sds((8, 128), f32),
         ],
         in_specs=[VM] * 20 + [ANY] * 6,
-        out_specs=[VM] * 7,
+        out_specs=[VM] * 6,
         scratch_shapes=[
             vmem((128, tok), bf16), vmem((tok, 128), f32), vmem((tok, 128), f32),
             vmem((tok, 128), f32), vmem((tok, feats), bf16), vmem((half, feats), bf16),
             vmem((half, width), bf16), vmem((half, width), bf16),
             vmem((tok, 3 * feats), bf16), vmem((width, tok), bf16),
-            vmem((2,) * (count + 1) + (rows, 3 * feats), bf16),
+            vmem((3,) + (2,) * (count + 1) + (rows, feats), bf16),
             vmem((half, width), bf16), vmem((8, width), f32), vmem((half, part), bf16),
             vmem((n_dp, room, part), bf16), vmem((n_dp, room, part), bf16),
             vmem((n_dp, room, part), bf16), vmem((count + 2, 8, width), f32),
@@ -1578,17 +1605,14 @@
     ff = ffn_out.shape[1]
     part_ff = ff // 2
 
-    shards = (
-        attn_in.reshape(attn_in.shape[0], -1), attn_out, ffn_in[:, 0], ffn_in[:, 1], ffn_out,
-    )
     kinds = ("plain", "late", "late", "late", "late")
     gather_pieces = [(0, "plain", 0, 3 * feats, 0)]
     quarter = ff // 4
     for turn, which in enumerate((2, 3, 4)):
         for c in range(4):
-            kind = ("late", "early")[c % 2]
+            kind = ("late", "early", "cross")[(4 * turn + c) % 3]
             gather_pieces.append((which, kind, c * quarter, quarter, 4 * turn + c))
-    gather_pieces.append((1, "late", 0, feats, 6))
+    gather_pieces.append((1, "early", 0, feats, 6))
     places = (jnp.arange(tok, dtype=jnp.int32) + model_idx * half) % tok
     pos_rel = jnp.where(model_idx == 0, pos, jnp.concatenate([pos[half:], pos[:half]]))
     lengths_row = seq_lengths[tower_idx, data_idx]
@@ -1597,8 +1621,8 @@
     seg_row, seg_col = segment[None, :], segment[:, None]
     named = heard[:, :, 0, : heard_room(tok, heard.shape[1])].reshape(2, 1, -1)
     kept, weights = forward_pass(
-        embedding, heard[0], pos_rel[:, None], norm_params[0:2], cosine, sine, seg_row, seg_col,
-        shards, kinds, gather_pieces,
+        embedding, heard, pos_rel[:, None], norm_params, cosine, sine, seg_row, seg_col,
+        (attn_in, attn_out, ffn_in, ffn_out), kinds, gather_pieces,
     )
     emb, stream_zero, input_zero, query, key, value, lse = kept[:7]
     att = kept[7:9]
@@ -1630,22 +1654,21 @@
 
     pieces = [(0, ("early", "late")[c % 2], c * quarter, quarter, c) for c in range(4)]
     out = hidden_back(
-        grad_pool, seg_col[:half], hat_two, scale_two, norm_params, input_one, hat_one, scale_one,
-        att, hidden, w_gate, w_up, w_down, pieces, 2,
+        grad_pool, seg_col, sum_two, norm_params, input_one, sum_one, att, hidden, w_gate, w_up, w_down, pieces, 2,
     )
     grad_sum_one, attn_low, norms = out[:3]
     grad_out, later, r_down, squares = out[3:5], out[5:9], out[9], out[10]
     pieces = [
-        (c // 4, ("early", "late")[c % 2], (c % 4) * quarter, quarter, c) for c in range(8)
+        (c // 4, ("early", "late", "cross")[c % 3], (c % 4) * quarter, quarter, c)
+        for c in range(8)
     ] + [(2, "late", 0, feats, 8)]
-    late_pieces = [(0, "plain", 0, 2 * feats, 0), (0, "plain", 2 * feats, feats, 0)]
-    embed_grad, norm_sum, r_gate, r_up, r_out, r_qkv, total = backward_pass(
+    late_pieces = [(c, "plain", 0, feats, 0) for c in range(3)]
+    embed_grad, norm_sum, r_ffn, r_out, r_qkv, total = backward_pass(
         attn_low, w_out, query, key, value, lse, cosine, sine, seg_row, seg_col, grad_sum_one,
-        emb, norm_params[0:2], w_qkv, norms, squares, input_zero, pos_rel[None, :], named,
+        emb, norm_params, w_qkv, norms, squares, input_zero, pos_rel[None, :], named,
         later, grad_out, row_count, pieces, late_pieces,
     )
     norm_grad = norm_sum[:6]
-    r_qkv = r_qkv.reshape(attn_in.shape)
     total_sq = total[0, 0] + scale_grad * scale_grad
     grad_norm = jnp.sqrt(total_sq)
     factor = jnp.minimum(1.0, clip_max / (grad_norm + 1e-06))
@@ -1653,7 +1676,6 @@
     embed_new = adamw(embedding, embed_grad, embed_m, embed_v, factor, step_num, learn_rate)
     qkv_new = adamw(attn_in, r_qkv, attn_in_m, attn_in_v, factor, step_num, learn_rate)
     out_new = adamw(attn_out, r_out, attn_out_m, attn_out_v, factor, step_num, out_rate)
-    r_ffn = jnp.stack([r_gate, r_up], 1)
     ffn_new = adamw(ffn_in, r_ffn, ffn_in_m, ffn_in_v, factor, step_num, learn_rate)
     down_new = adamw(ffn_out, r_down, ffn_out_m, ffn_out_v, factor, step_num, learn_rate)
     norms_new = adamw(norm_params, norm_grad, norm_m, norm_v, factor, step_num, norm_rate)

time: 473 us -> 445 us (0.941)
  Pallas kernels: 357 us -> 335 us
  local copies, waits for them, and re-layouts: 29.8 us -> 20.2 us
    pallas_call x1, Pallas kernels: 135 us -> 122 us  [forward_pass(): pl.pallas_call(lambda *refs: forward_body(room, kinds, pieces, stride, ev...]
    pallas_call x1, Pallas kernels: 142 us -> 136 us  [backward_pass(): pl.pallas_call(lambda *refs: backward_body(room, pieces, late_pieces, siz...]
    cond x68 -> x67, local copies, waits for them, and re-layouts: 10.2 us -> 5.98 us
where the time goes in v4:
time: 445 us; the launch traced here: 439 us
  Pallas kernels  335 us (75%)
  other arithmetic  33.1 us (7%)
  between operations  20.3 us (5%)
  local copies, waits for them, and re-layouts  20.2 us (5%)
  loops' own time  15.4 us (3%)
  matrix products  14.4 us (3%)
    pallas_call x1, Pallas kernels, backward_pass(): pl.pallas_call(lambda *refs: backward_body(room, pieces, late_pieces, siz...  136 us
    pallas_call x1, Pallas kernels, forward_pass(): pl.pallas_call(lambda *refs: forward_body(room, kinds, pieces, stride, ev...  122 us
    pallas_call x1, Pallas kernels, hidden_back(): pl.pallas_call(lambda *refs: hidden_body(pieces, (len(held), len(landed))...  49.7 us
    sub x6, other arithmetic, adamw(): weight_in - rate * (first_hat / (jnp.sqrt(second_hat) + adam_eps) + decay...  20.3 us
    pallas_call x1, Pallas kernels, loss_step(): pl.pallas_call(loss_body, out_shape=[sds(part.shape, f32), sds((8, 128),...  17.3 us
    another operation x1, loops' own time, local(): lax.cond(flag[1, 0] > 0, lambda values: plain_step(*values), lambda value...  15.4 us
    pallas_call x1, Pallas kernels, exchange_lists(): pl.pallas_call(lists_body, out_shape=[sds((2,) + lists.shape, jnp.int32),...  9.91 us

profile of v4, /device:TPU:1, one launch (start us, length us, event | category | flops | bytes accessed | tf_op | source)
XLA Modules:
  0.0 438.7 jit_solution(16136372151606867148)
XLA Ops:
  7.2 1.5 select_reduce_fusion.5
  10.2 1.5 convert_reduce_fusion.4
  13.0 1.0 select_reduce_fusion.4
  14.6 9.9 %lists.1 = (s32[2,8,8,128]{3,2,1,0:T(8,128)S(1)}, s32[8,128]{1,0:T(8,128)}) custom-call(s32[8,8,128]{2,1,0:T(8,128)} %concatenate.47.lists), custom_call_target="tpu_custom_call" | custom-call | tf_op jit(solution)/shard_map/lists/pallas_call | solution.py:311
  24.5 1.2 slice.111
  26.4 399.7 %conditional.1 = (f32[3816,384]{1,0:T(8,128)}, f32[3816,384]{1,0:T(8,128)}, f32[3816,384]{1,0:T(8,128)}, f32[48,3,384]{2,0,1:T(8,128)S(1)}, f32[48,3,384]{2,0,1:...) conditional(s32[]{:T(128)} %bitcast.63, ...), branch_computations={%region_4.12_spmd, %region_12.69_spmd} | conditional | flops 32450023424 | bytes 1181347840 | solution.py:1699
  34.8 1.4 reshape.739.target
  36.2 1.8 copy.225.refs_8_
  38.1 1.0 copy.199.refs_7_.refs_1_.refs_10_
  40.2 2.9 fusion.48
  43.2 122.0 %forward.1 = (bf16[512,768]{1,0:T(8,128)(2,1)}, f32[512,768]{1,0:T(8,128)}, bf16[1024,768]{1,0:T(8,128)(2,1)}, bf16[1024,384]{1,0:T(8,128)(2,1)}, bf16[1024,384]...) custom-call(f32[3816,384]{1,0:T(8,128)} %get-tuple-element.203.refs_, ...), custom_call_target="tpu_custom_call" | custom-call | tf_op jit(solution)/shard_map/cond/branch_0_fun/forward/pallas_call | solution.py:542
  165.2 1.9 fusion.192
  167.1 1.9 fusion.188
  169.7 1.6 copy-done.36
  171.3 1.4 fusion.195
  173.2 1.6 fusion.36.refs_9_
  174.9 1.4 fusion.193
  177.1 1.8 fusion.35.refs_8_
  178.9 1.1 copy-done.49
  180.0 1.4 fusion.194
  181.7 1.6 fusion.189
  183.6 1.5 fusion.37.part
  185.2 17.3 %loss.1 = (f32[16,768]{1,0:T(8,128)}, f32[8,128]{1,0:T(8,128)}) custom-call(f32[16,768]{1,0:T(8,128)} %fusion.37.part, f32[16,1]{1,0:T(8,128)} %maximum_convert_fusion.counts, f32[1,128]{1,0:T(1,128)} %reshape.695.doc_ok, f32[128,1]{1,0:T(8,128)} %reshape.738.query_ok, s32[128,1]{1,0:T(8,128)} %reshape.739.target, f32[1,1]{1,0:T(1,128)} %bitcast.12.scale), custom_call_target="tpu_custom_call" | custom-call | tf_op jit(solution)/shard_map/cond/branch_0_fun/loss/pallas_call | solution.py:1092
  202.5 49.7 %hidden.1 = (f32[512,768]{1,0:T(8,128)}, bf16[512,768]{1,0:T(8,128)(2,1)}, f32[8,768]{1,0:T(8,128)}, bf16[768,384]{1,0:T(8,128)(2,1)}, bf16[768,384]{1,0:T(8,128...) custom-call(f32[16,768]{1,0:T(8,128)} %get-tuple-element.230.refs_0_, ...), custom_call_target="tpu_custom_call" | custom-call | tf_op jit(solution)/shard_map/cond/branch_0_fun/hidden/pallas_call | solution.py:727
  252.3 136.3 %backward.1 = (f32[3816,384]{1,0:T(8,128)}, f32[8,768]{1,0:T(8,128)}, f32[48,2,1536]{2,1,0:T(2,128)}, f32[48,384]{1,0:T(8,128)}, f32[48,3,384]{2,1,0:T(4,128)}, /*index=5*/f32[8,128]{1,0:T(8,128)}) custom-call(bf16[512,768]{1,0:T(8,128)(2,1)} %get-tuple-element.231.refs_0_, bf16[768,384]{1,0:T(8,128)(2,1)} %bitcast.256, bf16[768,384]{1,0:T(8,128)(2,1)} %bitcast.258, ...), custom_call_target="tpu_custom_call" | custom-call | tf_op jit(solution)/shard_map/cond/branch_0_fun/backward/pallas_call | solution.py:996
  388.7 1.3 slice.86
  390.0 1.3 fusion.186
  394.8 1.4 multiply_subtract_fusion.5
  396.1 1.6 multiply_subtract_fusion.4
  398.0 1.7 multiply_subtract_fusion.3
  401.2 3.3 multiply_subtract_fusion.1
  404.5 12.1 %multiply_subtract_fusion = (f32[3816,384]{1,0:T(8,128)}, f32[3816,384]{1,0:T(8,128)}, f32[3816,384]{1,0:T(8,128)}) fusion(f32[3816,384]{1,0:T(8,128)} %get-tuple-element.203.refs_0_, f32[3816,384]{1,0:T(8,128)S(1)} %copy-done.24, f32[]{:T(128)} %bitcast.18, f32[3816,384]{1,0:T(8,128)} %get-tuple-element.204, f32[3816,384]{1,0:T(8,128)} %get-tuple-element.251), kind=kLoop, calls=%fused_computation.51 | loop fusion | flops 23445504 | bytes 41029636 | tf_op jit(solution)/shard_map/cond/branch_0_fun/sub | solution.py:1146
  (110 shorter events, 15.5 us)
Async XLA Ops:
  26.4 16.7 %copy-start.17 = (f32[48,2,1536]{2,1,0:T(2,128)S(1)}, f32[48,2,1536]{2,1,0:T(2,128)}, u32[]{:S(2)}) copy-start(f32[48,2,1536]{2,1,0:T(2,128)} %get-tuple-element.215.refs_10_) | copy-start | bytes 1769476 | tf_op jit(solution)/shard_map/cond
  26.4 16.7 %copy-start.25 = (f32[48,1536]{1,0:T(8,128)S(1)}, f32[48,1536]{1,0:T(8,128)}, u32[]{:S(2)}) copy-start(f32[48,1536]{1,0:T(8,128)} %get-tuple-element.216.refs_11_) | copy-start | bytes 884740 | tf_op jit(solution)/shard_map/cond
  26.4 16.7 %copy-start.51 = (f32[48,384]{1,0:T(8,128)S(1)}, f32[48,384]{1,0:T(8,128)}, u32[]{:S(2)}) copy-start(f32[48,384]{1,0:T(8,128)} %get-tuple-element.214.refs_9_) | copy-start | bytes 221188 | tf_op jit(solution)/shard_map/cond
  26.5 16.7 %copy-start.61 = (f32[6,768]{1,0:T(8,128)S(1)}, f32[6,768]{1,0:T(8,128)}, u32[]{:S(2)}) copy-start(f32[6,768]{1,0:T(8,128)} %get-tuple-element.212.refs_3_.refs_13_) | copy-start | bytes 55300 | tf_op jit(solution)/shard_map/cond
  30.1 135.2 %copy-start.114 = (s32[1024]{0:T(1024)}, s32[1024]{0:T(1024)S(1)}, u32[]{:S(2)}) copy-start(s32[1024]{0:T(1024)S(1)} %add_select_fusion.2) | copy-start | bytes 12292 | tf_op jit(solution)/shard_map/cond
  31.0 12.1 %copy-start.100 = (s32[1024]{0:T(1024)}, s32[1024]{0:T(1024)S(1)}, u32[]{:S(2)}) copy-start(s32[1024]{0:T(1024)S(1)} %convert_reduce_fusion) | copy-start | bytes 12292 | tf_op jit(solution)/shard_map/cond
  165.2 1.9 copy-start.50
  169.0 12.4 %copy-start.13 = (f32[512,768]{1,0:T(8,128)}, f32[512,768]{1,0:T(8,128)S(1)}, u32[]{:S(2)}) copy-start(f32[512,768]{1,0:T(8,128)S(1)} %get-tuple-element.984.refs_5_) | copy-start | bytes 4718596 | tf_op jit(solution)/shard_map/cond
  169.0 2.2 copy-start.36
  171.2 5.0 %copy-start.31 = (bf16[512,768]{1,0:T(8,128)(2,1)}, bf16[512,768]{1,0:T(8,128)(2,1)S(1)}, u32[]{:S(2)}) copy-start(bf16[512,768]{1,0:T(8,128)(2,1)S(1)} %fusion.42.refs_4_) | copy-start | bytes 2359300 | tf_op jit(solution)/shard_map/cond
  171.2 1.9 copy-start.38
  173.2 1.7 copy-start.35
  174.9 6.6 %copy-start.48 = (bf16[512,1536]{1,0:T(8,128)(2,1)}, bf16[512,1536]{1,0:T(8,128)(2,1)S(1)}, u32[]{:S(2)}) copy-start(bf16[512,1536]{1,0:T(8,128)(2,1)S(1)} %fusion.36.refs_9_) | copy-start | bytes 4718596 | tf_op jit(solution)/shard_map/cond
  174.9 2.2 copy-start.37
  177.1 2.9 copy-start.39
  178.9 1.1 copy-start.49
  180.0 1.7 copy-start.40
  183.3 19.2 %copy-start.14 = (f32[512,768]{1,0:T(8,128)}, f32[512,768]{1,0:T(8,128)S(1)}, u32[]{:S(2)}) copy-start(f32[512,768]{1,0:T(8,128)S(1)} %get-tuple-element.986.refs_2_) | copy-start | bytes 4718596 | tf_op jit(solution)/shard_map/cond
  252.2 142.5 %copy-start.103 = (f32[6,768]{1,0:T(8,128)S(1)}, f32[6,768]{1,0:T(8,128)}, u32[]{:S(2)}) copy-start(f32[6,768]{1,0:T(8,128)} %get-tuple-element.264) | copy-start | bytes 55300 | tf_op jit(solution)/shard_map/cond
  252.2 142.5 %copy-start.105 = (f32[6,768]{1,0:T(8,128)S(1)}, f32[6,768]{1,0:T(8,128)}, u32[]{:S(2)}) copy-start(f32[6,768]{1,0:T(8,128)} %get-tuple-element.266) | copy-start | bytes 55300 | tf_op jit(solution)/shard_map/cond
  252.2 143.9 %copy-start.88 = (f32[48,384]{1,0:T(8,128)S(1)}, f32[48,384]{1,0:T(8,128)}, u32[]{:S(2)}) copy-start(f32[48,384]{1,0:T(8,128)} %get-tuple-element.255) | copy-start | bytes 221188 | tf_op jit(solution)/shard_map/cond
  252.2 143.9 %copy-start.90 = (f32[48,384]{1,0:T(8,128)S(1)}, f32[48,384]{1,0:T(8,128)}, u32[]{:S(2)}) copy-start(f32[48,384]{1,0:T(8,128)} %get-tuple-element.257) | copy-start | bytes 221188 | tf_op jit(solution)/shard_map/cond
  252.3 145.5 %copy-start.54 = (f32[48,1536]{1,0:T(8,128)S(1)}, f32[48,1536]{1,0:T(8,128)}, u32[]{:S(2)}) copy-start(f32[48,1536]{1,0:T(8,128)} %get-tuple-element.261) | copy-start | bytes 884740 | tf_op jit(solution)/shard_map/cond
  252.3 145.5 %copy-start.56 = (f32[48,1536]{1,0:T(8,128)S(1)}, f32[48,1536]{1,0:T(8,128)}, u32[]{:S(2)}) copy-start(f32[48,1536]{1,0:T(8,128)} %get-tuple-element.263) | copy-start | bytes 884740 | tf_op jit(solution)/shard_map/cond
  252.3 145.5 %copy-start.84 = (f32[48,1536]{1,0:T(8,128)S(1)}, f32[48,1536]{1,0:T(8,128)}, u32[]{:S(2)}) copy-start(f32[48,1536]{1,0:T(8,128)} %get-tuple-element.262) | copy-start | bytes 884740 | tf_op jit(solution)/shard_map/cond
  252.3 145.7 %copy-start.28 = (f32[48,3,384]{2,0,1:T(8,128)S(1)}, f32[48,3,384]{2,0,1:T(8,128)}, u32[]{:S(2)}) copy-start(f32[48,3,384]{2,0,1:T(8,128)} %get-tuple-element.788) | copy-start | bytes 663556 | tf_op jit(solution)/shard_map/cond
  252.3 145.7 %copy-start.65 = (f32[48,3,384]{2,0,1:T(8,128)S(1)}, f32[48,3,384]{2,0,1:T(8,128)}, u32[]{:S(2)}) copy-start(f32[48,3,384]{2,0,1:T(8,128)} %get-tuple-element.795) | copy-start | bytes 663556 | tf_op jit(solution)/shard_map/cond
  252.3 145.7 %copy-start.67 = (f32[48,3,384]{2,0,1:T(8,128)S(1)}, f32[48,3,384]{2,0,1:T(8,128)}, u32[]{:S(2)}) copy-start(f32[48,3,384]{2,0,1:T(8,128)} %get-tuple-element.796) | copy-start | bytes 663556 | tf_op jit(solution)/shard_map/cond
  388.7 12.6 %copy-start.41 = (f32[48,2,1536]{2,1,0:T(2,128)S(1)}, f32[48,2,1536]{2,1,0:T(2,128)}, u32[]{:S(2)}) copy-start(f32[48,2,1536]{2,1,0:T(2,128)} %get-tuple-element.258) | copy-start | bytes 1769476 | tf_op jit(solution)/shard_map/cond
  388.7 12.6 %copy-start.43 = (f32[48,2,1536]{2,1,0:T(2,128)S(1)}, f32[48,2,1536]{2,1,0:T(2,128)}, u32[]{:S(2)}) copy-start(f32[48,2,1536]{2,1,0:T(2,128)} %get-tuple-element.260) | copy-start | bytes 1769476 | tf_op jit(solution)/shard_map/cond
  388.7 12.5 %copy-start.75 = (f32[48,2,1536]{2,1,0:T(2,128)S(1)}, f32[48,2,1536]{2,1,0:T(2,128)}, u32[]{:S(2)}) copy-start(f32[48,2,1536]{2,1,0:T(2,128)} %get-tuple-element.259) | copy-start | bytes 1769476 | tf_op jit(solution)/shard_map/cond
  398.0 6.5 %copy-start.24 = (f32[3816,384]{1,0:T(8,128)S(1)}, f32[3816,384]{1,0:T(8,128)}, u32[]{:S(2)}) copy-start(f32[3816,384]{1,0:T(8,128)} %get-tuple-element.248) | copy-start | bytes 17584132 | tf_op jit(solution)/shard_map/cond
  (4 other events, 3.3 us)

commit v5 on v4

--- a/solution.py
+++ b/solution.py
@@ -1652,7 +1652,10 @@
     def weight_grad(left, right):
         return jnp.einsum("td,tf->df", left, right, preferred_element_type=f32).astype(bf16)
 
-    pieces = [(0, ("early", "late")[c % 2], c * quarter, quarter, c) for c in range(4)]
+    pieces = [
+        (0, kind, c * quarter, quarter, c // 2)
+        for c, kind in enumerate(("early", "cross", "early", "late"))
+    ]
     out = hidden_back(
         grad_pool, seg_col, sum_two, norm_params, input_one, sum_one, att, hidden, w_gate, w_up, w_down, pieces, 2,
     )
@@ -1661,7 +1664,7 @@
     pieces = [
         (c // 4, ("early", "late", "cross")[c % 3], (c % 4) * quarter, quarter, c)
         for c in range(8)
-    ] + [(2, "late", 0, feats, 8)]
+    ] + [(2, "early", 0, feats, 3)]
     late_pieces = [(c, "plain", 0, feats, 0) for c in range(3)]
     embed_grad, norm_sum, r_ffn, r_out, r_qkv, total = backward_pass(
         attn_low, w_out, query, key, value, lse, cosine, sine, seg_row, seg_col, grad_sum_one,

time: 445 us -> 446 us (level)
  no operation moved by 1% of the time
where the time goes in v5:
time: 446 us; the launch traced here: 440 us
  Pallas kernels  336 us (75%)
  other arithmetic  33.1 us (7%)
  between operations  20.3 us (5%)
  local copies, waits for them, and re-layouts  20.2 us (5%)
  loops' own time  15.4 us (3%)
  matrix products  14.4 us (3%)
    pallas_call x1, Pallas kernels, backward_pass(): pl.pallas_call(lambda *refs: backward_body(room, pieces, late_pieces, siz...  137 us
    pallas_call x1, Pallas kernels, forward_pass(): pl.pallas_call(lambda *refs: forward_body(room, kinds, pieces, stride, ev...  122 us
    pallas_call x1, Pallas kernels, hidden_back(): pl.pallas_call(lambda *refs: hidden_body(pieces, (len(held), len(landed))...  49.8 us
    sub x6, other arithmetic, adamw(): weight_in - rate * (first_hat / (jnp.sqrt(second_hat) + adam_eps) + decay...  20.3 us
    pallas_call x1, Pallas kernels, loss_step(): pl.pallas_call(loss_body, out_shape=[sds(part.shape, f32), sds((8, 128),...  17.3 us
    another operation x1, loops' own time, local(): lax.cond(flag[1, 0] > 0, lambda values: plain_step(*values), lambda value...  15.4 us
    pallas_call x1, Pallas kernels, exchange_lists(): pl.pallas_call(lists_body, out_shape=[sds((2,) + lists.shape, jnp.int32),...  9.91 us

profile of v5, /device:TPU:1, one launch (start us, length us, event | category | flops | bytes accessed | tf_op | source)
XLA Modules:
  0.0 439.8 jit_solution(10300650086952964289)
XLA Ops:
  7.2 1.5 select_reduce_fusion.5
  10.2 1.5 convert_reduce_fusion.4
  13.0 1.0 select_reduce_fusion.4
  14.6 9.9 %lists.1 = (s32[2,8,8,128]{3,2,1,0:T(8,128)S(1)}, s32[8,128]{1,0:T(8,128)}) custom-call(s32[8,8,128]{2,1,0:T(8,128)} %concatenate.47.lists), custom_call_target="tpu_custom_call" | custom-call | tf_op jit(solution)/shard_map/lists/pallas_call | solution.py:311
  24.5 1.2 slice.111
  26.4 400.8 %conditional.1 = (f32[3816,384]{1,0:T(8,128)}, f32[3816,384]{1,0:T(8,128)}, f32[3816,384]{1,0:T(8,128)}, f32[48,3,384]{2,0,1:T(8,128)S(1)}, f32[48,3,384]{2,0,1:...) conditional(s32[]{:T(128)} %bitcast.63, ...), branch_computations={%region_4.12_spmd, %region_12.69_spmd} | conditional | flops 32450023424 | bytes 1181347840 | solution.py:1702
  34.8 1.4 reshape.739.target
  36.2 1.8 copy.225.refs_8_
  38.1 1.0 copy.199.refs_7_.refs_1_.refs_10_
  40.2 2.9 fusion.48
  43.2 122.0 %forward.1 = (bf16[512,768]{1,0:T(8,128)(2,1)}, f32[512,768]{1,0:T(8,128)}, bf16[1024,768]{1,0:T(8,128)(2,1)}, bf16[1024,384]{1,0:T(8,128)(2,1)}, bf16[1024,384]...) custom-call(f32[3816,384]{1,0:T(8,128)} %get-tuple-element.203.refs_, ...), custom_call_target="tpu_custom_call" | custom-call | tf_op jit(solution)/shard_map/cond/branch_0_fun/forward/pallas_call | solution.py:542
  165.2 1.9 fusion.192
  167.1 1.9 fusion.188
  169.7 1.6 copy-done.36
  171.3 1.4 fusion.195
  173.2 1.6 fusion.36.refs_9_
  174.9 1.4 fusion.193
  177.1 1.8 fusion.35.refs_8_
  178.9 1.1 copy-done.49
  180.0 1.4 fusion.194
  181.7 1.6 fusion.189
  183.6 1.5 fusion.37.part
  185.2 17.3 %loss.1 = (f32[16,768]{1,0:T(8,128)}, f32[8,128]{1,0:T(8,128)}) custom-call(f32[16,768]{1,0:T(8,128)} %fusion.37.part, f32[16,1]{1,0:T(8,128)} %maximum_convert_fusion.counts, f32[1,128]{1,0:T(1,128)} %reshape.695.doc_ok, f32[128,1]{1,0:T(8,128)} %reshape.738.query_ok, s32[128,1]{1,0:T(8,128)} %reshape.739.target, f32[1,1]{1,0:T(1,128)} %bitcast.12.scale), custom_call_target="tpu_custom_call" | custom-call | tf_op jit(solution)/shard_map/cond/branch_0_fun/loss/pallas_call | solution.py:1092
  202.5 49.8 %hidden.1 = (f32[512,768]{1,0:T(8,128)}, bf16[512,768]{1,0:T(8,128)(2,1)}, f32[8,768]{1,0:T(8,128)}, bf16[768,384]{1,0:T(8,128)(2,1)}, bf16[768,384]{1,0:T(8,128...) custom-call(f32[16,768]{1,0:T(8,128)} %get-tuple-element.230.refs_0_, ...), custom_call_target="tpu_custom_call" | custom-call | tf_op jit(solution)/shard_map/cond/branch_0_fun/hidden/pallas_call | solution.py:727
  252.5 137.3 %backward.1 = (f32[3816,384]{1,0:T(8,128)}, f32[8,768]{1,0:T(8,128)}, f32[48,2,1536]{2,1,0:T(2,128)}, f32[48,384]{1,0:T(8,128)}, f32[48,3,384]{2,1,0:T(4,128)}, /*index=5*/f32[8,128]{1,0:T(8,128)}) custom-call(bf16[512,768]{1,0:T(8,128)(2,1)} %get-tuple-element.231.refs_0_, bf16[768,384]{1,0:T(8,128)(2,1)} %bitcast.256, bf16[768,384]{1,0:T(8,128)(2,1)} %bitcast.258, ...), custom_call_target="tpu_custom_call" | custom-call | tf_op jit(solution)/shard_map/cond/branch_0_fun/backward/pallas_call | solution.py:996
  389.8 1.3 slice.86
  391.1 1.3 fusion.186
  395.9 1.4 multiply_subtract_fusion.5
  397.3 1.6 multiply_subtract_fusion.4
  399.2 1.7 multiply_subtract_fusion.3
  402.3 3.3 multiply_subtract_fusion.1
  405.6 12.1 %multiply_subtract_fusion = (f32[3816,384]{1,0:T(8,128)}, f32[3816,384]{1,0:T(8,128)}, f32[3816,384]{1,0:T(8,128)}) fusion(f32[3816,384]{1,0:T(8,128)} %get-tuple-element.203.refs_0_, f32[3816,384]{1,0:T(8,128)S(1)} %copy-done.24, f32[]{:T(128)} %bitcast.18, f32[3816,384]{1,0:T(8,128)} %get-tuple-element.204, f32[3816,384]{1,0:T(8,128)} %get-tuple-element.251), kind=kLoop, calls=%fused_computation.51 | loop fusion | flops 23445504 | bytes 41029636 | tf_op jit(solution)/shard_map/cond/branch_0_fun/sub | solution.py:1146
  (110 shorter events, 15.5 us)
Async XLA Ops:
  26.4 16.7 %copy-start.17 = (f32[48,2,1536]{2,1,0:T(2,128)S(1)}, f32[48,2,1536]{2,1,0:T(2,128)}, u32[]{:S(2)}) copy-start(f32[48,2,1536]{2,1,0:T(2,128)} %get-tuple-element.215.refs_10_) | copy-start | bytes 1769476 | tf_op jit(solution)/shard_map/cond
  26.4 16.7 %copy-start.25 = (f32[48,1536]{1,0:T(8,128)S(1)}, f32[48,1536]{1,0:T(8,128)}, u32[]{:S(2)}) copy-start(f32[48,1536]{1,0:T(8,128)} %get-tuple-element.216.refs_11_) | copy-start | bytes 884740 | tf_op jit(solution)/shard_map/cond
  26.4 16.7 %copy-start.51 = (f32[48,384]{1,0:T(8,128)S(1)}, f32[48,384]{1,0:T(8,128)}, u32[]{:S(2)}) copy-start(f32[48,384]{1,0:T(8,128)} %get-tuple-element.214.refs_9_) | copy-start | bytes 221188 | tf_op jit(solution)/shard_map/cond
  26.5 16.7 %copy-start.61 = (f32[6,768]{1,0:T(8,128)S(1)}, f32[6,768]{1,0:T(8,128)}, u32[]{:S(2)}) copy-start(f32[6,768]{1,0:T(8,128)} %get-tuple-element.212.refs_3_.refs_13_) | copy-start | bytes 55300 | tf_op jit(solution)/shard_map/cond
  30.1 135.2 %copy-start.114 = (s32[1024]{0:T(1024)}, s32[1024]{0:T(1024)S(1)}, u32[]{:S(2)}) copy-start(s32[1024]{0:T(1024)S(1)} %add_select_fusion.2) | copy-start | bytes 12292 | tf_op jit(solution)/shard_map/cond
  31.0 12.1 %copy-start.100 = (s32[1024]{0:T(1024)}, s32[1024]{0:T(1024)S(1)}, u32[]{:S(2)}) copy-start(s32[1024]{0:T(1024)S(1)} %convert_reduce_fusion) | copy-start | bytes 12292 | tf_op jit(solution)/shard_map/cond
  165.2 1.9 copy-start.50
  169.0 12.4 %copy-start.13 = (f32[512,768]{1,0:T(8,128)}, f32[512,768]{1,0:T(8,128)S(1)}, u32[]{:S(2)}) copy-start(f32[512,768]{1,0:T(8,128)S(1)} %get-tuple-element.984.refs_5_) | copy-start | bytes 4718596 | tf_op jit(solution)/shard_map/cond
  169.0 2.2 copy-start.36
  171.2 5.0 %copy-start.31 = (bf16[512,768]{1,0:T(8,128)(2,1)}, bf16[512,768]{1,0:T(8,128)(2,1)S(1)}, u32[]{:S(2)}) copy-start(bf16[512,768]{1,0:T(8,128)(2,1)S(1)} %fusion.42.refs_4_) | copy-start | bytes 2359300 | tf_op jit(solution)/shard_map/cond
  171.2 1.9 copy-start.38
  173.2 1.7 copy-start.35
  174.9 6.6 %copy-start.48 = (bf16[512,1536]{1,0:T(8,128)(2,1)}, bf16[512,1536]{1,0:T(8,128)(2,1)S(1)}, u32[]{:S(2)}) copy-start(bf16[512,1536]{1,0:T(8,128)(2,1)S(1)} %fusion.36.refs_9_) | copy-start | bytes 4718596 | tf_op jit(solution)/shard_map/cond
  174.9 2.2 copy-start.37
  177.1 2.9 copy-start.39
  178.9 1.1 copy-start.49
  180.0 1.7 copy-start.40
  183.3 19.2 %copy-start.14 = (f32[512,768]{1,0:T(8,128)}, f32[512,768]{1,0:T(8,128)S(1)}, u32[]{:S(2)}) copy-start(f32[512,768]{1,0:T(8,128)S(1)} %get-tuple-element.986.refs_2_) | copy-start | bytes 4718596 | tf_op jit(solution)/shard_map/cond
  252.4 143.5 %copy-start.103 = (f32[6,768]{1,0:T(8,128)S(1)}, f32[6,768]{1,0:T(8,128)}, u32[]{:S(2)}) copy-start(f32[6,768]{1,0:T(8,128)} %get-tuple-element.264) | copy-start | bytes 55300 | tf_op jit(solution)/shard_map/cond
  252.4 143.5 %copy-start.105 = (f32[6,768]{1,0:T(8,128)S(1)}, f32[6,768]{1,0:T(8,128)}, u32[]{:S(2)}) copy-start(f32[6,768]{1,0:T(8,128)} %get-tuple-element.266) | copy-start | bytes 55300 | tf_op jit(solution)/shard_map/cond
  252.4 144.9 %copy-start.88 = (f32[48,384]{1,0:T(8,128)S(1)}, f32[48,384]{1,0:T(8,128)}, u32[]{:S(2)}) copy-start(f32[48,384]{1,0:T(8,128)} %get-tuple-element.255) | copy-start | bytes 221188 | tf_op jit(solution)/shard_map/cond
  252.4 144.9 %copy-start.90 = (f32[48,384]{1,0:T(8,128)S(1)}, f32[48,384]{1,0:T(8,128)}, u32[]{:S(2)}) copy-start(f32[48,384]{1,0:T(8,128)} %get-tuple-element.257) | copy-start | bytes 221188 | tf_op jit(solution)/shard_map/cond
  252.4 146.5 %copy-start.54 = (f32[48,1536]{1,0:T(8,128)S(1)}, f32[48,1536]{1,0:T(8,128)}, u32[]{:S(2)}) copy-start(f32[48,1536]{1,0:T(8,128)} %get-tuple-element.261) | copy-start | bytes 884740 | tf_op jit(solution)/shard_map/cond
  252.4 146.4 %copy-start.56 = (f32[48,1536]{1,0:T(8,128)S(1)}, f32[48,1536]{1,0:T(8,128)}, u32[]{:S(2)}) copy-start(f32[48,1536]{1,0:T(8,128)} %get-tuple-element.263) | copy-start | bytes 884740 | tf_op jit(solution)/shard_map/cond
  252.4 146.4 %copy-start.84 = (f32[48,1536]{1,0:T(8,128)S(1)}, f32[48,1536]{1,0:T(8,128)}, u32[]{:S(2)}) copy-start(f32[48,1536]{1,0:T(8,128)} %get-tuple-element.262) | copy-start | bytes 884740 | tf_op jit(solution)/shard_map/cond
  252.4 146.7 %copy-start.28 = (f32[48,3,384]{2,0,1:T(8,128)S(1)}, f32[48,3,384]{2,0,1:T(8,128)}, u32[]{:S(2)}) copy-start(f32[48,3,384]{2,0,1:T(8,128)} %get-tuple-element.788) | copy-start | bytes 663556 | tf_op jit(solution)/shard_map/cond
  252.5 146.7 %copy-start.65 = (f32[48,3,384]{2,0,1:T(8,128)S(1)}, f32[48,3,384]{2,0,1:T(8,128)}, u32[]{:S(2)}) copy-start(f32[48,3,384]{2,0,1:T(8,128)} %get-tuple-element.795) | copy-start | bytes 663556 | tf_op jit(solution)/shard_map/cond
  252.5 146.7 %copy-start.67 = (f32[48,3,384]{2,0,1:T(8,128)S(1)}, f32[48,3,384]{2,0,1:T(8,128)}, u32[]{:S(2)}) copy-start(f32[48,3,384]{2,0,1:T(8,128)} %get-tuple-element.796) | copy-start | bytes 663556 | tf_op jit(solution)/shard_map/cond
  389.8 12.6 %copy-start.41 = (f32[48,2,1536]{2,1,0:T(2,128)S(1)}, f32[48,2,1536]{2,1,0:T(2,128)}, u32[]{:S(2)}) copy-start(f32[48,2,1536]{2,1,0:T(2,128)} %get-tuple-element.258) | copy-start | bytes 1769476 | tf_op jit(solution)/shard_map/cond
  389.8 12.6 %copy-start.43 = (f32[48,2,1536]{2,1,0:T(2,128)S(1)}, f32[48,2,1536]{2,1,0:T(2,128)}, u32[]{:S(2)}) copy-start(f32[48,2,1536]{2,1,0:T(2,128)} %get-tuple-element.260) | copy-start | bytes 1769476 | tf_op jit(solution)/shard_map/cond
  389.8 12.5 %copy-start.75 = (f32[48,2,1536]{2,1,0:T(2,128)S(1)}, f32[48,2,1536]{2,1,0:T(2,128)}, u32[]{:S(2)}) copy-start(f32[48,2,1536]{2,1,0:T(2,128)} %get-tuple-element.259) | copy-start | bytes 1769476 | tf_op jit(solution)/shard_map/cond
  399.2 6.5 %copy-start.24 = (f32[3816,384]{1,0:T(8,128)S(1)}, f32[3816,384]{1,0:T(8,128)}, u32[]{:S(2)}) copy-start(f32[3816,384]{1,0:T(8,128)} %get-tuple-element.248) | copy-start | bytes 17584132 | tf_op jit(solution)/shard_map/cond
  (4 other events, 3.3 us)

commit v6 on v4

--- a/solution.py
+++ b/solution.py
@@ -1661,7 +1661,7 @@
     pieces = [
         (c // 4, ("early", "late", "cross")[c % 3], (c % 4) * quarter, quarter, c)
         for c in range(8)
-    ] + [(2, "late", 0, feats, 8)]
+    ] + [(2, "early", 0, feats, 3)]
     late_pieces = [(c, "plain", 0, feats, 0) for c in range(3)]
     embed_grad, norm_sum, r_ffn, r_out, r_qkv, total = backward_pass(
         attn_low, w_out, query, key, value, lse, cosine, sine, seg_row, seg_col, grad_sum_one,

time: 445 us -> 447 us (level)
  no operation moved by 1% of the time
where the time goes in v6:
time: 447 us; the launch traced here: 441 us
  Pallas kernels  338 us (76%)
  other arithmetic  33.1 us (7%)
  between operations  20.3 us (5%)
  local copies, waits for them, and re-layouts  20.2 us (5%)
  loops' own time  15.4 us (3%)
  matrix products  14.4 us (3%)
    pallas_call x1, Pallas kernels, backward_pass(): pl.pallas_call(lambda *refs: backward_body(room, pieces, late_pieces, siz...  139 us
    pallas_call x1, Pallas kernels, forward_pass(): pl.pallas_call(lambda *refs: forward_body(room, kinds, pieces, stride, ev...  122 us
    pallas_call x1, Pallas kernels, hidden_back(): pl.pallas_call(lambda *refs: hidden_body(pieces, (len(held), len(landed))...  49.7 us
    sub x6, other arithmetic, adamw(): weight_in - rate * (first_hat / (jnp.sqrt(second_hat) + adam_eps) + decay...  20.3 us
    pallas_call x1, Pallas kernels, loss_step(): pl.pallas_call(loss_body, out_shape=[sds(part.shape, f32), sds((8, 128),...  17.3 us
    another operation x1, loops' own time, local(): lax.cond(flag[1, 0] > 0, lambda values: plain_step(*values), lambda value...  15.4 us
    pallas_call x1, Pallas kernels, exchange_lists(): pl.pallas_call(lists_body, out_shape=[sds((2,) + lists.shape, jnp.int32),...  9.91 us

profile of v6, /device:TPU:1, one launch (start us, length us, event | category | flops | bytes accessed | tf_op | source)
XLA Modules:
  0.0 441.1 jit_solution(14032703043163496084)
XLA Ops:
  7.2 1.5 select_reduce_fusion.5
  10.2 1.5 convert_reduce_fusion.4
  13.0 1.0 select_reduce_fusion.4
  14.6 9.9 %lists.1 = (s32[2,8,8,128]{3,2,1,0:T(8,128)S(1)}, s32[8,128]{1,0:T(8,128)}) custom-call(s32[8,8,128]{2,1,0:T(8,128)} %concatenate.47.lists), custom_call_target="tpu_custom_call" | custom-call | tf_op jit(solution)/shard_map/lists/pallas_call | solution.py:311
  24.5 1.2 slice.111
  26.4 402.0 %conditional.1 = (f32[3816,384]{1,0:T(8,128)}, f32[3816,384]{1,0:T(8,128)}, f32[3816,384]{1,0:T(8,128)}, f32[48,3,384]{2,0,1:T(8,128)S(1)}, f32[48,3,384]{2,0,1:...) conditional(s32[]{:T(128)} %bitcast.63, ...), branch_computations={%region_4.12_spmd, %region_12.69_spmd} | conditional | flops 32450023424 | bytes 1181347840 | solution.py:1699
  34.8 1.4 reshape.739.target
  36.2 1.8 copy.225.refs_8_
  38.1 1.0 copy.199.refs_7_.refs_1_.refs_10_
  40.2 2.9 fusion.48
  43.2 122.0 %forward.1 = (bf16[512,768]{1,0:T(8,128)(2,1)}, f32[512,768]{1,0:T(8,128)}, bf16[1024,768]{1,0:T(8,128)(2,1)}, bf16[1024,384]{1,0:T(8,128)(2,1)}, bf16[1024,384]...) custom-call(f32[3816,384]{1,0:T(8,128)} %get-tuple-element.203.refs_, ...), custom_call_target="tpu_custom_call" | custom-call | tf_op jit(solution)/shard_map/cond/branch_0_fun/forward/pallas_call | solution.py:542
  165.2 1.9 fusion.192
  167.1 1.9 fusion.188
  169.7 1.6 copy-done.36
  171.3 1.4 fusion.195
  173.2 1.6 fusion.36.refs_9_
  174.9 1.4 fusion.193
  177.1 1.8 fusion.35.refs_8_
  178.9 1.1 copy-done.49
  180.0 1.4 fusion.194
  181.7 1.6 fusion.189
  183.6 1.5 fusion.37.part
  185.2 17.3 %loss.1 = (f32[16,768]{1,0:T(8,128)}, f32[8,128]{1,0:T(8,128)}) custom-call(f32[16,768]{1,0:T(8,128)} %fusion.37.part, f32[16,1]{1,0:T(8,128)} %maximum_convert_fusion.counts, f32[1,128]{1,0:T(1,128)} %reshape.695.doc_ok, f32[128,1]{1,0:T(8,128)} %reshape.738.query_ok, s32[128,1]{1,0:T(8,128)} %reshape.739.target, f32[1,1]{1,0:T(1,128)} %bitcast.12.scale), custom_call_target="tpu_custom_call" | custom-call | tf_op jit(solution)/shard_map/cond/branch_0_fun/loss/pallas_call | solution.py:1092
  202.5 49.7 %hidden.1 = (f32[512,768]{1,0:T(8,128)}, bf16[512,768]{1,0:T(8,128)(2,1)}, f32[8,768]{1,0:T(8,128)}, bf16[768,384]{1,0:T(8,128)(2,1)}, bf16[768,384]{1,0:T(8,128...) custom-call(f32[16,768]{1,0:T(8,128)} %get-tuple-element.230.refs_0_, ...), custom_call_target="tpu_custom_call" | custom-call | tf_op jit(solution)/shard_map/cond/branch_0_fun/hidden/pallas_call | solution.py:727
  252.3 138.7 %backward.1 = (f32[3816,384]{1,0:T(8,128)}, f32[8,768]{1,0:T(8,128)}, f32[48,2,1536]{2,1,0:T(2,128)}, f32[48,384]{1,0:T(8,128)}, f32[48,3,384]{2,1,0:T(4,128)}, /*index=5*/f32[8,128]{1,0:T(8,128)}) custom-call(bf16[512,768]{1,0:T(8,128)(2,1)} %get-tuple-element.231.refs_0_, bf16[768,384]{1,0:T(8,128)(2,1)} %bitcast.256, bf16[768,384]{1,0:T(8,128)(2,1)} %bitcast.258, ...), custom_call_target="tpu_custom_call" | custom-call | tf_op jit(solution)/shard_map/cond/branch_0_fun/backward/pallas_call | solution.py:996
  391.1 1.3 slice.86
  392.4 1.3 fusion.186
  397.1 1.4 multiply_subtract_fusion.5
  398.5 1.6 multiply_subtract_fusion.4
  400.4 1.7 multiply_subtract_fusion.3
  403.6 3.3 multiply_subtract_fusion.1
  406.9 12.1 %multiply_subtract_fusion = (f32[3816,384]{1,0:T(8,128)}, f32[3816,384]{1,0:T(8,128)}, f32[3816,384]{1,0:T(8,128)}) fusion(f32[3816,384]{1,0:T(8,128)} %get-tuple-element.203.refs_0_, f32[3816,384]{1,0:T(8,128)S(1)} %copy-done.24, f32[]{:T(128)} %bitcast.18, f32[3816,384]{1,0:T(8,128)} %get-tuple-element.204, f32[3816,384]{1,0:T(8,128)} %get-tuple-element.251), kind=kLoop, calls=%fused_computation.51 | loop fusion | flops 23445504 | bytes 41029636 | tf_op jit(solution)/shard_map/cond/branch_0_fun/sub | solution.py:1146
  (110 shorter events, 15.5 us)
Async XLA Ops:
  26.4 16.7 %copy-start.17 = (f32[48,2,1536]{2,1,0:T(2,128)S(1)}, f32[48,2,1536]{2,1,0:T(2,128)}, u32[]{:S(2)}) copy-start(f32[48,2,1536]{2,1,0:T(2,128)} %get-tuple-element.215.refs_10_) | copy-start | bytes 1769476 | tf_op jit(solution)/shard_map/cond
  26.4 16.7 %copy-start.25 = (f32[48,1536]{1,0:T(8,128)S(1)}, f32[48,1536]{1,0:T(8,128)}, u32[]{:S(2)}) copy-start(f32[48,1536]{1,0:T(8,128)} %get-tuple-element.216.refs_11_) | copy-start | bytes 884740 | tf_op jit(solution)/shard_map/cond
  26.4 16.7 %copy-start.51 = (f32[48,384]{1,0:T(8,128)S(1)}, f32[48,384]{1,0:T(8,128)}, u32[]{:S(2)}) copy-start(f32[48,384]{1,0:T(8,128)} %get-tuple-element.214.refs_9_) | copy-start | bytes 221188 | tf_op jit(solution)/shard_map/cond
  26.5 16.7 %copy-start.61 = (f32[6,768]{1,0:T(8,128)S(1)}, f32[6,768]{1,0:T(8,128)}, u32[]{:S(2)}) copy-start(f32[6,768]{1,0:T(8,128)} %get-tuple-element.212.refs_3_.refs_13_) | copy-start | bytes 55300 | tf_op jit(solution)/shard_map/cond
  30.1 135.2 %copy-start.114 = (s32[1024]{0:T(1024)}, s32[1024]{0:T(1024)S(1)}, u32[]{:S(2)}) copy-start(s32[1024]{0:T(1024)S(1)} %add_select_fusion.2) | copy-start | bytes 12292 | tf_op jit(solution)/shard_map/cond
  31.0 12.1 %copy-start.100 = (s32[1024]{0:T(1024)}, s32[1024]{0:T(1024)S(1)}, u32[]{:S(2)}) copy-start(s32[1024]{0:T(1024)S(1)} %convert_reduce_fusion) | copy-start | bytes 12292 | tf_op jit(solution)/shard_map/cond
  165.2 1.9 copy-start.50
  169.0 12.4 %copy-start.13 = (f32[512,768]{1,0:T(8,128)}, f32[512,768]{1,0:T(8,128)S(1)}, u32[]{:S(2)}) copy-start(f32[512,768]{1,0:T(8,128)S(1)} %get-tuple-element.984.refs_5_) | copy-start | bytes 4718596 | tf_op jit(solution)/shard_map/cond
  169.0 2.2 copy-start.36
  171.2 5.0 %copy-start.31 = (bf16[512,768]{1,0:T(8,128)(2,1)}, bf16[512,768]{1,0:T(8,128)(2,1)S(1)}, u32[]{:S(2)}) copy-start(bf16[512,768]{1,0:T(8,128)(2,1)S(1)} %fusion.42.refs_4_) | copy-start | bytes 2359300 | tf_op jit(solution)/shard_map/cond
  171.2 1.9 copy-start.38
  173.2 1.7 copy-start.35
  174.9 6.6 %copy-start.48 = (bf16[512,1536]{1,0:T(8,128)(2,1)}, bf16[512,1536]{1,0:T(8,128)(2,1)S(1)}, u32[]{:S(2)}) copy-start(bf16[512,1536]{1,0:T(8,128)(2,1)S(1)} %fusion.36.refs_9_) | copy-start | bytes 4718596 | tf_op jit(solution)/shard_map/cond
  174.9 2.2 copy-start.37
  177.1 2.9 copy-start.39
  178.9 1.1 copy-start.49
  180.0 1.7 copy-start.40
  183.3 19.2 %copy-start.14 = (f32[512,768]{1,0:T(8,128)}, f32[512,768]{1,0:T(8,128)S(1)}, u32[]{:S(2)}) copy-start(f32[512,768]{1,0:T(8,128)S(1)} %get-tuple-element.986.refs_2_) | copy-start | bytes 4718596 | tf_op jit(solution)/shard_map/cond
  252.2 144.9 %copy-start.103 = (f32[6,768]{1,0:T(8,128)S(1)}, f32[6,768]{1,0:T(8,128)}, u32[]{:S(2)}) copy-start(f32[6,768]{1,0:T(8,128)} %get-tuple-element.264) | copy-start | bytes 55300 | tf_op jit(solution)/shard_map/cond
  252.2 144.9 %copy-start.105 = (f32[6,768]{1,0:T(8,128)S(1)}, f32[6,768]{1,0:T(8,128)}, u32[]{:S(2)}) copy-start(f32[6,768]{1,0:T(8,128)} %get-tuple-element.266) | copy-start | bytes 55300 | tf_op jit(solution)/shard_map/cond
  252.2 146.3 %copy-start.88 = (f32[48,384]{1,0:T(8,128)S(1)}, f32[48,384]{1,0:T(8,128)}, u32[]{:S(2)}) copy-start(f32[48,384]{1,0:T(8,128)} %get-tuple-element.255) | copy-start | bytes 221188 | tf_op jit(solution)/shard_map/cond
  252.2 146.3 %copy-start.90 = (f32[48,384]{1,0:T(8,128)S(1)}, f32[48,384]{1,0:T(8,128)}, u32[]{:S(2)}) copy-start(f32[48,384]{1,0:T(8,128)} %get-tuple-element.257) | copy-start | bytes 221188 | tf_op jit(solution)/shard_map/cond
  252.3 147.9 %copy-start.54 = (f32[48,1536]{1,0:T(8,128)S(1)}, f32[48,1536]{1,0:T(8,128)}, u32[]{:S(2)}) copy-start(f32[48,1536]{1,0:T(8,128)} %get-tuple-element.261) | copy-start | bytes 884740 | tf_op jit(solution)/shard_map/cond
  252.3 147.9 %copy-start.56 = (f32[48,1536]{1,0:T(8,128)S(1)}, f32[48,1536]{1,0:T(8,128)}, u32[]{:S(2)}) copy-start(f32[48,1536]{1,0:T(8,128)} %get-tuple-element.263) | copy-start | bytes 884740 | tf_op jit(solution)/shard_map/cond
  252.3 147.8 %copy-start.84 = (f32[48,1536]{1,0:T(8,128)S(1)}, f32[48,1536]{1,0:T(8,128)}, u32[]{:S(2)}) copy-start(f32[48,1536]{1,0:T(8,128)} %get-tuple-element.262) | copy-start | bytes 884740 | tf_op jit(solution)/shard_map/cond
  252.3 148.1 %copy-start.28 = (f32[48,3,384]{2,0,1:T(8,128)S(1)}, f32[48,3,384]{2,0,1:T(8,128)}, u32[]{:S(2)}) copy-start(f32[48,3,384]{2,0,1:T(8,128)} %get-tuple-element.788) | copy-start | bytes 663556 | tf_op jit(solution)/shard_map/cond
  252.3 148.1 %copy-start.65 = (f32[48,3,384]{2,0,1:T(8,128)S(1)}, f32[48,3,384]{2,0,1:T(8,128)}, u32[]{:S(2)}) copy-start(f32[48,3,384]{2,0,1:T(8,128)} %get-tuple-element.795) | copy-start | bytes 663556 | tf_op jit(solution)/shard_map/cond
  252.3 148.1 %copy-start.67 = (f32[48,3,384]{2,0,1:T(8,128)S(1)}, f32[48,3,384]{2,0,1:T(8,128)}, u32[]{:S(2)}) copy-start(f32[48,3,384]{2,0,1:T(8,128)} %get-tuple-element.796) | copy-start | bytes 663556 | tf_op jit(solution)/shard_map/cond
  391.0 12.6 %copy-start.41 = (f32[48,2,1536]{2,1,0:T(2,128)S(1)}, f32[48,2,1536]{2,1,0:T(2,128)}, u32[]{:S(2)}) copy-start(f32[48,2,1536]{2,1,0:T(2,128)} %get-tuple-element.258) | copy-start | bytes 1769476 | tf_op jit(solution)/shard_map/cond
  391.1 12.6 %copy-start.43 = (f32[48,2,1536]{2,1,0:T(2,128)S(1)}, f32[48,2,1536]{2,1,0:T(2,128)}, u32[]{:S(2)}) copy-start(f32[48,2,1536]{2,1,0:T(2,128)} %get-tuple-element.260) | copy-start | bytes 1769476 | tf_op jit(solution)/shard_map/cond
  391.1 12.5 %copy-start.75 = (f32[48,2,1536]{2,1,0:T(2,128)S(1)}, f32[48,2,1536]{2,1,0:T(2,128)}, u32[]{:S(2)}) copy-start(f32[48,2,1536]{2,1,0:T(2,128)} %get-tuple-element.259) | copy-start | bytes 1769476 | tf_op jit(solution)/shard_map/cond
  400.4 6.5 %copy-start.24 = (f32[3816,384]{1,0:T(8,128)S(1)}, f32[3816,384]{1,0:T(8,128)}, u32[]{:S(2)}) copy-start(f32[3816,384]{1,0:T(8,128)} %get-tuple-element.248) | copy-start | bytes 17584132 | tf_op jit(solution)/shard_map/cond
  (4 other events, 3.3 us)
